TPU v7x, 512 devices: a whole 4x8x8 slice. The times are simulated.
512 devices in a mesh: wide: 64 (over y, z), narrow: 8 (over x, core).
Axes of the slice: x: 4, y: 8, z: 8, core: 2. Of those that a mesh axis runs over, the one named last changes fastest.
Arguments:
- noise: bfloat16 [1024, 81920], P('narrow', 'wide'), may hold values from -6 to 6
- latents: bfloat16 [3072, 81920], P('narrow', 'wide'), may hold values from -18 to 18
Outputs:
- velocity: bfloat16 [1024, 81920], P('narrow', 'wide')
All inputs are finite; a program needn't handle non-finite values.
Results may differ from a plain program's by a relative error of at most 0.009.
Values may be sent and summed in bfloat16 or wider, within the bound.
No kernel may reach another device: no remote copies, remote signals or barrier semaphores. Data moves between devices by JAX's collectives and lax.ppermute only.
A program may use at most 64 MiB of HBM per device.

v0:
```python
import math

import jax
import jax.numpy as jnp
from jax import lax
from jax.sharding import PartitionSpec as P

F = 81920
BALANCE_ROUNDS = 3


def narrow_totals(kernel, col_scale):
    return lax.psum(jnp.sum(kernel * col_scale[None, :], axis=1), "narrow")


def body(noise, latents):
    inv_root = 1.0 / math.sqrt(F)
    rows_all = lax.all_gather(noise, "narrow", axis=0, tiled=True)
    total_noise = rows_all.shape[0]
    video_clip_rows = latents.shape[0]
    total_clips = video_clip_rows * lax.axis_size("narrow")
    affinity_scores = lax.psum_scatter(
        jnp.dot(rows_all, latents.T, preferred_element_type=jnp.float32),
        "wide",
        scatter_dimension=0,
        tiled=True,
    )
    kernel = jnp.exp(affinity_scores * inv_root)
    col_scale = jnp.ones((video_clip_rows,), jnp.float32)
    for iteration_step in range(BALANCE_ROUNDS):
        row_total = narrow_totals(kernel, col_scale)
        row_scale = 1.0 / total_noise / row_total
        column_mass_total = lax.psum(jnp.sum(kernel * row_scale[:, None], axis=0), "wide")
        col_scale = 1.0 / total_clips / column_mass_total
    final_total = narrow_totals(kernel, col_scale)
    weights = (kernel * col_scale[None, :] / final_total[:, None]).astype(jnp.bfloat16)
    partial_value = jnp.dot(
        lax.all_gather(weights, "wide", axis=0, tiled=True),
        latents,
        preferred_element_type=jnp.float32,
    )
    summed = lax.psum_scatter(
        partial_value.astype(jnp.bfloat16), "narrow", scatter_dimension=0, tiled=True
    ).astype(jnp.float32)
    return (summed - noise.astype(jnp.float32)).astype(jnp.bfloat16)


def solution(mesh):
    in_specs = (P("narrow", "wide"), P("narrow", "wide"))
    out_specs = P("narrow", "wide")
    return jax.shard_map(body, mesh=mesh, in_specs=in_specs, out_specs=out_specs, check_vma=False)
```

profile of v0, /device:TPU:24, one launch (start us, length us, event | category | flops | bytes accessed | tf_op | source)
XLA Modules:
  0.0 780.3 jit_solution(4682588615319569258)
XLA Ops:
  6.5 0.0 copy-start
  6.5 0.0 all-gather.2.cloned.1.call-start
  6.5 0.7 all-gather.2.cloned.1.call-update
  7.3 0.0 all-reduce.3.cloned.1.call-start
  7.3 38.0 %all-gather.2.cloned.1.call-done = bf16[1024,1280]{1,0:T(8,128)(2,1)} async-done(((bf16[128,1280]{1,0:T(8,128)(2,1)}), bf16[1024,1280]{1,0:T(8,128)(2,1)}) %all-gather.2.cloned.1.call-update) | async-done | bytes 2621456 | tf_op jit(solution)/shard_map/all_gather | solution.py:18
  45.4 0.0 copy-done
  45.4 4.4 fusion.2
  49.8 0.0 all-reduce.3.cloned.1.call-update
  49.8 0.0 reduce-scatter.2.cloned.1.call-start
  49.8 1.3 dynamic-slice
  51.8 160.0 %all-reduce.3.cloned.1.call-done = f32[1024,384]{1,0:T(8,128)} async-done(((f32[1024,384]{1,0:T(8,128)}), f32[1024,384]{1,0:T(8,128)}) %all-reduce.3.cloned.1.call-update) | async-done | bytes 1572880
  211.7 0.9 fusion.1
  212.6 12.4 %psum.49 = f32[16]{0:T(128)S(1)} all-reduce(f32[16]{0:T(128)S(1)} %fusion.1), channel_id=1, replica_groups=mesh['wide'=64,'narrow'=8] {'narrow'}, use_global_device_ids=true, to_apply=%region_2.0 | all-reduce | flops 16 | bytes 128 | tf_op jit(solution)/shard_map/psum | solution.py:13
  225.0 0.8 multiply_reduce_fusion.4
  225.8 128.7 %psum.50 = f32[384]{0:T(512)S(1)} all-reduce(f32[384]{0:T(512)S(1)} %multiply_reduce_fusion.4), channel_id=1, replica_groups=mesh['wide'=64,'narrow'=8] {'wide'}, use_global_device_ids=true, to_apply=%region_4.0 | all-reduce | flops 384 | bytes 3072 | tf_op jit(solution)/shard_map/psum | solution.py:33
  354.6 0.9 multiply_reduce_fusion.3
  355.5 12.4 %psum.51 = f32[16]{0:T(128)S(1)} all-reduce(f32[16]{0:T(128)S(1)} %multiply_reduce_fusion.3), channel_id=1, replica_groups=mesh['wide'=64,'narrow'=8] {'narrow'}, use_global_device_ids=true, to_apply=%region_6.0 | all-reduce | flops 16 | bytes 128 | tf_op jit(solution)/shard_map/psum | solution.py:13
  367.9 0.8 multiply_reduce_fusion.2
  368.7 138.9 %psum.52 = f32[384]{0:T(512)S(1)} all-reduce(f32[384]{0:T(512)S(1)} %multiply_reduce_fusion.2), channel_id=1, replica_groups=mesh['wide'=64,'narrow'=8] {'wide'}, use_global_device_ids=true, to_apply=%region_8.0 | all-reduce | flops 384 | bytes 3072 | tf_op jit(solution)/shard_map/psum | solution.py:33
  507.6 0.9 multiply_reduce_fusion.1
  508.5 12.4 %psum.53 = f32[16]{0:T(128)S(1)} all-reduce(f32[16]{0:T(128)S(1)} %multiply_reduce_fusion.1), channel_id=1, replica_groups=mesh['wide'=64,'narrow'=8] {'narrow'}, use_global_device_ids=true, to_apply=%region_10.0 | all-reduce | flops 16 | bytes 128 | tf_op jit(solution)/shard_map/psum | solution.py:13
  520.9 0.8 multiply_reduce_fusion
  521.7 139.0 %psum.54 = f32[384]{0:T(512)S(1)} all-reduce(f32[384]{0:T(512)S(1)} %multiply_reduce_fusion), channel_id=1, replica_groups=mesh['wide'=64,'narrow'=8] {'wide'}, use_global_device_ids=true, to_apply=%region_12.0 | all-reduce | flops 384 | bytes 3072 | tf_op jit(solution)/shard_map/psum | solution.py:33
  660.7 0.9 multiply_reduce_fusion.5
  661.6 12.4 %psum.55 = f32[16]{0:T(128)S(1)} all-reduce(f32[16]{0:T(128)S(1)} %multiply_reduce_fusion.5), channel_id=1, replica_groups=mesh['wide'=64,'narrow'=8] {'narrow'}, use_global_device_ids=true, to_apply=%region_14.0 | all-reduce | flops 16 | bytes 128 | tf_op jit(solution)/shard_map/psum | solution.py:13
  674.0 0.8 divide_convert_fusion
  674.8 60.6 %all_gather.7 = bf16[1024,384]{1,0:T(8,128)(2,1)S(1)} all-gather(bf16[16,384]{1,0:T(8,128)(2,1)S(1)} %divide_convert_fusion), channel_id=1, replica_groups=mesh['wide'=64,'narrow'=8] {'wide'}, dimensions={0}, use_global_device_ids=true | all-gather | bytes 798720 | tf_op jit(solution)/shard_map/all_gather | solution.py:38
  735.4 3.0 convolution_convert_fusion
  738.5 0.0 copy-start.1
  738.5 0.0 reduce-scatter.2.cloned.1.call-update
  738.5 33.5 %reduce-scatter.2.cloned.1.call-done = bf16[128,1280]{1,0:T(8,128)(2,1)} async-done(((bf16[1024,1280]{1,0:T(8,128)(2,1)}), bf16[128,1280]{1,0:T(8,128)(2,1)}) %reduce-scatter.2.cloned.1.call-update) | async-done | bytes 327696 | tf_op jit(solution)/shard_map/reduce_scatter | solution.py:42
  772.0 0.0 copy-done.1
  772.0 1.8 subtract_convert_fusion
  (6 shorter events, 0.0 us)
Async XLA Ops:
  6.5 38.8 %copy-start = (bf16[384,1280]{1,0:T(8,128)(2,1)S(1)}, bf16[384,1280]{1,0:T(8,128)(2,1)}, u32[]{:S(2)}) copy-start(bf16[384,1280]{1,0:T(8,128)(2,1)} %param.3) | copy-start | bytes 2949124
  6.5 38.8 %all-gather.2.cloned.1.call-start = ((), (), s32[]{:S(2)}) async-start(), calls=%async_computation.1 | async-start | bytes 2949120 | tf_op jit(solution)/shard_map/all_gather | solution.py:18
  7.3 204.5 %all-reduce.3.cloned.1.call-start = ((), (), s32[]{:S(2)}) async-start(), calls=%async_computation.3 | async-start | bytes 3145728
  49.8 722.2 %reduce-scatter.2.cloned.1.call-start = ((), (), s32[]{:S(2)}) async-start(), calls=%async_computation.2 | async-start | bytes 2949120 | tf_op jit(solution)/shard_map/reduce_scatter | solution.py:42
  738.5 33.5 %copy-start.1 = (bf16[128,1280]{1,0:T(8,128)(2,1)S(1)}, bf16[128,1280]{1,0:T(8,128)(2,1)}, u32[]{:S(2)}) copy-start(bf16[128,1280]{1,0:T(8,128)(2,1)} %param.2) | copy-start | bytes 983044
Sparse Core Ops, SparseCore 0:
  9.5 35.8 all-gather.1
  49.9 161.7 all-reduce.2
  738.6 33.3 reduce-scatter.1
where the time goes:
time: 781 us; the launch traced here: 780 us
  blocking collectives  517 us (66%)
  waiting for transfers between devices  232 us (30%)
  between operations  13.8 us (2%)
  other arithmetic  8.55 us (1%)
    psum x3, blocking collectives, body(): lax.psum(jnp.sum(kernel * row_scale[:, None], axis=0), 'wide')  407 us
    unnamed x4, waiting for transfers between devices  161 us
    all_gather x1, blocking collectives, body(): lax.all_gather(weights, 'wide', axis=0, tiled=True)  60.6 us
    psum x4, blocking collectives, narrow_totals(): return lax.psum(jnp.sum(kernel * col_scale[None, :], axis=1), 'narrow')  49.7 us
    all_gather x1, waiting for transfers between devices, body(): rows_all = lax.all_gather(noise, 'narrow', axis=0, tiled=True)  38 us
    reduce_scatter x1, waiting for transfers between devices, body(): lax.psum_scatter(partial_value.astype(jnp.bfloat16), 'narrow', scatter_di...  33.5 us
  transfers between devices with their start and end apart: 3, of which 3 were waited for; matrix products, arithmetic and copies ran while one was open for 0% of the time, Pallas kernels for 0%

commit v1 on v0

--- a/solution.py
+++ b/solution.py
@@ -19,26 +19,17 @@
     total_noise = rows_all.shape[0]
     video_clip_rows = latents.shape[0]
     total_clips = video_clip_rows * lax.axis_size("narrow")
-    affinity_scores = lax.psum_scatter(
-        jnp.dot(rows_all, latents.T, preferred_element_type=jnp.float32),
-        "wide",
-        scatter_dimension=0,
-        tiled=True,
-    )
+    affinity_scores = lax.psum(jnp.dot(rows_all, latents.T, preferred_element_type=jnp.float32), "wide")
     kernel = jnp.exp(affinity_scores * inv_root)
     col_scale = jnp.ones((video_clip_rows,), jnp.float32)
     for iteration_step in range(BALANCE_ROUNDS):
         row_total = narrow_totals(kernel, col_scale)
         row_scale = 1.0 / total_noise / row_total
-        column_mass_total = lax.psum(jnp.sum(kernel * row_scale[:, None], axis=0), "wide")
+        column_mass_total = jnp.sum(kernel * row_scale[:, None], axis=0)
         col_scale = 1.0 / total_clips / column_mass_total
     final_total = narrow_totals(kernel, col_scale)
     weights = (kernel * col_scale[None, :] / final_total[:, None]).astype(jnp.bfloat16)
-    partial_value = jnp.dot(
-        lax.all_gather(weights, "wide", axis=0, tiled=True),
-        latents,
-        preferred_element_type=jnp.float32,
-    )
+    partial_value = jnp.dot(weights, latents, preferred_element_type=jnp.float32)
     summed = lax.psum_scatter(
         partial_value.astype(jnp.bfloat16), "narrow", scatter_dimension=0, tiled=True
     ).astype(jnp.float32)

time: 781 us -> 312 us (0.40)
  the two profiles are of different devices: /device:TPU:24 before, /device:TPU:8 now
where the time goes in v1:
time: 312 us; the launch traced here: 311 us
  waiting for transfers between devices  235 us (75%)
  blocking collectives  49.7 us (16%)
  between operations  13.2 us (4%)
  matrix products  7.53 us (2%)
  other arithmetic  5.51 us (2%)
    psum x1, waiting for transfers between devices, body(): lax.psum(jnp.dot(rows_all, latents.T, preferred_element_type=jnp.float32)...  162 us
    psum x4, blocking collectives, narrow_totals(): return lax.psum(jnp.sum(kernel * col_scale[None, :], axis=1), 'narrow')  49.7 us
    all_gather x1, waiting for transfers between devices, body(): rows_all = lax.all_gather(noise, 'narrow', axis=0, tiled=True)  38.2 us
    reduce_scatter x1, waiting for transfers between devices, body(): lax.psum_scatter(partial_value.astype(jnp.bfloat16), 'narrow', scatter_di...  34.6 us
  transfers between devices with their start and end apart: 3, of which 3 were waited for; matrix products, arithmetic and copies ran while one was open for 0% of the time, Pallas kernels for 0%

profile of v1, /device:TPU:8, one launch (start us, length us, event | category | flops | bytes accessed | tf_op | source)
XLA Modules:
  0.0 311.4 jit_solution(9579354015074042121)
XLA Ops:
  6.5 0.0 copy-start
  6.5 0.0 all-gather.2.cloned.1.call-start
  6.5 0.7 all-gather.2.cloned.1.call-update
  7.3 0.0 all-reduce.2.cloned.1.call-start
  7.3 38.2 %all-gather.2.cloned.1.call-done = bf16[1024,1280]{1,0:T(8,128)(2,1)} async-done(((bf16[128,1280]{1,0:T(8,128)(2,1)}), bf16[1024,1280]{1,0:T(8,128)(2,1)}) %all-gather.2.cloned.1.call-update) | async-done | bytes 2621456 | tf_op jit(solution)/shard_map/all_gather | solution.py:18
  45.5 0.0 copy-done
  45.5 4.4 %fusion.4 = f32[1024,384]{1,0:T(8,128)} fusion(bf16[1024,1280]{1,0:T(8,128)(2,1)} %all-gather.2.cloned.1.call-done, bf16[384,1280]{1,0:T(8,128)(2,1)S(1)} %copy-done), kind=kOutput, calls=%fused_computation.20 | convolution fusion | flops 1006632960 | bytes 5177344 | tf_op jit(solution)/shard_map/dot_general | solution.py:22
  50.0 0.0 all-reduce.2.cloned.1.call-update
  50.0 0.0 reduce-scatter.2.cloned.1.call-start
  50.0 161.9 %all-reduce.2.cloned.1.call-done = f32[1024,384]{1,0:T(8,128)} async-done(((f32[1024,384]{1,0:T(8,128)}), f32[1024,384]{1,0:T(8,128)}) %all-reduce.2.cloned.1.call-update) | async-done | bytes 1572880 | tf_op jit(solution)/shard_map/psum | solution.py:22
  211.9 0.0 copy-start.1
  211.9 1.8 fusion.2
  213.8 12.4 %psum.36 = f32[1024]{0:T(1024)S(1)} all-reduce(f32[1024]{0:T(1024)S(1)} %fusion.2), channel_id=1, replica_groups=mesh['wide'=64,'narrow'=8] {'narrow'}, use_global_device_ids=true, to_apply=%region_2.0 | all-reduce | flops 1024 | bytes 8192 | tf_op jit(solution)/shard_map/psum | solution.py:13
  226.2 0.0 copy-done.1
  226.2 0.3 multiply_reduce_fusion.4
  226.5 0.3 multiply_reduce_fusion.3
  226.8 12.4 %psum.37 = f32[1024]{0:T(1024)S(1)} all-reduce(f32[1024]{0:T(1024)S(1)} %multiply_reduce_fusion.3), channel_id=1, replica_groups=mesh['wide'=64,'narrow'=8] {'narrow'}, use_global_device_ids=true, to_apply=%region_5.0 | all-reduce | flops 1024 | bytes 8192 | tf_op jit(solution)/shard_map/psum | solution.py:13
  239.3 0.3 multiply_reduce_fusion.2
  239.6 0.3 multiply_reduce_fusion.1
  239.9 12.4 %psum.38 = f32[1024]{0:T(1024)S(1)} all-reduce(f32[1024]{0:T(1024)S(1)} %multiply_reduce_fusion.1), channel_id=1, replica_groups=mesh['wide'=64,'narrow'=8] {'narrow'}, use_global_device_ids=true, to_apply=%region_8.0 | all-reduce | flops 1024 | bytes 8192 | tf_op jit(solution)/shard_map/psum | solution.py:13
  252.3 0.3 multiply_reduce_fusion
  252.7 0.3 multiply_reduce_fusion.5
  253.0 12.4 %psum.39 = f32[1024]{0:T(1024)S(1)} all-reduce(f32[1024]{0:T(1024)S(1)} %multiply_reduce_fusion.5), channel_id=1, replica_groups=mesh['wide'=64,'narrow'=8] {'narrow'}, use_global_device_ids=true, to_apply=%region_11.0 | all-reduce | flops 1024 | bytes 8192 | tf_op jit(solution)/shard_map/psum | solution.py:13
  265.4 3.1 convolution_convert_fusion
  268.5 0.0 copy-start.2
  268.5 0.0 reduce-scatter.2.cloned.1.call-update
  268.6 34.6 %reduce-scatter.2.cloned.1.call-done = bf16[128,1280]{1,0:T(8,128)(2,1)} async-done(((bf16[1024,1280]{1,0:T(8,128)(2,1)}), bf16[128,1280]{1,0:T(8,128)(2,1)}) %reduce-scatter.2.cloned.1.call-update) | async-done | bytes 327696 | tf_op jit(solution)/shard_map/reduce_scatter | solution.py:33
  303.1 0.0 copy-done.2
  303.1 1.8 subtract_convert_fusion
  (6 shorter events, 0.0 us)
Async XLA Ops:
  6.5 39.0 %copy-start = (bf16[384,1280]{1,0:T(8,128)(2,1)S(1)}, bf16[384,1280]{1,0:T(8,128)(2,1)}, u32[]{:S(2)}) copy-start(bf16[384,1280]{1,0:T(8,128)(2,1)} %param.3) | copy-start | bytes 2949124
  6.5 39.0 %all-gather.2.cloned.1.call-start = ((), (), s32[]{:S(2)}) async-start(), calls=%async_computation.1 | async-start | bytes 2949120 | tf_op jit(solution)/shard_map/all_gather | solution.py:18
  7.3 204.7 %all-reduce.2.cloned.1.call-start = ((), (), s32[]{:S(2)}) async-start(), calls=%async_computation.2 | async-start | bytes 3145728 | tf_op jit(solution)/shard_map/psum | solution.py:22
  50.0 253.1 %reduce-scatter.2.cloned.1.call-start = ((), (), s32[]{:S(2)}) async-start(), calls=%async_computation.3 | async-start | bytes 2949120 | tf_op jit(solution)/shard_map/reduce_scatter | solution.py:33
  211.9 14.3 %copy-start.1 = (f32[1024,384]{1,0:T(8,128)S(1)}, f32[1024,384]{1,0:T(8,128)}, u32[]{:S(2)}) copy-start(f32[1024,384]{1,0:T(8,128)} %all-reduce.2.cloned.1.call-done) | copy-start | bytes 4718596
  268.5 34.6 %copy-start.2 = (bf16[128,1280]{1,0:T(8,128)(2,1)S(1)}, bf16[128,1280]{1,0:T(8,128)(2,1)}, u32[]{:S(2)}) copy-start(bf16[128,1280]{1,0:T(8,128)(2,1)} %param.2) | copy-start | bytes 983044
Sparse Core Ops, SparseCore 0:
  9.5 36.0 all-gather.1
  50.1 161.7 all-reduce.1
  268.7 34.3 reduce-scatter.1

commit v2 on v1

v2 whole, which is shorter than its diff:
```python
import math

import jax
import jax.numpy as jnp
from jax import lax
from jax.sharding import Mesh
from jax.sharding import PartitionSpec as P

F = 81920
BALANCE_ROUNDS = 3
Y, Z, X, C = 8, 8, 4, 2
WIDE = ("y", "z")
NARROW = ("x", "c")
SWAP = [(0, 1), (1, 0)]
SEND_SCALE = 64.0


def gather_by_a2a(block, axes, n):
    return lax.all_to_all(jnp.broadcast_to(block[None], (n, *block.shape)), axes, 0, 0).reshape(
        n * block.shape[0], block.shape[1]
    )


def body(noise, latents):
    draws, features = noise.shape
    clips = latents.shape[0]
    total_noise = draws * X * C
    total_clips = clips * X * C
    half = draws * X
    first_core = lax.axis_index("c") == 0

    own_rows = gather_by_a2a(noise, "x", X)
    other_rows = lax.ppermute(own_rows, "c", SWAP)
    scale = SEND_SCALE / math.sqrt(F)

    def partial_scores(rows):
        scores = lax.dot_general(rows, latents, (((1,), (1,)), ((), ())), preferred_element_type=jnp.float32)
        return (scores * scale).astype(jnp.float16)

    partial = jnp.concatenate([partial_scores(own_rows), partial_scores(other_rows)], axis=0)
    arrived = lax.all_to_all(partial.reshape(Y * Z, total_noise // (Y * Z), clips), WIDE, 0, 0)
    scores = jnp.sum(arrived.astype(jnp.float32), axis=0)
    block = jnp.exp(scores * (1.0 / SEND_SCALE)).astype(jnp.bfloat16)
    kernel = gather_by_a2a(block, WIDE, Y * Z).astype(jnp.float32)

    def swap_order(vector):
        halves = vector.reshape(C, half)
        return jnp.where(first_core, halves, halves[::-1]).reshape(total_noise)

    def narrow_totals(col_scale):
        part = swap_order(jnp.sum(kernel * col_scale[None, :], axis=1))
        parts = lax.all_to_all(jnp.broadcast_to(part.reshape(1, 8, -1), (X * C, 8, total_noise // 8)), NARROW, 0, 0)
        return swap_order(jnp.sum(parts, axis=0).reshape(total_noise))

    col_scale = jnp.ones((clips,), jnp.float32)
    for _ in range(BALANCE_ROUNDS):
        row_scale = 1.0 / total_noise / narrow_totals(col_scale)
        col_scale = 1.0 / total_clips / jnp.sum(kernel * row_scale[:, None], axis=0)
    final_total = narrow_totals(col_scale)
    weights = (kernel * col_scale[None, :] / final_total[:, None]).astype(jnp.bfloat16)

    other_part = jnp.dot(weights[half:], latents, preferred_element_type=jnp.float32).astype(jnp.bfloat16)
    from_other = lax.ppermute(other_part, "c", SWAP)
    own_part = jnp.dot(weights[:half], latents, preferred_element_type=jnp.float32)
    pair = (own_part + from_other.astype(jnp.float32)).astype(jnp.bfloat16)
    parts = lax.all_to_all(pair.reshape(X, draws, features), "x", 0, 0)
    target = jnp.sum(parts.astype(jnp.float32), axis=0)
    return (target - noise.astype(jnp.float32)).astype(jnp.bfloat16)


def solution(mesh):
    mesh = Mesh(mesh.devices.reshape(Y, Z, X, C), (*WIDE, *NARROW))
    spec = P(NARROW, WIDE)
    return jax.shard_map(body, mesh=mesh, in_specs=(spec, spec), out_specs=spec, check_vma=False)
```

time: 312 us -> 167 us (0.54)
  the two profiles are of different devices: /device:TPU:8 before, /device:TPU:16 now
where the time goes in v2:
time: 167 us; the launch traced here: 166 us
  blocking collectives  116 us (69%)
  waiting for transfers between devices  29.9 us (18%)
  starting transfers between devices  9.27 us (6%)
  local copies, waits for them, and re-layouts  4.58 us (3%)
  matrix products  3.42 us (2%)
  other arithmetic  3.29 us (2%)
    all_to_all x1, blocking collectives, body(): lax.all_to_all(partial.reshape(Y * Z, total_noise // (Y * Z), clips), WID...  41.4 us
    all_to_all x4, blocking collectives, narrow_totals(): lax.all_to_all(jnp.broadcast_to(part.reshape(1, 8, -1), (X * C, 8, total_...  31.3 us
    all_to_all x1, waiting for transfers between devices, gather_by_a2a(): lax.all_to_all(jnp.broadcast_to(block[None], (n, *block.shape)), axes, 0, 0)  24.8 us
    all_to_all x1, blocking collectives, gather_by_a2a(): lax.all_to_all(jnp.broadcast_to(block[None], (n, *block.shape)), axes, 0, 0)  22 us
    all_to_all x1, blocking collectives, body(): parts = lax.all_to_all(pair.reshape(X, draws, features), 'x', 0, 0)  20.9 us
    all_to_all x1, starting transfers between devices, gather_by_a2a(): lax.all_to_all(jnp.broadcast_to(block[None], (n, *block.shape)), axes, 0, 0)  5.44 us
  transfers between devices with their start and end apart: 3, of which 3 were waited for; matrix products, arithmetic and copies ran while one was open for 1% of the time, Pallas kernels for 0%

profile of v2, /device:TPU:16, one launch (start us, length us, event | category | flops | bytes accessed | tf_op | source)
XLA Modules:
  0.0 166.4 jit_solution(16542474235689207976)
XLA Ops:
  0.0 0.0 copy-start
  0.0 1.1 broadcast_in_dim.20
  1.1 22.0 %all_to_all.40 = bf16[4,128,1280]{2,1,0:T(8,128)(2,1)S(1)} all-to-all(bf16[4,128,1280]{2,1,0:T(8,128)(2,1)S(1)} %broadcast_in_dim.20), channel_id=1, replica_groups=mesh['y'=8,'z'=8,'x'=4,'c'=2] {'x'}, dimensions={0} | all-to-all | bytes 2621440 | tf_op jit(solution)/shard_map/all_to_all | solution.py:19
  23.1 1.9 %collective-permute-start = (bf16[512,1280]{1,0:T(8,128)(2,1)S(1)}, bf16[512,1280]{1,0:T(8,128)(2,1)S(1)}, u32[]{:S(2)}, u32[]{:S(2)}) collective-permute-start(bf16[512,1280]{1,0:T(8,128)(2,1)S(1)} %bitcast.20), channel_id=1, source_target_pairs={{0,1},{1,0},{2,3},{3,2},{4,5},{5,4},{6,7},{7,6},{8,9},{9,8},{10,11... | collective-permute-start | bytes 3932168 | tf_op jit(solution)/shard_map/ppermute | solution.py:33
  25.1 0.9 fusion.8
  25.9 2.1 %collective-permute-done = bf16[512,1280]{1,0:T(8,128)(2,1)S(1)} collective-permute-done((bf16[512,1280]{1,0:T(8,128)(2,1)S(1)}, bf16[512,1280]{1,0:T(8,128)(2,1)S(1)}, u32[]{:S(2)}, u32[]{:S(2)}) %collective-permute-start) | collective-permute-done | bytes 1310752 | tf_op jit(solution)/shard_map/ppermute | solution.py:33
  28.1 0.9 fusion.9
  28.9 0.2 pad_maximum_fusion
  29.1 41.4 %all_to_all.41 = f16[64,16,384]{2,1,0:T(8,128)(2,1)S(1)} all-to-all(f16[64,16,384]{2,1,0:T(8,128)(2,1)S(1)} %bitcast.19), channel_id=1, replica_groups=mesh['y'=8,'z'=8,'x'=4,'c'=2] {'y','z'}, dimensions={0} | all-to-all | bytes 1572864 | tf_op jit(solution)/shard_map/all_to_all | solution.py:41
  70.6 0.1 convert_reduce_fusion.2
  70.7 0.9 broadcast_in_dim.21
  71.7 5.4 %all-to-all-start.2 = ((bf16[64,16,384]{2,1,0:T(8,128)(2,1)}), bf16[64,16,384]{2,1,0:T(8,128)(2,1)S(1)}, u32[]{:S(2)}, u32[]{:S(2)}) async-start(bf16[64,16,384]{2,1,0:T(8,128)(2,1)} %broadcast_in_dim.21), calls=%async_computation.2 | async-start | bytes 1572864 | tf_op jit(solution)/shard_map/all_to_all | solution.py:19
  77.1 24.8 %all-to-all-done.2 = bf16[64,16,384]{2,1,0:T(8,128)(2,1)S(1)} async-done(((bf16[64,16,384]{2,1,0:T(8,128)(2,1)}), bf16[64,16,384]{2,1,0:T(8,128)(2,1)S(1)}, u32[]{:S(2)}, u32[]{:S(2)}) %all-to-all-start.2) | async-done | bytes 786464 | tf_op jit(solution)/shard_map/all_to_all | solution.py:19
  101.9 0.2 convert_reduce_fusion
  102.1 0.1 reshape.108
  102.2 0.1 rev.24
  102.4 7.8 %all_to_all.42 = f32[8,8,128]{2,1,0:T(8,128)S(1)} all-to-all(f32[8,8,128]{2,1,0:T(8,128)S(1)} %broadcast_in_dim.23), channel_id=1, replica_groups=mesh['y'=8,'z'=8,'x'=4,'c'=2] {'x','c'}, dimensions={0} | all-to-all | bytes 65536 | tf_op jit(solution)/shard_map/all_to_all | solution.py:52
  110.2 0.1 rev.25
  110.4 0.1 div.62
  110.4 0.3 fusion
  110.7 0.2 fusion.1
  110.9 0.1 reshape.109
  111.0 0.1 rev.26
  111.2 7.8 %all_to_all.43 = f32[8,8,128]{2,1,0:T(8,128)S(1)} all-to-all(f32[8,8,128]{2,1,0:T(8,128)S(1)} %broadcast_in_dim.25), channel_id=1, replica_groups=mesh['y'=8,'z'=8,'x'=4,'c'=2] {'x','c'}, dimensions={0} | all-to-all | bytes 65536 | tf_op jit(solution)/shard_map/all_to_all | solution.py:52
  119.0 0.1 rev.27
  119.2 0.1 div.65
  119.3 0.3 fusion.2
  119.5 0.2 fusion.3
  119.8 0.1 reshape.110
  119.9 0.1 rev.28
  120.0 7.8 %all_to_all.44 = f32[8,8,128]{2,1,0:T(8,128)S(1)} all-to-all(f32[8,8,128]{2,1,0:T(8,128)S(1)} %broadcast_in_dim.54), channel_id=1, replica_groups=mesh['y'=8,'z'=8,'x'=4,'c'=2] {'x','c'}, dimensions={0} | all-to-all | bytes 65536 | tf_op jit(solution)/shard_map/all_to_all | solution.py:52
  127.9 0.1 rev.29
  128.0 0.1 div.68
  128.1 0.3 fusion.4
  128.4 0.2 fusion.5
  128.6 0.1 reshape.111
  128.7 0.1 rev.30
  128.9 7.8 %all_to_all.45 = f32[8,8,128]{2,1,0:T(8,128)S(1)} all-to-all(f32[8,8,128]{2,1,0:T(8,128)S(1)} %broadcast_in_dim.56), channel_id=1, replica_groups=mesh['y'=8,'z'=8,'x'=4,'c'=2] {'x','c'}, dimensions={0} | all-to-all | bytes 65536 | tf_op jit(solution)/shard_map/all_to_all | solution.py:52
  136.7 0.1 rev.31
  136.9 0.2 fusion.7
  137.1 0.8 convolution_convert_fusion
  138.0 1.9 %collective-permute-start.1 = (bf16[512,1280]{1,0:T(8,128)(2,1)S(1)}, bf16[512,1280]{1,0:T(8,128)(2,1)S(1)}, u32[]{:S(2)}, u32[]{:S(2)}) collective-permute-start(bf16[512,1280]{1,0:T(8,128)(2,1)S(1)} %convolution_convert_fusion), channel_id=1, source_target_pairs={{0,1},{1,0},{2,3},{3,2},{4,5},{5,4},{6,7},{7,6},{8,9},{9,8},{10,11... | collective-permute-start | bytes 3932168 | tf_op jit(solution)/shard_map/ppermute | solution.py:63
  139.9 3.0 %collective-permute-done.1 = bf16[512,1280]{1,0:T(8,128)(2,1)S(1)} collective-permute-done((bf16[512,1280]{1,0:T(8,128)(2,1)S(1)}, bf16[512,1280]{1,0:T(8,128)(2,1)S(1)}, u32[]{:S(2)}, u32[]{:S(2)}) %collective-permute-start.1) | collective-permute-done | bytes 1310752 | tf_op jit(solution)/shard_map/ppermute | solution.py:63
  142.9 0.8 add_convert_fusion
  143.7 20.9 %all_to_all.46 = bf16[4,128,1280]{2,1,0:T(8,128)(2,1)S(1)} all-to-all(bf16[4,128,1280]{2,1,0:T(8,128)(2,1)S(1)} %bitcast.18), channel_id=1, replica_groups=mesh['y'=8,'z'=8,'x'=4,'c'=2] {'x'}, dimensions={0} | all-to-all | bytes 2621440 | tf_op jit(solution)/shard_map/all_to_all | solution.py:66
  164.7 0.2 convert_reduce_fusion.1
  164.8 0.8 copy-done.1
  165.6 0.8 subtract_convert_fusion
  (31 shorter events, 0.2 us)
Async XLA Ops:
  0.0 25.1 %copy-start = (bf16[384,1280]{1,0:T(8,128)(2,1)S(1)}, bf16[384,1280]{1,0:T(8,128)(2,1)}, u32[]{:S(2)}) copy-start(bf16[384,1280]{1,0:T(8,128)(2,1)} %param.3) | copy-start | bytes 2949124
  23.1 4.9 %collective-permute-start = (bf16[512,1280]{1,0:T(8,128)(2,1)S(1)}, bf16[512,1280]{1,0:T(8,128)(2,1)S(1)}, u32[]{:S(2)}, u32[]{:S(2)}) collective-permute-start(bf16[512,1280]{1,0:T(8,128)(2,1)S(1)} %bitcast.20), channel_id=1, source_target_pairs={{0,1},{1,0},{2,3},{3,2},{4,5},{5,4},{6,7},{7,6},{8,9},{9,8},{10,11... | collective-permute-start | bytes 3932168 | tf_op jit(solution)/shard_map/ppermute | solution.py:33
  71.7 30.2 %all-to-all-start.2 = ((bf16[64,16,384]{2,1,0:T(8,128)(2,1)}), bf16[64,16,384]{2,1,0:T(8,128)(2,1)S(1)}, u32[]{:S(2)}, u32[]{:S(2)}) async-start(bf16[64,16,384]{2,1,0:T(8,128)(2,1)} %broadcast_in_dim.21), calls=%async_computation.2 | async-start | bytes 1572864 | tf_op jit(solution)/shard_map/all_to_all | solution.py:19
  138.0 4.9 %collective-permute-start.1 = (bf16[512,1280]{1,0:T(8,128)(2,1)S(1)}, bf16[512,1280]{1,0:T(8,128)(2,1)S(1)}, u32[]{:S(2)}, u32[]{:S(2)}) collective-permute-start(bf16[512,1280]{1,0:T(8,128)(2,1)S(1)} %convolution_convert_fusion), channel_id=1, source_target_pairs={{0,1},{1,0},{2,3},{3,2},{4,5},{5,4},{6,7},{7,6},{8,9},{9,8},{10,11... | collective-permute-start | bytes 3932168 | tf_op jit(solution)/shard_map/ppermute | solution.py:63
  164.7 1.0 copy-start.1

commit v3 on v2

v3 whole, which is shorter than its diff:
```python
import math

import jax
import jax.numpy as jnp
from jax import lax
from jax.sharding import Mesh
from jax.sharding import PartitionSpec as P

F = 81920
BALANCE_ROUNDS = 3
Y, Z, X, C = 8, 8, 4, 2
WIDE = ("y", "z")
NARROW = ("x", "c")
SWAP = [(0, 1), (1, 0)]
SEND_SCALE = 64.0


def gather_by_a2a(block, axes, n):
    return lax.all_to_all(jnp.broadcast_to(block[None], (n, *block.shape)), axes, 0, 0).reshape(
        n * block.shape[0], block.shape[1]
    )


def body(noise, latents):
    draws, features = noise.shape
    total_noise = draws * X * C
    total_clips = latents.shape[0] * X * C
    rows = draws * X
    clips = latents.shape[0] * C

    other = lax.ppermute(latents, "c", SWAP)
    chip_latents = jnp.where(
        lax.axis_index("c") == 0,
        jnp.concatenate([latents, other], axis=0),
        jnp.concatenate([other, latents], axis=0),
    )
    noise_rows = gather_by_a2a(noise, "x", X)
    scores = lax.dot_general(noise_rows, chip_latents, (((1,), (1,)), ((), ())), preferred_element_type=jnp.float32)
    partial = (scores * (SEND_SCALE / math.sqrt(F))).astype(jnp.float16)
    arrived = lax.all_to_all(partial.reshape(Y * Z, rows // (Y * Z), clips), WIDE, 0, 0)
    block = jnp.exp(jnp.sum(arrived.astype(jnp.float32), axis=0) * (1.0 / SEND_SCALE))
    kernel = gather_by_a2a(block.astype(jnp.bfloat16), WIDE, Y * Z).astype(jnp.float32)

    col_scale = jnp.ones((clips,), jnp.float32)
    for _ in range(BALANCE_ROUNDS):
        part = jnp.sum(kernel * col_scale[None, :], axis=1).reshape(1, rows // 128, 128)
        parts = lax.all_to_all(jnp.broadcast_to(part, (X, *part.shape[1:])), "x", 0, 0)
        row_scale = 1.0 / total_noise / jnp.sum(parts, axis=0).reshape(rows)
        col_scale = 1.0 / total_clips / lax.psum(jnp.sum(kernel * row_scale[:, None], axis=0), "c")

    plan = kernel * col_scale[None, :] * (row_scale * total_noise)[:, None]
    partial_target = jnp.dot(plan.astype(jnp.bfloat16), chip_latents, preferred_element_type=jnp.float32)
    parts = lax.all_to_all(partial_target.astype(jnp.bfloat16).reshape(X, draws, features), "x", 0, 0)
    final_total = lax.psum(jnp.sum(plan, axis=1).reshape(X, draws), "x")
    own_total = lax.dynamic_index_in_dim(final_total, lax.axis_index("x"), 0, keepdims=False)
    target = jnp.sum(parts.astype(jnp.float32), axis=0) / own_total[:, None]
    return (target - noise.astype(jnp.float32)).astype(jnp.bfloat16)


def solution(mesh):
    mesh = Mesh(mesh.devices.reshape(Y, Z, X, C), (*WIDE, *NARROW))
    spec = P(NARROW, WIDE)
    return jax.shard_map(body, mesh=mesh, in_specs=(spec, spec), out_specs=spec, check_vma=False)
```

time: 167 us -> 156 us (0.934)
  waiting for transfers between devices: 29.9 us -> 16 us
  blocking collectives: 116 us -> 120 us
  local copies, waits for them, and re-layouts: 4.58 us -> 2.84 us
    all_to_all x6 -> x4, blocking collectives: 93.6 us -> 63 us  [the longest x1 40.1 us: body(): lax.all_to_all(partial.reshape(Y * Z, rows // (Y * Z), clips), WIDE, 0, 0)]
    psum x0 -> x4, blocking collectives: none -> 27.8 us  [the longest x1 20.3 us: body(): final_total = lax.psum(jnp.sum(plan, axis=1).reshape(X, draws), 'x')]
    all_to_all x1, waiting for transfers between devices: 24.8 us -> 16 us  [gather_by_a2a(): lax.all_to_all(jnp.broadcast_to(block[None], (n, *block.shape)), axes, 0, 0)]
    all_to_all x1, blocking collectives: 22 us -> 28.8 us  [gather_by_a2a(): lax.all_to_all(jnp.broadcast_to(block[None], (n, *block.shape)), axes, 0, 0)]
    ppermute x2 -> x1, waiting for transfers between devices: 5.12 us -> 0.01 us  [body(): other = lax.ppermute(latents, 'c', SWAP)]
    all_to_all x0 -> x1, starting transfers between devices: none -> 3.54 us  [body(): lax.all_to_all(partial_target.astype(jnp.bfloat16).reshape(X, draws, feat...]
    ppermute x2 -> x1, starting transfers between devices: 3.83 us -> 1.91 us  [body(): other = lax.ppermute(latents, 'c', SWAP)]
    dot_general x4 -> x2, matrix products: 3.42 us -> 3.68 us  [the longest x1 2.41 us: body(): jnp.dot(plan.astype(jnp.bfloat16), chip_latents, preferred_element_type=j...]
  transfers between devices with their start and end apart: 3 -> 3, of which waited for: 3 -> 1; matrix products, arithmetic and copies ran while one was open for 1% -> 0% of each run, Pallas kernels for 0% -> 0%
where the time goes in v3:
time: 156 us; the launch traced here: 155 us
  blocking collectives  120 us (77%)
  waiting for transfers between devices  16 us (10%)
  starting transfers between devices  9.87 us (6%)
  matrix products  3.68 us (2%)
  other arithmetic  2.94 us (2%)
  local copies, waits for them, and re-layouts  2.84 us (2%)
    all_to_all x1, blocking collectives, body(): lax.all_to_all(partial.reshape(Y * Z, rows // (Y * Z), clips), WIDE, 0, 0)  40.1 us
    all_to_all x1, blocking collectives, gather_by_a2a(): lax.all_to_all(jnp.broadcast_to(block[None], (n, *block.shape)), axes, 0, 0)  28.8 us
    all_to_all x3, blocking collectives, body(): lax.all_to_all(jnp.broadcast_to(part, (X, *part.shape[1:])), 'x', 0, 0)  23 us
    psum x1, blocking collectives, body(): final_total = lax.psum(jnp.sum(plan, axis=1).reshape(X, draws), 'x')  20.3 us
    all_to_all x1, waiting for transfers between devices, gather_by_a2a(): lax.all_to_all(jnp.broadcast_to(block[None], (n, *block.shape)), axes, 0, 0)  16 us
    psum x3, blocking collectives, body(): lax.psum(jnp.sum(kernel * row_scale[:, None], axis=0), 'c')  7.55 us
    all_to_all x1, starting transfers between devices, gather_by_a2a(): lax.all_to_all(jnp.broadcast_to(block[None], (n, *block.shape)), axes, 0, 0)  4.42 us
    all_to_all x1, starting transfers between devices, body(): lax.all_to_all(partial_target.astype(jnp.bfloat16).reshape(X, draws, feat...  3.54 us
  transfers between devices with their start and end apart: 3, of which 1 were waited for; matrix products, arithmetic and copies ran while one was open for 0% of the time, Pallas kernels for 0%

profile of v3, /device:TPU:16, one launch (start us, length us, event | category | flops | bytes accessed | tf_op | source)
XLA Modules:
  0.0 155.2 jit_solution(6570270738921045317)
XLA Ops:
  0.0 2.1 %broadcast_in_dim.16 = bf16[4,128,1280]{2,1,0:T(8,128)(2,1)} broadcast(bf16[128,1280]{1,0:T(8,128)(2,1)} %param.2), dimensions={1,2} | broadcast | bytes 1638400 | tf_op jit(solution)/shard_map/broadcast_in_dim | solution.py:19
  2.1 0.0 copy-start.1
  2.1 4.4 %all-to-all-start = ((bf16[4,128,1280]{2,1,0:T(8,128)(2,1)}), bf16[4,128,1280]{2,1,0:T(8,128)(2,1)S(1)}, u32[]{:S(2)}, u32[]{:S(2)}) async-start(bf16[4,128,1280]{2,1,0:T(8,128)(2,1)} %broadcast_in_dim.16), calls=%async_computation | async-start | bytes 2621440 | tf_op jit(solution)/shard_map/all_to_all | solution.py:19
  6.5 0.0 copy-done.1
  6.5 1.9 %collective-permute-start = (bf16[384,1280]{1,0:T(8,128)(2,1)S(1)}, bf16[384,1280]{1,0:T(8,128)(2,1)S(1)}, u32[]{:S(2)}, u32[]{:S(2)}) collective-permute-start(bf16[384,1280]{1,0:T(8,128)(2,1)S(1)} %copy-done.1), channel_id=1, source_target_pairs={{0,1},{1,0},{2,3},{3,2},{4,5},{5,4},{6,7},{7,6},{8,9},{9,8},{10,11... | collective-permute-start | bytes 2949128 | tf_op jit(solution)/shard_map/ppermute | solution.py:31
  8.5 16.0 %all-to-all-done = bf16[4,128,1280]{2,1,0:T(8,128)(2,1)S(1)} async-done(((bf16[4,128,1280]{2,1,0:T(8,128)(2,1)}), bf16[4,128,1280]{2,1,0:T(8,128)(2,1)S(1)}, u32[]{:S(2)}, u32[]{:S(2)}) %all-to-all-start) | async-done | bytes 1310752 | tf_op jit(solution)/shard_map/all_to_all | solution.py:19
  24.5 0.0 collective-permute-done
  24.5 0.0 copy-start.2
  24.5 1.3 fusion.10
  25.7 0.0 copy-done.2
  25.7 40.1 %all_to_all.35 = f16[64,8,768]{2,1,0:T(8,128)(2,1)S(1)} all-to-all(f16[64,8,768]{2,1,0:T(8,128)(2,1)S(1)} %fusion.10), channel_id=1, replica_groups=mesh['y'=8,'z'=8,'x'=4,'c'=2] {'y','z'}, dimensions={0} | all-to-all | bytes 1572864 | tf_op jit(solution)/shard_map/all_to_all | solution.py:40
  65.8 0.1 convert_reduce_fusion.2
  66.0 0.1 broadcast_in_dim.17
  66.0 28.8 %all_to_all.36 = bf16[64,8,768]{2,1,0:T(8,128)(2,1)S(1)} all-to-all(bf16[64,8,768]{2,1,0:T(8,128)(2,1)S(1)} %broadcast_in_dim.17), channel_id=1, replica_groups=mesh['y'=8,'z'=8,'x'=4,'c'=2] {'y','z'}, dimensions={0} | all-to-all | bytes 1572864 | tf_op jit(solution)/shard_map/all_to_all | solution.py:19
  94.8 0.2 convert_reduce_fusion
  95.0 0.1 broadcast_in_dim.18
  95.1 7.7 %all_to_all.37 = f32[4,4,128]{2,1,0:T(4,128)S(1)} all-to-all(f32[4,4,128]{2,1,0:T(4,128)S(1)} %broadcast_in_dim.19), channel_id=1, replica_groups=mesh['y'=8,'z'=8,'x'=4,'c'=2] {'x'}, dimensions={0} | all-to-all | bytes 16384 | tf_op jit(solution)/shard_map/all_to_all | solution.py:47
  102.8 0.1 div.55
  102.9 0.2 fusion.3
  103.1 2.5 %psum.28 = f32[768]{0:T(1024)S(1)} all-reduce(f32[768]{0:T(1024)S(1)} %fusion.3), channel_id=1, replica_groups=mesh['y'=8,'z'=8,'x'=4,'c'=2] {'c'}, use_global_device_ids=true, to_apply=%region_4.5 | all-reduce | flops 768 | bytes 6144 | tf_op jit(solution)/shard_map/psum | solution.py:49
  105.6 0.2 fusion.4
  105.8 0.1 broadcast_in_dim.20
  106.0 7.7 %all_to_all.38 = f32[4,4,128]{2,1,0:T(4,128)S(1)} all-to-all(f32[4,4,128]{2,1,0:T(4,128)S(1)} %broadcast_in_dim.21), channel_id=1, replica_groups=mesh['y'=8,'z'=8,'x'=4,'c'=2] {'x'}, dimensions={0} | all-to-all | bytes 16384 | tf_op jit(solution)/shard_map/all_to_all | solution.py:47
  113.6 0.1 div.58
  113.7 0.0 copy-start.3
  113.7 0.2 fusion.5
  114.0 2.6 %psum.29 = f32[768]{0:T(1024)S(1)} all-reduce(f32[768]{0:T(1024)S(1)} %fusion.5), channel_id=1, replica_groups=mesh['y'=8,'z'=8,'x'=4,'c'=2] {'c'}, use_global_device_ids=true, to_apply=%region_8.9 | all-reduce | flops 768 | bytes 6144 | tf_op jit(solution)/shard_map/psum | solution.py:49
  116.6 0.2 fusion.6
  116.8 0.1 broadcast_in_dim.22
  116.9 7.7 %all_to_all.39 = f32[4,4,128]{2,1,0:T(4,128)S(1)} all-to-all(f32[4,4,128]{2,1,0:T(4,128)S(1)} %broadcast_in_dim.23), channel_id=1, replica_groups=mesh['y'=8,'z'=8,'x'=4,'c'=2] {'x'}, dimensions={0} | all-to-all | bytes 16384 | tf_op jit(solution)/shard_map/all_to_all | solution.py:47
  124.6 0.1 div.61
  124.7 0.2 fusion.7
  124.9 2.5 %psum.30 = f32[768]{0:T(1024)S(1)} all-reduce(f32[768]{0:T(1024)S(1)} %fusion.7), channel_id=1, replica_groups=mesh['y'=8,'z'=8,'x'=4,'c'=2] {'c'}, use_global_device_ids=true, to_apply=%region_12.13 | all-reduce | flops 768 | bytes 6144 | tf_op jit(solution)/shard_map/psum | solution.py:49
  127.4 0.0 copy-done.3
  127.4 2.4 %convolution_convert_fusion = bf16[512,1280]{1,0:T(8,128)(2,1)} fusion(bf16[64,8,768]{2,1,0:T(8,128)(2,1)S(1)} %all_to_all.36, f32[512]{0:T(512)S(1)} %get-tuple-element.5, f32[768]{0:T(1024)S(1)} %broadcast_divide_fusion, bf16[384,1280]{1,0:T(8,128)(2,1)S(1)} %copy-done.3, bf16[384,1280]{1,0:T(8,128)(2,1)S(1)} %copy-done.1, pred[]{:T(512)S(6)} %eq.3), kind=kOutput, calls=%fused_computation.8 | convolution fusion | flops 1017708544 | bytes 4068353 | tf_op jit(solution)/shard_map/dot_general | solution.py:52
  129.8 3.5 %all-to-all-start.6 = ((bf16[4,128,1280]{2,1,0:T(8,128)(2,1)}), bf16[4,128,1280]{2,1,0:T(8,128)(2,1)S(1)}, u32[]{:S(2)}, u32[]{:S(2)}) async-start(bf16[4,128,1280]{2,1,0:T(8,128)(2,1)} %bitcast.5), calls=%async_computation.6 | async-start | bytes 2621440 | tf_op jit(solution)/shard_map/all_to_all | solution.py:53
  133.4 0.0 copy-start
  133.4 0.3 fusion.9
  133.7 0.1 reshape.110
  133.8 20.3 %psum.31 = f32[4,128]{1,0:T(4,128)S(1)} all-reduce(f32[4,128]{1,0:T(4,128)S(1)} %reshape.110), channel_id=1, replica_groups=mesh['y'=8,'z'=8,'x'=4,'c'=2] {'x'}, use_global_device_ids=true, to_apply=%region_15.16 | all-reduce | flops 512 | bytes 4096 | tf_op jit(solution)/shard_map/psum | solution.py:54
  154.1 0.0 all-to-all-done.6
  154.1 0.2 convert_reduce_fusion.1
  154.3 0.0 copy-done
  154.3 0.9 subtract_convert_fusion
  (15 shorter events, 0.1 us)
Async XLA Ops:
  2.1 4.4 %copy-start.1 = (bf16[384,1280]{1,0:T(8,128)(2,1)S(1)}, bf16[384,1280]{1,0:T(8,128)(2,1)}, u32[]{:S(2)}) copy-start(bf16[384,1280]{1,0:T(8,128)(2,1)} %param.3) | copy-start | bytes 2949124
  2.1 22.3 %all-to-all-start = ((bf16[4,128,1280]{2,1,0:T(8,128)(2,1)}), bf16[4,128,1280]{2,1,0:T(8,128)(2,1)S(1)}, u32[]{:S(2)}, u32[]{:S(2)}) async-start(bf16[4,128,1280]{2,1,0:T(8,128)(2,1)} %broadcast_in_dim.16), calls=%async_computation | async-start | bytes 2621440 | tf_op jit(solution)/shard_map/all_to_all | solution.py:19
  6.5 17.9 %collective-permute-start = (bf16[384,1280]{1,0:T(8,128)(2,1)S(1)}, bf16[384,1280]{1,0:T(8,128)(2,1)S(1)}, u32[]{:S(2)}, u32[]{:S(2)}) collective-permute-start(bf16[384,1280]{1,0:T(8,128)(2,1)S(1)} %copy-done.1), channel_id=1, source_target_pairs={{0,1},{1,0},{2,3},{3,2},{4,5},{5,4},{6,7},{7,6},{8,9},{9,8},{10,11... | collective-permute-start | bytes 2949128 | tf_op jit(solution)/shard_map/ppermute | solution.py:31
  24.5 1.3 copy-start.2
  113.7 13.7 %copy-start.3 = (bf16[384,1280]{1,0:T(8,128)(2,1)S(1)}, bf16[384,1280]{1,0:T(8,128)(2,1)}, u32[]{:S(2)}) copy-start(bf16[384,1280]{1,0:T(8,128)(2,1)} %copy-done.2) | copy-start | bytes 2949124
  129.8 24.3 %all-to-all-start.6 = ((bf16[4,128,1280]{2,1,0:T(8,128)(2,1)}), bf16[4,128,1280]{2,1,0:T(8,128)(2,1)S(1)}, u32[]{:S(2)}, u32[]{:S(2)}) async-start(bf16[4,128,1280]{2,1,0:T(8,128)(2,1)} %bitcast.5), calls=%async_computation.6 | async-start | bytes 2621440 | tf_op jit(solution)/shard_map/all_to_all | solution.py:53
  133.4 20.9 %copy-start = (bf16[128,1280]{1,0:T(8,128)(2,1)S(1)}, bf16[128,1280]{1,0:T(8,128)(2,1)}, u32[]{:S(2)}) copy-start(bf16[128,1280]{1,0:T(8,128)(2,1)} %param.2) | copy-start | bytes 983044

commit v4 on v3

v4 whole, which is shorter than its diff:
```python
import math

import jax
import jax.numpy as jnp
from jax import lax
from jax.sharding import Mesh
from jax.sharding import PartitionSpec as P

F = 81920
BALANCE_ROUNDS = 3
Y, Z, X, C = 8, 8, 4, 2
WIDE = ("y", "z")
NARROW = ("x", "c")
SWAP = [(0, 1), (1, 0)]
SEND_SCALE = 64.0
LANES = 128
TILE = 8


def gather_by_a2a(block, axes, n):
    return lax.all_to_all(jnp.broadcast_to(block[None], (n, *block.shape)), axes, 0, 0).reshape(
        n * block.shape[0], block.shape[1]
    )


def sum_over_x(*parts):
    sizes = [p.shape[0] // LANES for p in parts]
    send = jnp.concatenate([p.reshape(1, -1, LANES) for p in parts], axis=1)
    total = jnp.sum(lax.all_to_all(jnp.broadcast_to(send, (X, *send.shape[1:])), "x", 0, 0), axis=0)
    out, at = [], 0
    for size in sizes:
        out.append(total[at : at + size].reshape(size * LANES))
        at += size
    return out


def body(noise, latents):
    draws, features = noise.shape
    total_noise = draws * X * C
    total_clips = latents.shape[0] * X * C
    rows = draws * X
    clips = latents.shape[0] * C

    other = lax.ppermute(latents, "c", SWAP)
    chip_latents = jnp.where(
        lax.axis_index("c") == 0,
        jnp.concatenate([latents, other], axis=0),
        jnp.concatenate([other, latents], axis=0),
    )
    noise_rows = gather_by_a2a(noise, "x", X)
    scores = lax.dot_general(noise_rows, chip_latents, (((1,), (1,)), ((), ())), preferred_element_type=jnp.float32)
    partial = (scores * (SEND_SCALE / math.sqrt(F))).astype(jnp.float16)
    arrived = lax.all_to_all(partial.reshape(Y * Z, rows // (Y * Z), clips), WIDE, 0, 0)
    block = jnp.exp(jnp.sum(arrived.astype(jnp.float32), axis=0) * (1.0 / SEND_SCALE))
    own = gather_by_a2a(block.astype(jnp.bfloat16), WIDE, Y * Z)
    halves = [own, lax.ppermute(own, "c", SWAP)]

    def row_part(kernel, col_scale):
        return jnp.sum(kernel.astype(jnp.float32) * col_scale[None, :], axis=1)

    def col_part(kernel, row_scale):
        return jnp.sum(kernel.astype(jnp.float32) * row_scale[:, None], axis=0)

    (row_total,) = sum_over_x(jnp.sum(own.astype(jnp.float32), axis=1))
    row_scale = 1.0 / total_noise / row_total
    col_scale = 1.0 / total_clips / lax.psum(col_part(own, row_scale), "c")
    for _ in range(BALANCE_ROUNDS - 1):
        row_scales = [1.0 / total_noise / t for t in sum_over_x(*(row_part(k, col_scale) for k in halves))]
        row_scale = row_scales[0]
        col_scale = 1.0 / total_clips / (col_part(halves[0], row_scales[0]) + col_part(halves[1], row_scales[1]))

    plan = own.astype(jnp.float32) * col_scale[None, :] * (row_scale * total_noise)[:, None]
    weights = lax.optimization_barrier(plan.astype(jnp.bfloat16))
    last = jnp.sum(plan, axis=1).reshape(X, 1, draws)
    high = lax.reduce_precision(last, 8, 7)
    totals = jnp.concatenate([high, last - high], axis=1).astype(jnp.bfloat16)
    totals = jnp.pad(totals, ((0, 0), (0, TILE - 2), (0, features - draws)))
    partial_target = jnp.dot(weights, chip_latents, preferred_element_type=jnp.float32).astype(jnp.bfloat16)
    send = jnp.concatenate([partial_target.reshape(X, draws, features), totals], axis=1)
    parts = jnp.sum(lax.all_to_all(send, "x", 0, 0).astype(jnp.float32), axis=0)
    own_total = parts[draws, :draws] + parts[draws + 1, :draws]
    return (parts[:draws] / own_total[:, None] - noise.astype(jnp.float32)).astype(jnp.bfloat16)


def solution(mesh):
    mesh = Mesh(mesh.devices.reshape(Y, Z, X, C), (*WIDE, *NARROW))
    spec = P(NARROW, WIDE)
    return jax.shard_map(body, mesh=mesh, in_specs=(spec, spec), out_specs=spec, check_vma=False)
```

time: 156 us -> 152 us (0.974)
  blocking collectives: 120 us -> 114 us
  matrix products: 3.68 us -> 5.56 us
  starting transfers between devices: 9.87 us -> 8.24 us
    psum x4 -> x1, blocking collectives: 27.8 us -> 2.47 us  [body(): col_scale = 1.0 / total_clips / lax.psum(col_part(own, row_scale), 'c')]
    all_to_all x3 -> x4, blocking collectives: 23 us -> 42.6 us  [the longest x3 23.1 us: sum_over_x(): lax.all_to_all(jnp.broadcast_to(send, (X, *send.shape[1:])), 'x', 0, 0)]
    all_to_all x1 -> x0, starting transfers between devices: 3.54 us -> none  [body(): lax.all_to_all(partial_target.astype(jnp.bfloat16).reshape(X, draws, feat...]
    ppermute x0 -> x1, starting transfers between devices: none -> 1.91 us  [body(): halves = [own, lax.ppermute(own, 'c', SWAP)]]
  transfers between devices with their start and end apart: 3 -> 3, of which waited for: 1 -> 1; matrix products, arithmetic and copies ran while one was open for 0% -> 1% of each run, Pallas kernels for 0% -> 0%
where the time goes in v4:
time: 152 us
  blocking collectives  114 us (75%)
  waiting for transfers between devices  16 us (11%)
  starting transfers between devices  8.24 us (5%)
  matrix products  5.56 us (4%)
  other arithmetic  4.22 us (3%)
  local copies, waits for them, and re-layouts  3.58 us (2%)
    all_to_all x1, blocking collectives, body(): lax.all_to_all(partial.reshape(Y * Z, rows // (Y * Z), clips), WIDE, 0, 0)  40.1 us
    all_to_all x1, blocking collectives, gather_by_a2a(): lax.all_to_all(jnp.broadcast_to(block[None], (n, *block.shape)), axes, 0, 0)  28.8 us
    all_to_all x3, blocking collectives, sum_over_x(): lax.all_to_all(jnp.broadcast_to(send, (X, *send.shape[1:])), 'x', 0, 0)  23.1 us
    all_to_all x1, blocking collectives, body(): parts = jnp.sum(lax.all_to_all(send, 'x', 0, 0).astype(jnp.float32), axis=0)  19.5 us
    all_to_all x1, waiting for transfers between devices, gather_by_a2a(): lax.all_to_all(jnp.broadcast_to(block[None], (n, *block.shape)), axes, 0, 0)  16 us
    all_to_all x1, starting transfers between devices, gather_by_a2a(): lax.all_to_all(jnp.broadcast_to(block[None], (n, *block.shape)), axes, 0, 0)  4.42 us
  transfers between devices with their start and end apart: 3, of which 1 were waited for; matrix products, arithmetic and copies ran while one was open for 1% of the time, Pallas kernels for 0%

profile of v4, /device:TPU:16, one launch (start us, length us, event | category | flops | bytes accessed | tf_op | source)
XLA Modules:
  0.0 151.8 jit_solution(11364398777288924661)
XLA Ops:
  0.0 2.1 %broadcast_in_dim.16 = bf16[4,128,1280]{2,1,0:T(8,128)(2,1)} broadcast(bf16[128,1280]{1,0:T(8,128)(2,1)} %param.2), dimensions={1,2} | broadcast | bytes 1638400 | tf_op jit(solution)/shard_map/broadcast_in_dim | solution.py:21
  2.1 0.0 copy-start.1
  2.1 4.4 %all-to-all-start = ((bf16[4,128,1280]{2,1,0:T(8,128)(2,1)}), bf16[4,128,1280]{2,1,0:T(8,128)(2,1)S(1)}, u32[]{:S(2)}, u32[]{:S(2)}) async-start(bf16[4,128,1280]{2,1,0:T(8,128)(2,1)} %broadcast_in_dim.16), calls=%async_computation | async-start | bytes 2621440 | tf_op jit(solution)/shard_map/all_to_all | solution.py:21
  6.5 0.0 copy-done.1
  6.5 1.9 %collective-permute-start = (bf16[384,1280]{1,0:T(8,128)(2,1)S(1)}, bf16[384,1280]{1,0:T(8,128)(2,1)}, u32[]{:S(2)}, u32[]{:S(2)}) collective-permute-start(bf16[384,1280]{1,0:T(8,128)(2,1)S(1)} %copy-done.1), channel_id=1, source_target_pairs={{0,1},{1,0},{2,3},{3,2},{4,5},{5,4},{6,7},{7,6},{8,9},{9,8},{10,11... | collective-permute-start | bytes 2949128 | tf_op jit(solution)/shard_map/ppermute | solution.py:44
  8.5 16.0 %all-to-all-done = bf16[4,128,1280]{2,1,0:T(8,128)(2,1)S(1)} async-done(((bf16[4,128,1280]{2,1,0:T(8,128)(2,1)}), bf16[4,128,1280]{2,1,0:T(8,128)(2,1)S(1)}, u32[]{:S(2)}, u32[]{:S(2)}) %all-to-all-start) | async-done | bytes 1310752 | tf_op jit(solution)/shard_map/all_to_all | solution.py:21
  24.5 0.0 collective-permute-done
  24.5 2.8 %fusion.13 = f16[64,8,768]{2,1,0:T(8,128)(2,1)S(1)} fusion(bf16[512,1280]{1,0:T(8,128)(2,1)S(1)} %bitcast.25, bf16[384,1280]{1,0:T(8,128)(2,1)} %collective-permute-done, bf16[384,1280]{1,0:T(8,128)(2,1)S(1)} %copy-done.1, pred[]{:T(512)S(6)} %eq.3), kind=kOutput, calls=%fused_computation.31 | convolution fusion | flops 1016266752 | bytes 4063233 | tf_op jit(solution)/shard_map/dot_general | solution.py:51
  27.2 40.1 %all_to_all.35 = f16[64,8,768]{2,1,0:T(8,128)(2,1)S(1)} all-to-all(f16[64,8,768]{2,1,0:T(8,128)(2,1)S(1)} %fusion.13), channel_id=1, replica_groups=mesh['y'=8,'z'=8,'x'=4,'c'=2] {'y','z'}, dimensions={0} | all-to-all | bytes 1572864 | tf_op jit(solution)/shard_map/all_to_all | solution.py:53
  67.3 0.1 convert_reduce_fusion.2
  67.5 0.1 broadcast_in_dim.17
  67.5 28.8 %all_to_all.36 = bf16[64,8,768]{2,1,0:T(8,128)(2,1)S(1)} all-to-all(bf16[64,8,768]{2,1,0:T(8,128)(2,1)S(1)} %broadcast_in_dim.17), channel_id=1, replica_groups=mesh['y'=8,'z'=8,'x'=4,'c'=2] {'y','z'}, dimensions={0} | all-to-all | bytes 1572864 | tf_op jit(solution)/shard_map/all_to_all | solution.py:21
  96.3 1.9 %collective-permute-start.1 = (bf16[512,768]{1,0:T(8,128)(2,1)S(1)}, bf16[512,768]{1,0:T(8,128)(2,1)S(1)}, u32[]{:S(2)}, u32[]{:S(2)}) collective-permute-start(bf16[512,768]{1,0:T(8,128)(2,1)S(1)} %bitcast.24), channel_id=1, source_target_pairs={{0,1},{1,0},{2,3},{3,2},{4,5},{5,4},{6,7},{7,6},{8,9},{9,8},{10,11... | collective-permute-start | bytes 2359304 | tf_op jit(solution)/shard_map/ppermute | solution.py:56
  98.3 0.2 convert_reduce_fusion
  98.4 0.1 broadcast_in_dim.18
  98.5 7.7 %all_to_all.37 = f32[4,4,128]{2,1,0:T(4,128)S(1)} all-to-all(f32[4,4,128]{2,1,0:T(4,128)S(1)} %broadcast_in_dim.19), channel_id=1, replica_groups=mesh['y'=8,'z'=8,'x'=4,'c'=2] {'x'}, dimensions={0} | all-to-all | bytes 16384 | tf_op jit(solution)/shard_map/all_to_all | solution.py:29
  106.2 0.1 div.81
  106.3 0.2 fusion.5
  106.5 2.5 %psum.7 = f32[768]{0:T(1024)S(1)} all-reduce(f32[768]{0:T(1024)S(1)} %fusion.5), channel_id=1, replica_groups=mesh['y'=8,'z'=8,'x'=4,'c'=2] {'c'}, use_global_device_ids=true, to_apply=%region_4.5 | all-reduce | flops 768 | bytes 6144 | tf_op jit(solution)/shard_map/psum | solution.py:66
  109.0 0.2 fusion.6
  109.3 0.1 reshape.183
  109.4 0.0 collective-permute-done.1
  109.4 0.2 fusion.1
  109.6 7.7 %all_to_all.38 = f32[4,8,128]{2,1,0:T(8,128)S(1)} all-to-all(f32[4,8,128]{2,1,0:T(8,128)S(1)} %broadcast_in_dim.21), channel_id=1, replica_groups=mesh['y'=8,'z'=8,'x'=4,'c'=2] {'x'}, dimensions={0} | all-to-all | bytes 32768 | tf_op jit(solution)/shard_map/all_to_all | solution.py:29
  117.3 0.1 div.84
  117.4 0.2 fusion.7
  117.7 0.2 fusion.2
  117.9 0.2 fusion.8
  118.1 0.1 reshape.185
  118.2 0.2 fusion.3
  118.5 7.7 %all_to_all.39 = f32[4,8,128]{2,1,0:T(8,128)S(1)} all-to-all(f32[4,8,128]{2,1,0:T(8,128)S(1)} %broadcast_in_dim.23), channel_id=1, replica_groups=mesh['y'=8,'z'=8,'x'=4,'c'=2] {'x'}, dimensions={0} | all-to-all | bytes 32768 | tf_op jit(solution)/shard_map/all_to_all | solution.py:29
  126.2 0.1 div.89
  126.3 0.2 fusion.9
  126.6 0.2 fusion.4
  126.8 0.3 fusion.11
  127.1 0.1 reshape.188
  127.3 0.2 multiply_convert_fusion
  127.5 2.8 %convolution_convert_fusion = bf16[512,1280]{1,0:T(8,128)(2,1)S(1)} fusion(bf16[512,768]{1,0:T(8,128)(2,1)S(1)} %multiply_convert_fusion, bf16[384,1280]{1,0:T(8,128)(2,1)} %collective-permute-done, bf16[384,1280]{1,0:T(8,128)(2,1)S(1)} %copy-done.1, pred[]{:T(512)S(6)} %eq.3), kind=kOutput, calls=%fused_computation.7 | convolution fusion | flops 1016135680 | bytes 4063233 | tf_op jit(solution)/shard_map/dot_general | solution.py:78
  130.3 0.1 fusion.12
  130.4 19.5 %all_to_all.40 = bf16[4,136,1280]{2,1,0:T(8,128)(2,1)S(1)} all-to-all(bf16[4,136,1280]{2,1,0:T(8,128)(2,1)S(1)} %fusion.12), channel_id=1, replica_groups=mesh['y'=8,'z'=8,'x'=4,'c'=2] {'x'}, dimensions={0} | all-to-all | bytes 2785280 | tf_op jit(solution)/shard_map/all_to_all | solution.py:80
  149.9 0.0 copy-start
  149.9 0.2 convert_reduce_fusion.1
  150.1 0.8 copy-done
  150.9 0.9 fusion.15
  (20 shorter events, 0.2 us)
Async XLA Ops:
  2.1 4.4 %copy-start.1 = (bf16[384,1280]{1,0:T(8,128)(2,1)S(1)}, bf16[384,1280]{1,0:T(8,128)(2,1)}, u32[]{:S(2)}) copy-start(bf16[384,1280]{1,0:T(8,128)(2,1)} %param.3) | copy-start | bytes 2949124
  2.1 22.3 %all-to-all-start = ((bf16[4,128,1280]{2,1,0:T(8,128)(2,1)}), bf16[4,128,1280]{2,1,0:T(8,128)(2,1)S(1)}, u32[]{:S(2)}, u32[]{:S(2)}) async-start(bf16[4,128,1280]{2,1,0:T(8,128)(2,1)} %broadcast_in_dim.16), calls=%async_computation | async-start | bytes 2621440 | tf_op jit(solution)/shard_map/all_to_all | solution.py:21
  6.5 17.9 %collective-permute-start = (bf16[384,1280]{1,0:T(8,128)(2,1)S(1)}, bf16[384,1280]{1,0:T(8,128)(2,1)}, u32[]{:S(2)}, u32[]{:S(2)}) collective-permute-start(bf16[384,1280]{1,0:T(8,128)(2,1)S(1)} %copy-done.1), channel_id=1, source_target_pairs={{0,1},{1,0},{2,3},{3,2},{4,5},{5,4},{6,7},{7,6},{8,9},{9,8},{10,11... | collective-permute-start | bytes 2949128 | tf_op jit(solution)/shard_map/ppermute | solution.py:44
  96.3 13.0 %collective-permute-start.1 = (bf16[512,768]{1,0:T(8,128)(2,1)S(1)}, bf16[512,768]{1,0:T(8,128)(2,1)S(1)}, u32[]{:S(2)}, u32[]{:S(2)}) collective-permute-start(bf16[512,768]{1,0:T(8,128)(2,1)S(1)} %bitcast.24), channel_id=1, source_target_pairs={{0,1},{1,0},{2,3},{3,2},{4,5},{5,4},{6,7},{7,6},{8,9},{9,8},{10,11... | collective-permute-start | bytes 2359304 | tf_op jit(solution)/shard_map/ppermute | solution.py:56
  149.9 1.0 copy-start

commit v5 on v4

v5 whole, which is shorter than its diff:
```python
import math

import jax
import jax.numpy as jnp
from jax import lax
from jax.sharding import Mesh
from jax.sharding import PartitionSpec as P

F = 81920
BALANCE_ROUNDS = 3
Y, Z, X, C = 8, 8, 4, 2
WIDE = ("y", "z")
NARROW = ("x", "c")
SWAP = [(0, 1), (1, 0)]
SEND_SCALE = 64.0
LANES = 128
TILE = 8


def gather_by_a2a(block, axes, n):
    return lax.all_to_all(jnp.broadcast_to(block[None], (n, *block.shape)), axes, 0, 0)


def sum_over_x(*parts):
    shape = parts[0].shape
    send = jnp.concatenate([p.reshape(1, -1, LANES) for p in parts], axis=1)
    total = jnp.sum(lax.all_to_all(jnp.broadcast_to(send, (X, *send.shape[1:])), "x", 0, 0), axis=0)
    return total.reshape(len(parts), *shape)


def row_part(kernel, col_scale):
    return jnp.sum(kernel.astype(jnp.float32) * col_scale[None, :, None, :], axis=(1, 3))


def col_part(kernel, row_scale):
    return jnp.sum(kernel.astype(jnp.float32) * row_scale[:, None, :, None], axis=(0, 2))


def body(noise, latents):
    draws, features = noise.shape
    block_clips = latents.shape[0]
    total_noise = draws * X * C
    total_clips = block_clips * X * C
    rows = draws * X
    wide = Y * Z
    share = rows // wide

    other = lax.ppermute(latents, "c", SWAP)
    noise_rows = gather_by_a2a(noise, "x", X).reshape(rows, features)

    def partial_scores(block):
        scores = lax.dot_general(noise_rows, block, (((1,), (1,)), ((), ())), preferred_element_type=jnp.float32)
        return (scores * (SEND_SCALE / math.sqrt(F))).astype(jnp.float16).reshape(wide, 1, share, block_clips)

    partial = jnp.concatenate([partial_scores(latents), partial_scores(other)], axis=1)
    arrived = lax.all_to_all(partial, WIDE, 0, 0)
    block = jnp.exp(jnp.sum(arrived.astype(jnp.float32), axis=0) * (1.0 / SEND_SCALE))
    own = gather_by_a2a(block.astype(jnp.bfloat16), WIDE, wide)
    theirs = lax.ppermute(own, "c", SWAP)

    (row_total,) = sum_over_x(jnp.sum(own.astype(jnp.float32), axis=(1, 3)))
    row_scale = 1.0 / total_noise / row_total
    mass = col_part(own, row_scale)
    col_scale = 1.0 / total_clips / (mass + lax.ppermute(mass, "c", SWAP)[::-1])
    for _ in range(BALANCE_ROUNDS - 1):
        row_total, their_total = sum_over_x(row_part(own, col_scale), row_part(theirs, col_scale[::-1]))
        row_scale = 1.0 / total_noise / row_total
        mass = col_part(own, row_scale) + col_part(theirs, 1.0 / total_noise / their_total)[::-1]
        col_scale = 1.0 / total_clips / mass

    plan = own.astype(jnp.float32) * col_scale[None, :, None, :] * (row_scale * total_noise)[:, None, :, None]
    own_w, other_w = (plan[:, b].reshape(rows, block_clips).astype(jnp.bfloat16) for b in range(C))
    own_w, other_w = lax.optimization_barrier((own_w, other_w))
    last = jnp.sum(plan, axis=(1, 3)).reshape(X, 1, draws)
    high = lax.reduce_precision(last, 8, 7)
    totals = jnp.concatenate([high, last - high], axis=1).astype(jnp.bfloat16)
    totals = jnp.pad(totals, ((0, 0), (0, TILE - 2), (0, features - draws)))
    partial_target = jnp.dot(own_w, latents, preferred_element_type=jnp.float32)
    partial_target += jnp.dot(other_w, other, preferred_element_type=jnp.float32)
    send = jnp.concatenate([partial_target.astype(jnp.bfloat16).reshape(X, draws, features), totals], axis=1)
    parts = jnp.sum(lax.all_to_all(send, "x", 0, 0).astype(jnp.float32), axis=0)
    own_total = parts[draws, :draws] + parts[draws + 1, :draws]
    return (parts[:draws] / own_total[:, None] - noise.astype(jnp.float32)).astype(jnp.bfloat16)


def solution(mesh):
    mesh = Mesh(mesh.devices.reshape(Y, Z, X, C), (*WIDE, *NARROW))
    spec = P(NARROW, WIDE)
    return jax.shard_map(body, mesh=mesh, in_specs=(spec, spec), out_specs=spec, check_vma=False)
```

time: 152 us -> 166 us (1.092)
  blocking collectives: 114 us -> 104 us
  other arithmetic: 4.22 us -> 12.4 us
  local copies, waits for them, and re-layouts: 3.58 us -> 10.6 us
  starting transfers between devices: 8.24 us -> 13.4 us
  waiting for transfers between devices: 16 us -> 20.5 us
  matrix products: 5.56 us -> 3.43 us
    all_to_all x3 -> x2, blocking collectives: 23.1 us -> 15.4 us  [sum_over_x(): lax.all_to_all(jnp.broadcast_to(send, (X, *send.shape[1:])), 'x', 0, 0)]
    reduce_sum x11 -> x10, other arithmetic: 2.54 us -> 7.73 us  [the longest x5 4.18 us: col_part(): jnp.sum(kernel.astype(jnp.float32) * row_scale[:, None, :, None], axis=(0...]
    all_to_all x0 -> x1, waiting for transfers between devices: none -> 3.35 us  [sum_over_x(): lax.all_to_all(jnp.broadcast_to(send, (X, *send.shape[1:])), 'x', 0, 0)]
    all_to_all x0 -> x1, starting transfers between devices: none -> 3.25 us  [sum_over_x(): lax.all_to_all(jnp.broadcast_to(send, (X, *send.shape[1:])), 'x', 0, 0)]
    reshape x2 -> x4, local copies, waits for them, and re-layouts: 0.18 us -> 3.38 us  [sum_over_x(): send = jnp.concatenate([p.reshape(1, -1, LANES) for p in parts], axis=1)]
    psum x1 -> x0, blocking collectives: 2.47 us -> none  [body(): col_scale = 1.0 / total_clips / lax.psum(col_part(own, row_scale), 'c')]
    dot_general x2 -> x4, matrix products: 5.56 us -> 3.43 us  [the longest x2 1.72 us: partial_scores(): lax.dot_general(noise_rows, block, (((1,), (1,)), ((), ())), preferred_el...]
    ppermute x1 -> x2, starting transfers between devices: 1.91 us -> 3.84 us  [the longest x1 1.92 us: body(): theirs = lax.ppermute(own, 'c', SWAP)]
  transfers between devices with their start and end apart: 3 -> 5, of which waited for: 1 -> 3; matrix products, arithmetic and copies ran while one was open for 1% -> 3% of each run, Pallas kernels for 0% -> 0%
where the time goes in v5:
time: 166 us; the launch traced here: 165 us
  blocking collectives  104 us (63%)
  waiting for transfers between devices  20.5 us (12%)
  starting transfers between devices  13.4 us (8%)
  other arithmetic  12.4 us (7%)
  local copies, waits for them, and re-layouts  10.6 us (6%)
  matrix products  3.43 us (2%)
    all_to_all x1, blocking collectives, body(): arrived = lax.all_to_all(partial, WIDE, 0, 0)  40.1 us
    all_to_all x1, blocking collectives, gather_by_a2a(): lax.all_to_all(jnp.broadcast_to(block[None], (n, *block.shape)), axes, 0, 0)  28.8 us
    all_to_all x1, blocking collectives, body(): parts = jnp.sum(lax.all_to_all(send, 'x', 0, 0).astype(jnp.float32), axis=0)  19.5 us
    all_to_all x1, waiting for transfers between devices, gather_by_a2a(): lax.all_to_all(jnp.broadcast_to(block[None], (n, *block.shape)), axes, 0, 0)  16 us
    all_to_all x2, blocking collectives, sum_over_x(): lax.all_to_all(jnp.broadcast_to(send, (X, *send.shape[1:])), 'x', 0, 0)  15.4 us
    all_to_all x1, starting transfers between devices, gather_by_a2a(): lax.all_to_all(jnp.broadcast_to(block[None], (n, *block.shape)), axes, 0, 0)  4.42 us
    reduce_sum x5, other arithmetic, col_part(): jnp.sum(kernel.astype(jnp.float32) * row_scale[:, None, :, None], axis=(0...  4.18 us
    reshape x4, local copies, waits for them, and re-layouts, sum_over_x(): send = jnp.concatenate([p.reshape(1, -1, LANES) for p in parts], axis=1)  3.38 us
  transfers between devices with their start and end apart: 5, of which 3 were waited for; matrix products, arithmetic and copies ran while one was open for 3% of the time, Pallas kernels for 0%

profile of v5, /device:TPU:16, one launch (start us, length us, event | category | flops | bytes accessed | tf_op | source)
XLA Modules:
  0.0 164.5 jit_solution(13573775042117756125)
XLA Ops:
  0.0 2.1 %broadcast_in_dim.16 = bf16[4,128,1280]{2,1,0:T(8,128)(2,1)} broadcast(bf16[128,1280]{1,0:T(8,128)(2,1)} %param.2), dimensions={1,2} | broadcast | bytes 1638400 | tf_op jit(solution)/shard_map/broadcast_in_dim | solution.py:21
  2.1 4.4 %all-to-all-start = ((bf16[4,128,1280]{2,1,0:T(8,128)(2,1)}), bf16[4,128,1280]{2,1,0:T(8,128)(2,1)S(1)}, u32[]{:S(2)}, u32[]{:S(2)}) async-start(bf16[4,128,1280]{2,1,0:T(8,128)(2,1)} %broadcast_in_dim.16), calls=%async_computation | async-start | bytes 2621440 | tf_op jit(solution)/shard_map/all_to_all | solution.py:21
  6.5 1.9 %collective-permute-start = (bf16[384,1280]{1,0:T(8,128)(2,1)S(1)}, bf16[384,1280]{1,0:T(8,128)(2,1)S(1)}, u32[]{:S(2)}, u32[]{:S(2)}) collective-permute-start(bf16[384,1280]{1,0:T(8,128)(2,1)S(1)} %copy-done.1), channel_id=1, source_target_pairs={{0,1},{1,0},{2,3},{3,2},{4,5},{5,4},{6,7},{7,6},{8,9},{9,8},{10,11... | collective-permute-start | bytes 2949128 | tf_op jit(solution)/shard_map/ppermute | solution.py:48
  8.5 16.0 %all-to-all-done = bf16[4,128,1280]{2,1,0:T(8,128)(2,1)S(1)} async-done(((bf16[4,128,1280]{2,1,0:T(8,128)(2,1)}), bf16[4,128,1280]{2,1,0:T(8,128)(2,1)S(1)}, u32[]{:S(2)}, u32[]{:S(2)}) %all-to-all-start) | async-done | bytes 1310752 | tf_op jit(solution)/shard_map/all_to_all | solution.py:21
  24.5 0.9 fusion.18
  25.3 0.9 fusion.17
  26.2 0.2 pad_maximum_fusion
  26.4 40.1 %all_to_all.35 = f16[64,2,8,384]{3,2,1,0:T(8,128)(2,1)S(1)} all-to-all(f16[64,2,8,384]{3,2,1,0:T(8,128)(2,1)S(1)} %pad_maximum_fusion), channel_id=1, replica_groups=mesh['y'=8,'z'=8,'x'=4,'c'=2] {'y','z'}, dimensions={0} | all-to-all | bytes 1572864 | tf_op jit(solution)/shard_map/all_to_all | solution.py:56
  66.5 0.1 convert_reduce_fusion.2
  66.7 28.8 %all_to_all.36 = bf16[64,2,8,384]{3,2,1,0:T(8,128)(2,1)S(1)} all-to-all(bf16[64,2,8,384]{3,2,1,0:T(8,128)(2,1)S(1)} %broadcast_in_dim.17), channel_id=1, replica_groups=mesh['y'=8,'z'=8,'x'=4,'c'=2] {'y','z'}, dimensions={0} | all-to-all | bytes 1572864 | tf_op jit(solution)/shard_map/all_to_all | solution.py:21
  95.5 0.2 convert_reduce_fusion
  95.8 0.6 broadcast_in_dim.19
  96.4 3.2 %all-to-all-start.3 = ((f32[4,4,128]{2,1,0:T(4,128)}), f32[4,4,128]{2,1,0:T(4,128)S(1)}, u32[]{:S(2)}, u32[]{:S(2)}) async-start(f32[4,4,128]{2,1,0:T(4,128)} %broadcast_in_dim.19), calls=%async_computation.3 | async-start | bytes 16384 | tf_op jit(solution)/shard_map/all_to_all | solution.py:27
  99.7 1.9 %collective-permute-start.2 = (bf16[64,2,8,384]{3,2,1,0:T(8,128)(2,1)S(1)}, bf16[64,2,8,384]{3,2,1,0:T(8,128)(2,1)S(1)}, u32[]{:S(2)}, u32[]{:S(2)}) collective-permute-start(bf16[64,2,8,384]{3,2,1,0:T(8,128)(2,1)S(1)} %all_to_all.36), channel_id=1, source_target_pairs={{0,1},{1,0},{2,3},{3,2},{4,5},{5,4},{6,7},{7,6},{8,9},{9,8},{10,11... | collective-permute-start | bytes 2359304 | tf_op jit(solution)/shard_map/ppermute | solution.py:59
  101.6 3.4 %all-to-all-done.3 = f32[4,4,128]{2,1,0:T(4,128)S(1)} async-done(((f32[4,4,128]{2,1,0:T(4,128)}), f32[4,4,128]{2,1,0:T(4,128)S(1)}, u32[]{:S(2)}, u32[]{:S(2)}) %all-to-all-start.3) | async-done | bytes 8224 | tf_op jit(solution)/shard_map/all_to_all | solution.py:27
  105.0 0.7 div.71
  105.7 1.0 fusion.6
  106.7 1.9 %collective-permute-start.1 = (f32[2,384]{1,0:T(2,128)S(1)}, f32[2,384]{1,0:T(2,128)S(1)}, u32[]{:S(2)}, u32[]{:S(2)}) collective-permute-start(f32[2,384]{1,0:T(2,128)S(1)} %fusion.6), channel_id=1, source_target_pairs={{0,1},{1,0},{2,3},{3,2},{4,5},{5,4},{6,7},{7,6},{8,9},{9,8},{10,11... | collective-permute-start | bytes 9224 | tf_op jit(solution)/shard_map/ppermute | solution.py:64
  108.6 1.1 collective-permute-done.1
  109.8 0.1 reverse.6
  109.9 0.8 fusion.7
  110.8 0.8 reshape.132
  111.6 0.8 fusion.2
  112.5 0.8 reshape.133
  113.4 7.7 %all_to_all.37 = f32[4,8,128]{2,1,0:T(8,128)S(1)} all-to-all(f32[4,8,128]{2,1,0:T(8,128)S(1)} %broadcast_in_dim.21), channel_id=1, replica_groups=mesh['y'=8,'z'=8,'x'=4,'c'=2] {'x'}, dimensions={0} | all-to-all | bytes 32768 | tf_op jit(solution)/shard_map/all_to_all | solution.py:27
  121.1 0.6 reduce_sum.150
  121.7 0.8 slice_divide_fusion.3
  122.4 0.7 div.76
  123.1 1.0 fusion.3
  124.3 0.7 div.74
  125.0 1.0 fusion.8
  126.1 0.8 fusion.4
  126.9 0.8 reshape.135
  127.8 0.8 fusion.9
  128.6 0.8 reshape.134
  129.5 7.7 %all_to_all.38 = f32[4,8,128]{2,1,0:T(8,128)S(1)} all-to-all(f32[4,8,128]{2,1,0:T(8,128)S(1)} %broadcast_in_dim.23), channel_id=1, replica_groups=mesh['y'=8,'z'=8,'x'=4,'c'=2] {'x'}, dimensions={0} | all-to-all | bytes 32768 | tf_op jit(solution)/shard_map/all_to_all | solution.py:27
  137.2 0.6 reduce_sum.155
  137.8 0.8 slice_divide_fusion.1
  138.6 0.7 div.81
  139.3 1.0 fusion.5
  140.5 0.2 fusion.10
  140.7 0.4 fusion.13
  141.3 0.8 fusion.23
  142.2 0.9 fusion
  143.1 19.5 %all_to_all.39 = bf16[4,136,1280]{2,1,0:T(8,128)(2,1)S(1)} all-to-all(bf16[4,136,1280]{2,1,0:T(8,128)(2,1)S(1)} %fusion.14), channel_id=1, replica_groups=mesh['y'=8,'z'=8,'x'=4,'c'=2] {'x'}, dimensions={0} | all-to-all | bytes 2785280 | tf_op jit(solution)/shard_map/all_to_all | solution.py:81
  162.7 0.2 convert_reduce_fusion.1
  162.9 0.8 copy-done
  163.6 0.9 fusion.20
  (32 shorter events, 1.0 us)
Async XLA Ops:
  2.1 4.4 %copy-start.1 = (bf16[384,1280]{1,0:T(8,128)(2,1)S(1)}, bf16[384,1280]{1,0:T(8,128)(2,1)}, u32[]{:S(2)}) copy-start(bf16[384,1280]{1,0:T(8,128)(2,1)} %param.3) | copy-start | bytes 2949124
  2.1 22.3 %all-to-all-start = ((bf16[4,128,1280]{2,1,0:T(8,128)(2,1)}), bf16[4,128,1280]{2,1,0:T(8,128)(2,1)S(1)}, u32[]{:S(2)}, u32[]{:S(2)}) async-start(bf16[4,128,1280]{2,1,0:T(8,128)(2,1)} %broadcast_in_dim.16), calls=%async_computation | async-start | bytes 2621440 | tf_op jit(solution)/shard_map/all_to_all | solution.py:21
  6.5 18.8 %collective-permute-start = (bf16[384,1280]{1,0:T(8,128)(2,1)S(1)}, bf16[384,1280]{1,0:T(8,128)(2,1)S(1)}, u32[]{:S(2)}, u32[]{:S(2)}) collective-permute-start(bf16[384,1280]{1,0:T(8,128)(2,1)S(1)} %copy-done.1), channel_id=1, source_target_pairs={{0,1},{1,0},{2,3},{3,2},{4,5},{5,4},{6,7},{7,6},{8,9},{9,8},{10,11... | collective-permute-start | bytes 2949128 | tf_op jit(solution)/shard_map/ppermute | solution.py:48
  96.4 8.5 %all-to-all-start.3 = ((f32[4,4,128]{2,1,0:T(4,128)}), f32[4,4,128]{2,1,0:T(4,128)S(1)}, u32[]{:S(2)}, u32[]{:S(2)}) async-start(f32[4,4,128]{2,1,0:T(4,128)} %broadcast_in_dim.19), calls=%async_computation.3 | async-start | bytes 16384 | tf_op jit(solution)/shard_map/all_to_all | solution.py:27
  99.7 12.0 %collective-permute-start.2 = (bf16[64,2,8,384]{3,2,1,0:T(8,128)(2,1)S(1)}, bf16[64,2,8,384]{3,2,1,0:T(8,128)(2,1)S(1)}, u32[]{:S(2)}, u32[]{:S(2)}) collective-permute-start(bf16[64,2,8,384]{3,2,1,0:T(8,128)(2,1)S(1)} %all_to_all.36), channel_id=1, source_target_pairs={{0,1},{1,0},{2,3},{3,2},{4,5},{5,4},{6,7},{7,6},{8,9},{9,8},{10,11... | collective-permute-start | bytes 2359304 | tf_op jit(solution)/shard_map/ppermute | solution.py:59
  106.7 3.1 %collective-permute-start.1 = (f32[2,384]{1,0:T(2,128)S(1)}, f32[2,384]{1,0:T(2,128)S(1)}, u32[]{:S(2)}, u32[]{:S(2)}) collective-permute-start(f32[2,384]{1,0:T(2,128)S(1)} %fusion.6), channel_id=1, source_target_pairs={{0,1},{1,0},{2,3},{3,2},{4,5},{5,4},{6,7},{7,6},{8,9},{9,8},{10,11... | collective-permute-start | bytes 9224 | tf_op jit(solution)/shard_map/ppermute | solution.py:64
  162.7 1.0 copy-start

commit v6 on v5

--- a/solution.py
+++ b/solution.py
@@ -69,14 +69,14 @@
         col_scale = 1.0 / total_clips / mass
 
     plan = own.astype(jnp.float32) * col_scale[None, :, None, :] * (row_scale * total_noise)[:, None, :, None]
-    own_w, other_w = (plan[:, b].reshape(rows, block_clips).astype(jnp.bfloat16) for b in range(C))
-    own_w, other_w = lax.optimization_barrier((own_w, other_w))
+    weights = jnp.concatenate([plan[:, b].reshape(rows, block_clips) for b in range(C)], axis=1)
+    weights = lax.optimization_barrier(weights.astype(jnp.bfloat16))
     last = jnp.sum(plan, axis=(1, 3)).reshape(X, 1, draws)
     high = lax.reduce_precision(last, 8, 7)
     totals = jnp.concatenate([high, last - high], axis=1).astype(jnp.bfloat16)
     totals = jnp.pad(totals, ((0, 0), (0, TILE - 2), (0, features - draws)))
-    partial_target = jnp.dot(own_w, latents, preferred_element_type=jnp.float32)
-    partial_target += jnp.dot(other_w, other, preferred_element_type=jnp.float32)
+    chip_latents = jnp.concatenate([latents, other], axis=0)
+    partial_target = jnp.dot(weights, chip_latents, preferred_element_type=jnp.float32)
     send = jnp.concatenate([partial_target.astype(jnp.bfloat16).reshape(X, draws, features), totals], axis=1)
     parts = jnp.sum(lax.all_to_all(send, "x", 0, 0).astype(jnp.float32), axis=0)
     own_total = parts[draws, :draws] + parts[draws + 1, :draws]

time: 166 us -> 153 us (0.922)
  other arithmetic: 12.4 us -> 4.33 us
  local copies, waits for them, and re-layouts: 10.6 us -> 5.13 us
  matrix products: 3.43 us -> 5.33 us
    reshape x4, local copies, waits for them, and re-layouts: 3.38 us -> 0.36 us  [sum_over_x(): send = jnp.concatenate([p.reshape(1, -1, LANES) for p in parts], axis=1)]
    reduce_sum x5, other arithmetic: 4.18 us -> 1.16 us  [col_part(): jnp.sum(kernel.astype(jnp.float32) * row_scale[:, None, :, None], axis=(0...]
    reduce_sum x4, other arithmetic: 3.37 us -> 0.92 us  [row_part(): jnp.sum(kernel.astype(jnp.float32) * col_scale[None, :, None, :], axis=(1...]
  transfers between devices with their start and end apart: 5 -> 5, of which waited for: 3 -> 3; matrix products, arithmetic and copies ran while one was open for 3% -> 1% of each run, Pallas kernels for 0% -> 0%
where the time goes in v6:
time: 153 us
  blocking collectives  104 us (68%)
  waiting for transfers between devices  20.5 us (13%)
  starting transfers between devices  13.4 us (9%)
  matrix products  5.33 us (3%)
  local copies, waits for them, and re-layouts  5.13 us (3%)
  other arithmetic  4.33 us (3%)
    all_to_all x1, blocking collectives, body(): arrived = lax.all_to_all(partial, WIDE, 0, 0)  40.1 us
    all_to_all x1, blocking collectives, gather_by_a2a(): lax.all_to_all(jnp.broadcast_to(block[None], (n, *block.shape)), axes, 0, 0)  28.8 us
    all_to_all x1, blocking collectives, body(): parts = jnp.sum(lax.all_to_all(send, 'x', 0, 0).astype(jnp.float32), axis=0)  19.5 us
    all_to_all x1, waiting for transfers between devices, gather_by_a2a(): lax.all_to_all(jnp.broadcast_to(block[None], (n, *block.shape)), axes, 0, 0)  16 us
    all_to_all x2, blocking collectives, sum_over_x(): lax.all_to_all(jnp.broadcast_to(send, (X, *send.shape[1:])), 'x', 0, 0)  15.4 us
    all_to_all x1, starting transfers between devices, gather_by_a2a(): lax.all_to_all(jnp.broadcast_to(block[None], (n, *block.shape)), axes, 0, 0)  4.42 us
    all_to_all x1, waiting for transfers between devices, sum_over_x(): lax.all_to_all(jnp.broadcast_to(send, (X, *send.shape[1:])), 'x', 0, 0)  3.35 us
    all_to_all x1, starting transfers between devices, sum_over_x(): lax.all_to_all(jnp.broadcast_to(send, (X, *send.shape[1:])), 'x', 0, 0)  3.25 us
  transfers between devices with their start and end apart: 5, of which 3 were waited for; matrix products, arithmetic and copies ran while one was open for 1% of the time, Pallas kernels for 0%

profile of v6, /device:TPU:16, one launch (start us, length us, event | category | flops | bytes accessed | tf_op | source)
XLA Modules:
  0.0 152.8 jit_solution(6422529462712576225)
XLA Ops:
  0.0 2.1 %broadcast_in_dim.16 = bf16[4,128,1280]{2,1,0:T(8,128)(2,1)} broadcast(bf16[128,1280]{1,0:T(8,128)(2,1)} %param.2), dimensions={1,2} | broadcast | bytes 1638400 | tf_op jit(solution)/shard_map/broadcast_in_dim | solution.py:21
  2.1 4.4 %all-to-all-start = ((bf16[4,128,1280]{2,1,0:T(8,128)(2,1)}), bf16[4,128,1280]{2,1,0:T(8,128)(2,1)S(1)}, u32[]{:S(2)}, u32[]{:S(2)}) async-start(bf16[4,128,1280]{2,1,0:T(8,128)(2,1)} %broadcast_in_dim.16), calls=%async_computation | async-start | bytes 2621440 | tf_op jit(solution)/shard_map/all_to_all | solution.py:21
  6.5 1.9 %collective-permute-start = (bf16[384,1280]{1,0:T(8,128)(2,1)S(1)}, bf16[384,1280]{1,0:T(8,128)(2,1)}, u32[]{:S(2)}, u32[]{:S(2)}) collective-permute-start(bf16[384,1280]{1,0:T(8,128)(2,1)S(1)} %copy-done.1), channel_id=1, source_target_pairs={{0,1},{1,0},{2,3},{3,2},{4,5},{5,4},{6,7},{7,6},{8,9},{9,8},{10,11... | collective-permute-start | bytes 2949128 | tf_op jit(solution)/shard_map/ppermute | solution.py:48
  8.5 16.0 %all-to-all-done = bf16[4,128,1280]{2,1,0:T(8,128)(2,1)S(1)} async-done(((bf16[4,128,1280]{2,1,0:T(8,128)(2,1)}), bf16[4,128,1280]{2,1,0:T(8,128)(2,1)S(1)}, u32[]{:S(2)}, u32[]{:S(2)}) %all-to-all-start) | async-done | bytes 1310752 | tf_op jit(solution)/shard_map/all_to_all | solution.py:21
  24.5 0.9 fusion.20
  25.3 2.1 %fusion.19 = f16[64,1,8,384]{3,2,1,0:T(8,128)(2,1)S(1)} fusion(bf16[512,1280]{1,0:T(8,128)(2,1)S(1)} %bitcast.26, bf16[384,1280]{1,0:T(8,128)(2,1)} %collective-permute-done), kind=kOutput, calls=%fused_computation.36 | convolution fusion | flops 503709696 | bytes 2686976 | tf_op jit(solution)/shard_map/dot_general | solution.py:52
  27.4 0.2 pad_maximum_fusion
  27.6 40.1 %all_to_all.35 = f16[64,2,8,384]{3,2,1,0:T(8,128)(2,1)S(1)} all-to-all(f16[64,2,8,384]{3,2,1,0:T(8,128)(2,1)S(1)} %pad_maximum_fusion), channel_id=1, replica_groups=mesh['y'=8,'z'=8,'x'=4,'c'=2] {'y','z'}, dimensions={0} | all-to-all | bytes 1572864 | tf_op jit(solution)/shard_map/all_to_all | solution.py:56
  67.7 0.1 convert_reduce_fusion.2
  67.9 28.8 %all_to_all.36 = bf16[64,2,8,384]{3,2,1,0:T(8,128)(2,1)S(1)} all-to-all(bf16[64,2,8,384]{3,2,1,0:T(8,128)(2,1)S(1)} %broadcast_in_dim.17), channel_id=1, replica_groups=mesh['y'=8,'z'=8,'x'=4,'c'=2] {'y','z'}, dimensions={0} | all-to-all | bytes 1572864 | tf_op jit(solution)/shard_map/all_to_all | solution.py:21
  96.7 0.2 convert_reduce_fusion
  96.9 0.1 broadcast_in_dim.18
  97.0 0.6 broadcast_in_dim.19
  97.6 3.2 %all-to-all-start.3 = ((f32[4,4,128]{2,1,0:T(4,128)}), f32[4,4,128]{2,1,0:T(4,128)S(1)}, u32[]{:S(2)}, u32[]{:S(2)}) async-start(f32[4,4,128]{2,1,0:T(4,128)} %broadcast_in_dim.19), calls=%async_computation.3 | async-start | bytes 16384 | tf_op jit(solution)/shard_map/all_to_all | solution.py:27
  100.9 1.9 %collective-permute-start.2 = (bf16[64,2,8,384]{3,2,1,0:T(8,128)(2,1)S(1)}, bf16[64,2,8,384]{3,2,1,0:T(8,128)(2,1)S(1)}, u32[]{:S(2)}, u32[]{:S(2)}) collective-permute-start(bf16[64,2,8,384]{3,2,1,0:T(8,128)(2,1)S(1)} %all_to_all.36), channel_id=1, source_target_pairs={{0,1},{1,0},{2,3},{3,2},{4,5},{5,4},{6,7},{7,6},{8,9},{9,8},{10,11... | collective-permute-start | bytes 2359304 | tf_op jit(solution)/shard_map/ppermute | solution.py:59
  102.8 3.4 %all-to-all-done.3 = f32[4,4,128]{2,1,0:T(4,128)S(1)} async-done(((f32[4,4,128]{2,1,0:T(4,128)}), f32[4,4,128]{2,1,0:T(4,128)S(1)}, u32[]{:S(2)}, u32[]{:S(2)}) %all-to-all-start.3) | async-done | bytes 8224 | tf_op jit(solution)/shard_map/all_to_all | solution.py:27
  106.2 0.1 div.71
  106.3 0.2 fusion.8
  106.5 1.9 %collective-permute-start.1 = (f32[2,384]{1,0:T(2,128)S(1)}, f32[2,384]{1,0:T(2,128)S(1)}, u32[]{:S(2)}, u32[]{:S(2)}) collective-permute-start(f32[2,384]{1,0:T(2,128)S(1)} %fusion.8), channel_id=1, source_target_pairs={{0,1},{1,0},{2,3},{3,2},{4,5},{5,4},{6,7},{7,6},{8,9},{9,8},{10,11... | collective-permute-start | bytes 9224 | tf_op jit(solution)/shard_map/ppermute | solution.py:64
  108.4 1.1 collective-permute-done.1
  109.7 0.1 reverse.6
  109.8 0.2 fusion.9
  110.0 0.1 reshape.130
  110.1 0.2 fusion.4
  110.3 0.1 reshape.131
  110.5 7.7 %all_to_all.37 = f32[4,8,128]{2,1,0:T(8,128)S(1)} all-to-all(f32[4,8,128]{2,1,0:T(8,128)S(1)} %broadcast_in_dim.21), channel_id=1, replica_groups=mesh['y'=8,'z'=8,'x'=4,'c'=2] {'x'}, dimensions={0} | all-to-all | bytes 32768 | tf_op jit(solution)/shard_map/all_to_all | solution.py:27
  118.2 0.1 div.74
  118.4 0.2 fusion.5
  118.6 0.1 rev.17
  118.7 0.2 fusion.10
  119.0 0.1 reverse.7
  119.1 0.2 fusion.6
  119.3 0.1 reshape.133
  119.4 0.2 fusion.11
  119.7 0.1 reshape.132
  119.8 7.7 %all_to_all.38 = f32[4,8,128]{2,1,0:T(8,128)S(1)} all-to-all(f32[4,8,128]{2,1,0:T(8,128)S(1)} %broadcast_in_dim.23), channel_id=1, replica_groups=mesh['y'=8,'z'=8,'x'=4,'c'=2] {'x'}, dimensions={0} | all-to-all | bytes 32768 | tf_op jit(solution)/shard_map/all_to_all | solution.py:27
  127.5 0.1 div.79
  127.7 0.2 fusion.7
  127.9 0.1 rev.19
  128.1 0.2 fusion.12
  128.3 0.4 fusion.15
  128.7 0.1 reshape.135
  128.9 2.4 %convolution_convert_fusion = bf16[512,1280]{1,0:T(8,128)(2,1)S(1)} fusion(bf16[512,768]{1,0:T(8,128)(2,1)S(1)} %pad_maximum_fusion.1, bf16[384,1280]{1,0:T(8,128)(2,1)} %collective-permute-done, bf16[384,1280]{1,0:T(8,128)(2,1)S(1)} %copy-done.1), kind=kOutput, calls=%fused_computation.7 | convolution fusion | flops 1011220480 | bytes 4063232 | tf_op jit(solution)/shard_map/dot_general | solution.py:79
  131.4 0.1 fusion.16
  131.5 19.5 %all_to_all.39 = bf16[4,136,1280]{2,1,0:T(8,128)(2,1)S(1)} all-to-all(bf16[4,136,1280]{2,1,0:T(8,128)(2,1)S(1)} %fusion.16), channel_id=1, replica_groups=mesh['y'=8,'z'=8,'x'=4,'c'=2] {'x'}, dimensions={0} | all-to-all | bytes 2785280 | tf_op jit(solution)/shard_map/all_to_all | solution.py:81
  151.0 0.2 convert_reduce_fusion.1
  151.2 0.8 copy-done
  151.9 0.9 fusion.22
  (32 shorter events, 0.6 us)
Async XLA Ops:
  2.1 4.4 %copy-start.1 = (bf16[384,1280]{1,0:T(8,128)(2,1)S(1)}, bf16[384,1280]{1,0:T(8,128)(2,1)}, u32[]{:S(2)}) copy-start(bf16[384,1280]{1,0:T(8,128)(2,1)} %param.3) | copy-start | bytes 2949124
  2.1 22.3 %all-to-all-start = ((bf16[4,128,1280]{2,1,0:T(8,128)(2,1)}), bf16[4,128,1280]{2,1,0:T(8,128)(2,1)S(1)}, u32[]{:S(2)}, u32[]{:S(2)}) async-start(bf16[4,128,1280]{2,1,0:T(8,128)(2,1)} %broadcast_in_dim.16), calls=%async_computation | async-start | bytes 2621440 | tf_op jit(solution)/shard_map/all_to_all | solution.py:21
  6.5 18.8 %collective-permute-start = (bf16[384,1280]{1,0:T(8,128)(2,1)S(1)}, bf16[384,1280]{1,0:T(8,128)(2,1)}, u32[]{:S(2)}, u32[]{:S(2)}) collective-permute-start(bf16[384,1280]{1,0:T(8,128)(2,1)S(1)} %copy-done.1), channel_id=1, source_target_pairs={{0,1},{1,0},{2,3},{3,2},{4,5},{5,4},{6,7},{7,6},{8,9},{9,8},{10,11... | collective-permute-start | bytes 2949128 | tf_op jit(solution)/shard_map/ppermute | solution.py:48
  97.6 8.5 %all-to-all-start.3 = ((f32[4,4,128]{2,1,0:T(4,128)}), f32[4,4,128]{2,1,0:T(4,128)S(1)}, u32[]{:S(2)}, u32[]{:S(2)}) async-start(f32[4,4,128]{2,1,0:T(4,128)} %broadcast_in_dim.19), calls=%async_computation.3 | async-start | bytes 16384 | tf_op jit(solution)/shard_map/all_to_all | solution.py:27
  100.9 9.2 %collective-permute-start.2 = (bf16[64,2,8,384]{3,2,1,0:T(8,128)(2,1)S(1)}, bf16[64,2,8,384]{3,2,1,0:T(8,128)(2,1)S(1)}, u32[]{:S(2)}, u32[]{:S(2)}) collective-permute-start(bf16[64,2,8,384]{3,2,1,0:T(8,128)(2,1)S(1)} %all_to_all.36), channel_id=1, source_target_pairs={{0,1},{1,0},{2,3},{3,2},{4,5},{5,4},{6,7},{7,6},{8,9},{9,8},{10,11... | collective-permute-start | bytes 2359304 | tf_op jit(solution)/shard_map/ppermute | solution.py:59
  106.5 3.1 %collective-permute-start.1 = (f32[2,384]{1,0:T(2,128)S(1)}, f32[2,384]{1,0:T(2,128)S(1)}, u32[]{:S(2)}, u32[]{:S(2)}) collective-permute-start(f32[2,384]{1,0:T(2,128)S(1)} %fusion.8), channel_id=1, source_target_pairs={{0,1},{1,0},{2,3},{3,2},{4,5},{5,4},{6,7},{7,6},{8,9},{9,8},{10,11... | collective-permute-start | bytes 9224 | tf_op jit(solution)/shard_map/ppermute | solution.py:64
  151.0 1.0 copy-start

commit v7 on v4

v7 whole, which is shorter than its diff:
```python
import math

import jax
import jax.numpy as jnp
from jax import lax
from jax.sharding import Mesh
from jax.sharding import PartitionSpec as P

F = 81920
BALANCE_ROUNDS = 3
Y, Z, X, C = 8, 8, 4, 2
WIDE = ("y", "z")
NARROW = ("x", "c")
SWAP = [(0, 1), (1, 0)]
SEND_SCALE = 64.0
LANES = 128
TILE = 8


def gather_by_a2a(block, axes, n):
    return lax.all_to_all(jnp.broadcast_to(block[None], (n, *block.shape)), axes, 0, 0).reshape(
        n * block.shape[0], block.shape[1]
    )


def sum_over_x(*parts):
    sizes = [p.shape[0] // LANES for p in parts]
    send = jnp.concatenate([p.reshape(1, -1, LANES) for p in parts], axis=1)
    got = lax.all_to_all(jnp.broadcast_to(send, (X, *send.shape[1:])), "x", 0, 0)
    total = (got[0] + got[1]) + (got[2] + got[3])
    out, at = [], 0
    for size in sizes:
        out.append(total[at : at + size].reshape(size * LANES))
        at += size
    return out


def body(noise, latents):
    draws, features = noise.shape
    total_noise = draws * X * C
    total_clips = latents.shape[0] * X * C
    rows = draws * X
    clips = latents.shape[0] * C

    other = lax.ppermute(latents, "c", SWAP)
    noise_rows = gather_by_a2a(noise, "x", X)

    def partial_scores(block):
        scores = lax.dot_general(noise_rows, block, (((1,), (1,)), ((), ())), preferred_element_type=jnp.float32)
        return (scores * (SEND_SCALE / math.sqrt(F))).astype(jnp.float16).reshape(Y * Z, 1, rows // (Y * Z), -1)

    partial = jnp.concatenate([partial_scores(latents), partial_scores(other)], axis=1)
    arrived = lax.all_to_all(partial, WIDE, 0, 0)
    scores = jnp.sum(arrived.astype(jnp.float32), axis=0) * (1.0 / SEND_SCALE)
    block = jnp.concatenate([scores[0], scores[1]], axis=1)
    own = lax.optimization_barrier(gather_by_a2a(jnp.exp(block).astype(jnp.bfloat16), WIDE, Y * Z))
    theirs = lax.ppermute(own, "c", SWAP)

    def flip(vector):
        return jnp.roll(vector, clips // 2)

    def row_part(kernel, col_scale):
        return jnp.sum(kernel.astype(jnp.float32) * col_scale[None, :], axis=1)

    def col_part(kernel, row_scale):
        return jnp.sum(kernel.astype(jnp.float32) * row_scale[:, None], axis=0)

    (row_total,) = sum_over_x(jnp.sum(own.astype(jnp.float32), axis=1))
    row_scale = 1.0 / total_noise / row_total
    mass = col_part(own, row_scale)
    col_scale = 1.0 / total_clips / (mass + flip(lax.ppermute(mass, "c", SWAP)))
    for _ in range(BALANCE_ROUNDS - 1):
        row_total, their_total = sum_over_x(row_part(own, col_scale), row_part(theirs, flip(col_scale)))
        row_scale = 1.0 / total_noise / row_total
        mass = col_part(own, row_scale) + flip(col_part(theirs, 1.0 / total_noise / their_total))
        col_scale = 1.0 / total_clips / mass

    plan = own.astype(jnp.float32) * col_scale[None, :] * (row_scale * total_noise)[:, None]
    weights = lax.optimization_barrier(plan.astype(jnp.bfloat16))
    last = jnp.sum(plan, axis=1).reshape(X, 1, draws)
    high = lax.reduce_precision(last, 8, 7)
    totals = jnp.concatenate([high, last - high], axis=1).astype(jnp.bfloat16)
    totals = jnp.pad(totals, ((0, 0), (0, TILE - 2), (0, features - draws)))
    partial_target = jnp.dot(weights[:, : clips // 2], latents, preferred_element_type=jnp.float32)
    partial_target += jnp.dot(weights[:, clips // 2 :], other, preferred_element_type=jnp.float32)
    send = jnp.concatenate([partial_target.astype(jnp.bfloat16).reshape(X, draws, features), totals], axis=1)
    parts = jnp.sum(lax.all_to_all(send, "x", 0, 0).astype(jnp.float32), axis=0)
    own_total = parts[draws, :draws] + parts[draws + 1, :draws]
    return (parts[:draws] / own_total[:, None] - noise.astype(jnp.float32)).astype(jnp.bfloat16)


def solution(mesh):
    mesh = Mesh(mesh.devices.reshape(Y, Z, X, C), (*WIDE, *NARROW))
    spec = P(NARROW, WIDE)
    return jax.shard_map(body, mesh=mesh, in_specs=(spec, spec), out_specs=spec, check_vma=False)
```

time: 152 us -> 151 us (level)
  starting transfers between devices: 8.24 us -> 10.7 us
  matrix products: 5.56 us -> 3.41 us
  blocking collectives: 114 us -> 112 us
  waiting for transfers between devices: 16 us -> 17.6 us
    psum x1 -> x0, blocking collectives: 2.47 us -> none  [body(): col_scale = 1.0 / total_clips / lax.psum(col_part(own, row_scale), 'c')]
    ppermute x1 -> x2, starting transfers between devices: 1.91 us -> 4.33 us  [the longest x1 2.41 us: body(): theirs = lax.ppermute(own, 'c', SWAP)]
    dot_general x2 -> x4, matrix products: 5.56 us -> 3.41 us  [the longest x2 1.72 us: partial_scores(): lax.dot_general(noise_rows, block, (((1,), (1,)), ((), ())), preferred_el...]
    ppermute x1 -> x2, waiting for transfers between devices: 0.01 us -> 1.6 us  [the longest x1 1.59 us: body(): theirs = lax.ppermute(own, 'c', SWAP)]
  transfers between devices with their start and end apart: 3 -> 4, of which waited for: 1 -> 2; matrix products, arithmetic and copies ran while one was open for 1% -> 1% of each run, Pallas kernels for 0% -> 0%
where the time goes in v7:
time: 151 us
  blocking collectives  112 us (74%)
  waiting for transfers between devices  17.6 us (12%)
  starting transfers between devices  10.7 us (7%)
  other arithmetic  4.16 us (3%)
  matrix products  3.41 us (2%)
  local copies, waits for them, and re-layouts  2.98 us (2%)
    all_to_all x1, blocking collectives, body(): arrived = lax.all_to_all(partial, WIDE, 0, 0)  40.1 us
    all_to_all x1, blocking collectives, gather_by_a2a(): lax.all_to_all(jnp.broadcast_to(block[None], (n, *block.shape)), axes, 0, 0)  28.8 us
    all_to_all x3, blocking collectives, sum_over_x(): lax.all_to_all(jnp.broadcast_to(send, (X, *send.shape[1:])), 'x', 0, 0)  23.1 us
    all_to_all x1, blocking collectives, body(): parts = jnp.sum(lax.all_to_all(send, 'x', 0, 0).astype(jnp.float32), axis=0)  19.7 us
    all_to_all x1, waiting for transfers between devices, gather_by_a2a(): lax.all_to_all(jnp.broadcast_to(block[None], (n, *block.shape)), axes, 0, 0)  16 us
    all_to_all x1, starting transfers between devices, gather_by_a2a(): lax.all_to_all(jnp.broadcast_to(block[None], (n, *block.shape)), axes, 0, 0)  4.42 us
  transfers between devices with their start and end apart: 4, of which 2 were waited for; matrix products, arithmetic and copies ran while one was open for 1% of the time, Pallas kernels for 0%

profile of v7, /device:TPU:16, one launch (start us, length us, event | category | flops | bytes accessed | tf_op | source)
XLA Modules:
  0.0 150.8 jit_solution(18129622061651983625)
XLA Ops:
  0.0 2.1 %broadcast_in_dim.16 = bf16[4,128,1280]{2,1,0:T(8,128)(2,1)} broadcast(bf16[128,1280]{1,0:T(8,128)(2,1)} %param.2), dimensions={1,2} | broadcast | bytes 1638400 | tf_op jit(solution)/shard_map/broadcast_in_dim | solution.py:21
  2.1 0.0 copy-start.1
  2.1 4.4 %all-to-all-start = ((bf16[4,128,1280]{2,1,0:T(8,128)(2,1)}), bf16[4,128,1280]{2,1,0:T(8,128)(2,1)S(1)}, u32[]{:S(2)}, u32[]{:S(2)}) async-start(bf16[4,128,1280]{2,1,0:T(8,128)(2,1)} %broadcast_in_dim.16), calls=%async_computation | async-start | bytes 2621440 | tf_op jit(solution)/shard_map/all_to_all | solution.py:21
  6.5 0.0 copy-done.1
  6.5 1.9 %collective-permute-start = (bf16[384,1280]{1,0:T(8,128)(2,1)S(1)}, bf16[384,1280]{1,0:T(8,128)(2,1)S(1)}, u32[]{:S(2)}, u32[]{:S(2)}) collective-permute-start(bf16[384,1280]{1,0:T(8,128)(2,1)S(1)} %copy-done.1), channel_id=1, source_target_pairs={{0,1},{1,0},{2,3},{3,2},{4,5},{5,4},{6,7},{7,6},{8,9},{9,8},{10,11... | collective-permute-start | bytes 2949128 | tf_op jit(solution)/shard_map/ppermute | solution.py:45
  8.5 16.0 %all-to-all-done = bf16[4,128,1280]{2,1,0:T(8,128)(2,1)S(1)} async-done(((bf16[4,128,1280]{2,1,0:T(8,128)(2,1)}), bf16[4,128,1280]{2,1,0:T(8,128)(2,1)S(1)}, u32[]{:S(2)}, u32[]{:S(2)}) %all-to-all-start) | async-done | bytes 1310752 | tf_op jit(solution)/shard_map/all_to_all | solution.py:21
  24.5 0.9 fusion.16
  25.3 0.0 collective-permute-done
  25.3 0.9 fusion.15
  26.2 0.2 pad_maximum_fusion.1
  26.4 40.1 %all_to_all.35 = f16[64,2,8,384]{3,2,1,0:T(8,128)(2,1)S(1)} all-to-all(f16[64,2,8,384]{3,2,1,0:T(8,128)(2,1)S(1)} %pad_maximum_fusion.1), channel_id=1, replica_groups=mesh['y'=8,'z'=8,'x'=4,'c'=2] {'y','z'}, dimensions={0} | all-to-all | bytes 1572864 | tf_op jit(solution)/shard_map/all_to_all | solution.py:53
  66.5 0.1 convert_reduce_fusion.2
  66.6 0.1 broadcast_in_dim.17
  66.7 28.8 %all_to_all.36 = bf16[64,8,768]{2,1,0:T(8,128)(2,1)S(1)} all-to-all(bf16[64,8,768]{2,1,0:T(8,128)(2,1)S(1)} %broadcast_in_dim.17), channel_id=1, replica_groups=mesh['y'=8,'z'=8,'x'=4,'c'=2] {'y','z'}, dimensions={0} | all-to-all | bytes 1572864 | tf_op jit(solution)/shard_map/all_to_all | solution.py:21
  95.5 0.2 convert_reduce_fusion
  95.7 7.7 %all_to_all.37 = f32[4,4,128]{2,1,0:T(4,128)S(1)} all-to-all(f32[4,4,128]{2,1,0:T(4,128)S(1)} %broadcast_in_dim.19), channel_id=1, replica_groups=mesh['y'=8,'z'=8,'x'=4,'c'=2] {'x'}, dimensions={0} | all-to-all | bytes 16384 | tf_op jit(solution)/shard_map/all_to_all | solution.py:29
  103.4 0.2 fusion.5
  103.6 1.9 %collective-permute-start.1 = (f32[768]{0:T(1024)S(1)}, f32[768]{0:T(1024)S(1)}, u32[]{:S(2)}, u32[]{:S(2)}) collective-permute-start(f32[768]{0:T(1024)S(1)} %fusion.5), channel_id=1, source_target_pairs={{0,1},{1,0},{2,3},{3,2},{4,5},{5,4},{6,7},{7,6},{8,9},{9,8},{10,11... | collective-permute-start | bytes 9224 | tf_op jit(solution)/shard_map/ppermute | solution.py:71
  105.5 2.4 %collective-permute-start.2 = (bf16[512,768]{1,0:T(8,128)(2,1)S(1)}, bf16[512,768]{1,0:T(8,128)(2,1)S(1)}, u32[]{:S(2)}, u32[]{:S(2)}) collective-permute-start(bf16[512,768]{1,0:T(8,128)(2,1)S(1)} %bitcast.46), channel_id=1, source_target_pairs={{0,1},{1,0},{2,3},{3,2},{4,5},{5,4},{6,7},{7,6},{8,9},{9,8},{10,11... | collective-permute-start | bytes 2359304 | tf_op jit(solution)/shard_map/ppermute | solution.py:57
  108.0 0.0 collective-permute-done.1
  108.0 0.2 fusion.6
  108.3 1.6 %collective-permute-done.2 = bf16[512,768]{1,0:T(8,128)(2,1)S(1)} collective-permute-done((bf16[512,768]{1,0:T(8,128)(2,1)S(1)}, bf16[512,768]{1,0:T(8,128)(2,1)S(1)}, u32[]{:S(2)}, u32[]{:S(2)}) %collective-permute-start.2) | collective-permute-done | bytes 786464 | tf_op jit(solution)/shard_map/ppermute | solution.py:57
  109.9 0.2 fusion.1
  110.1 7.7 %all_to_all.38 = f32[4,8,128]{2,1,0:T(8,128)S(1)} all-to-all(f32[4,8,128]{2,1,0:T(8,128)S(1)} %broadcast_in_dim.21), channel_id=1, replica_groups=mesh['y'=8,'z'=8,'x'=4,'c'=2] {'x'}, dimensions={0} | all-to-all | bytes 32768 | tf_op jit(solution)/shard_map/all_to_all | solution.py:29
  117.8 0.4 fusion.2
  118.3 0.2 fusion.8
  118.5 0.2 fusion.3
  118.8 7.7 %all_to_all.39 = f32[4,8,128]{2,1,0:T(8,128)S(1)} all-to-all(f32[4,8,128]{2,1,0:T(8,128)S(1)} %broadcast_in_dim.23), channel_id=1, replica_groups=mesh['y'=8,'z'=8,'x'=4,'c'=2] {'x'}, dimensions={0} | all-to-all | bytes 32768 | tf_op jit(solution)/shard_map/all_to_all | solution.py:29
  126.5 0.2 fusion.4
  126.8 0.2 fusion.9
  127.0 0.3 fusion.12
  127.4 0.8 fusion.20
  128.2 0.8 fusion
  129.1 0.1 pad_maximum_fusion
  129.2 19.7 %all_to_all.40 = bf16[4,136,1280]{2,1,0:T(8,128)(2,1)S(1)} all-to-all(bf16[4,136,1280]{2,1,0:T(8,128)(2,1)S(1)} %pad_maximum_fusion), channel_id=1, replica_groups=mesh['y'=8,'z'=8,'x'=4,'c'=2] {'x'}, dimensions={0} | all-to-all | bytes 2785280 | tf_op jit(solution)/shard_map/all_to_all | solution.py:87
  148.9 0.0 copy-start
  148.9 0.2 convert_reduce_fusion.1
  149.1 0.8 copy-done
  149.9 0.9 fusion.18
  (27 shorter events, 0.2 us)
Async XLA Ops:
  2.1 4.4 %copy-start.1 = (bf16[384,1280]{1,0:T(8,128)(2,1)S(1)}, bf16[384,1280]{1,0:T(8,128)(2,1)}, u32[]{:S(2)}) copy-start(bf16[384,1280]{1,0:T(8,128)(2,1)} %param.3) | copy-start | bytes 2949124
  2.1 22.3 %all-to-all-start = ((bf16[4,128,1280]{2,1,0:T(8,128)(2,1)}), bf16[4,128,1280]{2,1,0:T(8,128)(2,1)S(1)}, u32[]{:S(2)}, u32[]{:S(2)}) async-start(bf16[4,128,1280]{2,1,0:T(8,128)(2,1)} %broadcast_in_dim.16), calls=%async_computation | async-start | bytes 2621440 | tf_op jit(solution)/shard_map/all_to_all | solution.py:21
  6.5 18.8 %collective-permute-start = (bf16[384,1280]{1,0:T(8,128)(2,1)S(1)}, bf16[384,1280]{1,0:T(8,128)(2,1)S(1)}, u32[]{:S(2)}, u32[]{:S(2)}) collective-permute-start(bf16[384,1280]{1,0:T(8,128)(2,1)S(1)} %copy-done.1), channel_id=1, source_target_pairs={{0,1},{1,0},{2,3},{3,2},{4,5},{5,4},{6,7},{7,6},{8,9},{9,8},{10,11... | collective-permute-start | bytes 2949128 | tf_op jit(solution)/shard_map/ppermute | solution.py:45
  103.6 4.3 %collective-permute-start.1 = (f32[768]{0:T(1024)S(1)}, f32[768]{0:T(1024)S(1)}, u32[]{:S(2)}, u32[]{:S(2)}) collective-permute-start(f32[768]{0:T(1024)S(1)} %fusion.5), channel_id=1, source_target_pairs={{0,1},{1,0},{2,3},{3,2},{4,5},{5,4},{6,7},{7,6},{8,9},{9,8},{10,11... | collective-permute-start | bytes 9224 | tf_op jit(solution)/shard_map/ppermute | solution.py:71
  105.5 4.3 %collective-permute-start.2 = (bf16[512,768]{1,0:T(8,128)(2,1)S(1)}, bf16[512,768]{1,0:T(8,128)(2,1)S(1)}, u32[]{:S(2)}, u32[]{:S(2)}) collective-permute-start(bf16[512,768]{1,0:T(8,128)(2,1)S(1)} %bitcast.46), channel_id=1, source_target_pairs={{0,1},{1,0},{2,3},{3,2},{4,5},{5,4},{6,7},{7,6},{8,9},{9,8},{10,11... | collective-permute-start | bytes 2359304 | tf_op jit(solution)/shard_map/ppermute | solution.py:57
  148.9 1.0 copy-start

commit v8 on v7

--- a/solution.py
+++ b/solution.py
@@ -54,7 +54,7 @@
     scores = jnp.sum(arrived.astype(jnp.float32), axis=0) * (1.0 / SEND_SCALE)
     block = jnp.concatenate([scores[0], scores[1]], axis=1)
     own = lax.optimization_barrier(gather_by_a2a(jnp.exp(block).astype(jnp.bfloat16), WIDE, Y * Z))
-    theirs = lax.ppermute(own, "c", SWAP)
+    theirs, minus_noise = lax.optimization_barrier((lax.ppermute(own, "c", SWAP), -noise))
 
     def flip(vector):
         return jnp.roll(vector, clips // 2)
@@ -65,11 +65,8 @@
     def col_part(kernel, row_scale):
         return jnp.sum(kernel.astype(jnp.float32) * row_scale[:, None], axis=0)
 
-    (row_total,) = sum_over_x(jnp.sum(own.astype(jnp.float32), axis=1))
-    row_scale = 1.0 / total_noise / row_total
-    mass = col_part(own, row_scale)
-    col_scale = 1.0 / total_clips / (mass + flip(lax.ppermute(mass, "c", SWAP)))
-    for _ in range(BALANCE_ROUNDS - 1):
+    col_scale = jnp.ones((clips,), jnp.float32)
+    for _ in range(BALANCE_ROUNDS):
         row_total, their_total = sum_over_x(row_part(own, col_scale), row_part(theirs, flip(col_scale)))
         row_scale = 1.0 / total_noise / row_total
         mass = col_part(own, row_scale) + flip(col_part(theirs, 1.0 / total_noise / their_total))
@@ -86,7 +83,7 @@
     send = jnp.concatenate([partial_target.astype(jnp.bfloat16).reshape(X, draws, features), totals], axis=1)
     parts = jnp.sum(lax.all_to_all(send, "x", 0, 0).astype(jnp.float32), axis=0)
     own_total = parts[draws, :draws] + parts[draws + 1, :draws]
-    return (parts[:draws] / own_total[:, None] - noise.astype(jnp.float32)).astype(jnp.bfloat16)
+    return (parts[:draws] / own_total[:, None] + minus_noise.astype(jnp.float32)).astype(jnp.bfloat16)
 
 
 def solution(mesh):

time: 151 us -> 148 us (0.980)
  starting transfers between devices: 10.7 us -> 8.24 us
  blocking collectives: 112 us -> 110 us
    ppermute x2 -> x1, starting transfers between devices: 4.33 us -> 1.91 us  [body(): lax.ppermute(own, 'c', SWAP)]
  transfers between devices with their start and end apart: 4 -> 3, of which waited for: 2 -> 2; matrix products, arithmetic and copies ran while one was open for 1% -> 1% of each run, Pallas kernels for 0% -> 0%
where the time goes in v8:
time: 148 us; the launch traced here: 147 us
  blocking collectives  110 us (74%)
  waiting for transfers between devices  18 us (12%)
  starting transfers between devices  8.24 us (6%)
  other arithmetic  4.7 us (3%)
  matrix products  3.41 us (2%)
  local copies, waits for them, and re-layouts  2.22 us (2%)
    all_to_all x1, blocking collectives, body(): arrived = lax.all_to_all(partial, WIDE, 0, 0)  40.1 us
    all_to_all x1, blocking collectives, gather_by_a2a(): lax.all_to_all(jnp.broadcast_to(block[None], (n, *block.shape)), axes, 0, 0)  28.8 us
    all_to_all x3, blocking collectives, sum_over_x(): lax.all_to_all(jnp.broadcast_to(send, (X, *send.shape[1:])), 'x', 0, 0)  23.1 us
    all_to_all x1, blocking collectives, body(): parts = jnp.sum(lax.all_to_all(send, 'x', 0, 0).astype(jnp.float32), axis=0)  18.3 us
    all_to_all x1, waiting for transfers between devices, gather_by_a2a(): lax.all_to_all(jnp.broadcast_to(block[None], (n, *block.shape)), axes, 0, 0)  16 us
    all_to_all x1, starting transfers between devices, gather_by_a2a(): lax.all_to_all(jnp.broadcast_to(block[None], (n, *block.shape)), axes, 0, 0)  4.42 us
  transfers between devices with their start and end apart: 3, of which 2 were waited for; matrix products, arithmetic and copies ran while one was open for 1% of the time, Pallas kernels for 0%

profile of v8, /device:TPU:16, one launch (start us, length us, event | category | flops | bytes accessed | tf_op | source)
XLA Modules:
  0.0 147.2 jit_solution(13567865549706370469)
XLA Ops:
  0.0 2.1 %broadcast_in_dim.16 = bf16[4,128,1280]{2,1,0:T(8,128)(2,1)} broadcast(bf16[128,1280]{1,0:T(8,128)(2,1)} %param.2), dimensions={1,2} | broadcast | bytes 1638400 | tf_op jit(solution)/shard_map/broadcast_in_dim | solution.py:21
  2.1 0.0 copy-start.1
  2.1 4.4 %all-to-all-start = ((bf16[4,128,1280]{2,1,0:T(8,128)(2,1)}), bf16[4,128,1280]{2,1,0:T(8,128)(2,1)S(1)}, u32[]{:S(2)}, u32[]{:S(2)}) async-start(bf16[4,128,1280]{2,1,0:T(8,128)(2,1)} %broadcast_in_dim.16), calls=%async_computation | async-start | bytes 2621440 | tf_op jit(solution)/shard_map/all_to_all | solution.py:21
  6.5 0.0 copy-done.1
  6.5 1.9 %collective-permute-start = (bf16[384,1280]{1,0:T(8,128)(2,1)S(1)}, bf16[384,1280]{1,0:T(8,128)(2,1)S(1)}, u32[]{:S(2)}, u32[]{:S(2)}) collective-permute-start(bf16[384,1280]{1,0:T(8,128)(2,1)S(1)} %copy-done.1), channel_id=1, source_target_pairs={{0,1},{1,0},{2,3},{3,2},{4,5},{5,4},{6,7},{7,6},{8,9},{9,8},{10,11... | collective-permute-start | bytes 2949128 | tf_op jit(solution)/shard_map/ppermute | solution.py:45
  8.5 16.0 %all-to-all-done = bf16[4,128,1280]{2,1,0:T(8,128)(2,1)S(1)} async-done(((bf16[4,128,1280]{2,1,0:T(8,128)(2,1)}), bf16[4,128,1280]{2,1,0:T(8,128)(2,1)S(1)}, u32[]{:S(2)}, u32[]{:S(2)}) %all-to-all-start) | async-done | bytes 1310752 | tf_op jit(solution)/shard_map/all_to_all | solution.py:21
  24.5 0.9 fusion.18
  25.3 0.0 collective-permute-done
  25.3 0.9 fusion.17
  26.2 0.2 pad_maximum_fusion.1
  26.4 40.1 %all_to_all.35 = f16[64,2,8,384]{3,2,1,0:T(8,128)(2,1)S(1)} all-to-all(f16[64,2,8,384]{3,2,1,0:T(8,128)(2,1)S(1)} %pad_maximum_fusion.1), channel_id=1, replica_groups=mesh['y'=8,'z'=8,'x'=4,'c'=2] {'y','z'}, dimensions={0} | all-to-all | bytes 1572864 | tf_op jit(solution)/shard_map/all_to_all | solution.py:53
  66.5 0.0 copy-start
  66.5 0.1 convert_reduce_fusion.2
  66.6 0.1 broadcast_in_dim.17
  66.7 28.8 %all_to_all.36 = bf16[64,8,768]{2,1,0:T(8,128)(2,1)S(1)} all-to-all(bf16[64,8,768]{2,1,0:T(8,128)(2,1)S(1)} %broadcast_in_dim.17), channel_id=1, replica_groups=mesh['y'=8,'z'=8,'x'=4,'c'=2] {'y','z'}, dimensions={0} | all-to-all | bytes 1572864 | tf_op jit(solution)/shard_map/all_to_all | solution.py:21
  95.5 1.9 %collective-permute-start.1 = (bf16[512,768]{1,0:T(8,128)(2,1)S(1)}, bf16[512,768]{1,0:T(8,128)(2,1)S(1)}, u32[]{:S(2)}, u32[]{:S(2)}) collective-permute-start(bf16[512,768]{1,0:T(8,128)(2,1)S(1)} %bitcast.49), channel_id=1, source_target_pairs={{0,1},{1,0},{2,3},{3,2},{4,5},{5,4},{6,7},{7,6},{8,9},{9,8},{10,11... | collective-permute-start | bytes 2359304 | tf_op jit(solution)/shard_map/ppermute | solution.py:57
  97.4 0.0 copy-done
  97.5 0.1 neg.3
  97.5 0.2 convert_reduce_fusion
  97.7 2.0 %collective-permute-done.1 = bf16[512,768]{1,0:T(8,128)(2,1)S(1)} collective-permute-done((bf16[512,768]{1,0:T(8,128)(2,1)S(1)}, bf16[512,768]{1,0:T(8,128)(2,1)S(1)}, u32[]{:S(2)}, u32[]{:S(2)}) %collective-permute-start.1) | collective-permute-done | bytes 786464 | tf_op jit(solution)/shard_map/ppermute | solution.py:57
  99.7 0.2 fusion.1
  100.0 7.7 %all_to_all.37 = f32[4,8,128]{2,1,0:T(8,128)S(1)} all-to-all(f32[4,8,128]{2,1,0:T(8,128)S(1)} %broadcast_in_dim.19), channel_id=1, replica_groups=mesh['y'=8,'z'=8,'x'=4,'c'=2] {'x'}, dimensions={0} | all-to-all | bytes 32768 | tf_op jit(solution)/shard_map/all_to_all | solution.py:29
  107.7 0.4 fusion.2
  108.1 0.2 fusion.8
  108.4 0.2 fusion.3
  108.6 7.7 %all_to_all.38 = f32[4,8,128]{2,1,0:T(8,128)S(1)} all-to-all(f32[4,8,128]{2,1,0:T(8,128)S(1)} %broadcast_in_dim.21), channel_id=1, replica_groups=mesh['y'=8,'z'=8,'x'=4,'c'=2] {'x'}, dimensions={0} | all-to-all | bytes 32768 | tf_op jit(solution)/shard_map/all_to_all | solution.py:29
  116.3 0.2 fusion.4
  116.6 0.2 fusion.9
  116.8 0.2 fusion.10
  117.1 0.2 fusion.5
  117.4 7.7 %all_to_all.39 = f32[4,8,128]{2,1,0:T(8,128)S(1)} all-to-all(f32[4,8,128]{2,1,0:T(8,128)S(1)} %broadcast_in_dim.23), channel_id=1, replica_groups=mesh['y'=8,'z'=8,'x'=4,'c'=2] {'x'}, dimensions={0} | all-to-all | bytes 32768 | tf_op jit(solution)/shard_map/all_to_all | solution.py:29
  125.1 0.2 fusion.6
  125.3 0.2 fusion.11
  125.6 0.3 fusion.14
  125.9 0.8 fusion.22
  126.8 0.8 fusion
  127.7 0.1 pad_maximum_fusion
  127.8 18.3 %all_to_all.40 = bf16[4,136,1280]{2,1,0:T(8,128)(2,1)S(1)} all-to-all(bf16[4,136,1280]{2,1,0:T(8,128)(2,1)S(1)} %pad_maximum_fusion), channel_id=1, replica_groups=mesh['y'=8,'z'=8,'x'=4,'c'=2] {'x'}, dimensions={0} | all-to-all | bytes 2785280 | tf_op jit(solution)/shard_map/all_to_all | solution.py:84
  146.1 0.2 convert_reduce_fusion.1
  146.3 0.9 fusion.20
  (31 shorter events, 0.2 us)
Async XLA Ops:
  2.1 4.4 %copy-start.1 = (bf16[384,1280]{1,0:T(8,128)(2,1)S(1)}, bf16[384,1280]{1,0:T(8,128)(2,1)}, u32[]{:S(2)}) copy-start(bf16[384,1280]{1,0:T(8,128)(2,1)} %param.3) | copy-start | bytes 2949124
  2.1 22.3 %all-to-all-start = ((bf16[4,128,1280]{2,1,0:T(8,128)(2,1)}), bf16[4,128,1280]{2,1,0:T(8,128)(2,1)S(1)}, u32[]{:S(2)}, u32[]{:S(2)}) async-start(bf16[4,128,1280]{2,1,0:T(8,128)(2,1)} %broadcast_in_dim.16), calls=%async_computation | async-start | bytes 2621440 | tf_op jit(solution)/shard_map/all_to_all | solution.py:21
  6.5 18.8 %collective-permute-start = (bf16[384,1280]{1,0:T(8,128)(2,1)S(1)}, bf16[384,1280]{1,0:T(8,128)(2,1)S(1)}, u32[]{:S(2)}, u32[]{:S(2)}) collective-permute-start(bf16[384,1280]{1,0:T(8,128)(2,1)S(1)} %copy-done.1), channel_id=1, source_target_pairs={{0,1},{1,0},{2,3},{3,2},{4,5},{5,4},{6,7},{7,6},{8,9},{9,8},{10,11... | collective-permute-start | bytes 2949128 | tf_op jit(solution)/shard_map/ppermute | solution.py:45
  66.5 31.0 %copy-start = (bf16[128,1280]{1,0:T(8,128)(2,1)S(1)}, bf16[128,1280]{1,0:T(8,128)(2,1)}, u32[]{:S(2)}) copy-start(bf16[128,1280]{1,0:T(8,128)(2,1)} %param.2) | copy-start | bytes 983044
  95.5 4.2 %collective-permute-start.1 = (bf16[512,768]{1,0:T(8,128)(2,1)S(1)}, bf16[512,768]{1,0:T(8,128)(2,1)S(1)}, u32[]{:S(2)}, u32[]{:S(2)}) collective-permute-start(bf16[512,768]{1,0:T(8,128)(2,1)S(1)} %bitcast.49), channel_id=1, source_target_pairs={{0,1},{1,0},{2,3},{3,2},{4,5},{5,4},{6,7},{7,6},{8,9},{9,8},{10,11... | collective-permute-start | bytes 2359304 | tf_op jit(solution)/shard_map/ppermute | solution.py:57

commit v9 on v8

--- a/solution.py
+++ b/solution.py
@@ -3,6 +3,8 @@
 import jax
 import jax.numpy as jnp
 from jax import lax
+from jax.experimental import pallas as pl
+from jax.experimental.pallas import tpu as pltpu
 from jax.sharding import Mesh
 from jax.sharding import PartitionSpec as P
 
@@ -21,6 +23,32 @@
     return lax.all_to_all(jnp.broadcast_to(block[None], (n, *block.shape)), axes, 0, 0).reshape(
         n * block.shape[0], block.shape[1]
     )
+
+
+def copy_kernel(block_ref, copies_ref, sems):
+    half = block_ref.shape[0] // 2
+    copies = []
+    for k in range(X):
+        for h in range(2):
+            part = pl.ds(h * half, half)
+            copies.append(pltpu.make_async_copy(block_ref.at[part], copies_ref.at[k, part], sems.at[k, h]))
+    for copy in copies:
+        copy.start()
+    for copy in copies:
+        copy.wait()
+
+
+def copies_for_x(block):
+    return pl.pallas_call(
+        copy_kernel,
+        out_shape=jax.ShapeDtypeStruct((X, *block.shape), block.dtype),
+        in_specs=[pl.BlockSpec(memory_space=pltpu.HBM)],
+        out_specs=pl.BlockSpec(memory_space=pltpu.HBM),
+        scratch_shapes=[pltpu.SemaphoreType.DMA((X, 2))],
+        compiler_params=pltpu.CompilerParams(vmem_limit_bytes=4 * 1024 * 1024),
+        cost_estimate=pl.CostEstimate(flops=0, bytes_accessed=5 * block.size * 2, transcendentals=0),
+        name="noise_copies",
+    )(block)
 
 
 def sum_over_x(*parts):
@@ -43,7 +71,7 @@
     clips = latents.shape[0] * C
 
     other = lax.ppermute(latents, "c", SWAP)
-    noise_rows = gather_by_a2a(noise, "x", X)
+    noise_rows = lax.all_to_all(copies_for_x(noise), "x", 0, 0).reshape(rows, features)
 
     def partial_scores(block):
         scores = lax.dot_general(noise_rows, block, (((1,), (1,)), ((), ())), preferred_element_type=jnp.float32)

time: 148 us -> 148 us (level)
    broadcast_in_dim x2 -> x1, local copies, waits for them, and re-layouts: 2.17 us -> 0.05 us  [gather_by_a2a(): jnp.broadcast_to(block[None], (n, *block.shape))]
where the time goes in v9:
time: 148 us; the launch traced here: 147 us
  blocking collectives  110 us (74%)
  waiting for transfers between devices  18 us (12%)
  starting transfers between devices  8.25 us (6%)
  other arithmetic  4.7 us (3%)
  matrix products  3.41 us (2%)
    all_to_all x1, blocking collectives, body(): arrived = lax.all_to_all(partial, WIDE, 0, 0)  40.1 us
    all_to_all x1, blocking collectives, gather_by_a2a(): lax.all_to_all(jnp.broadcast_to(block[None], (n, *block.shape)), axes, 0, 0)  28.8 us
    all_to_all x3, blocking collectives, sum_over_x(): lax.all_to_all(jnp.broadcast_to(send, (X, *send.shape[1:])), 'x', 0, 0)  23.1 us
    all_to_all x1, blocking collectives, body(): parts = jnp.sum(lax.all_to_all(send, 'x', 0, 0).astype(jnp.float32), axis=0)  18.3 us
    all_to_all x1, waiting for transfers between devices, body(): lax.all_to_all(copies_for_x(noise), 'x', 0, 0).reshape(rows, features)  16 us
    all_to_all x1, starting transfers between devices, body(): lax.all_to_all(copies_for_x(noise), 'x', 0, 0).reshape(rows, features)  4.44 us
  transfers between devices with their start and end apart: 3, of which 2 were waited for; matrix products, arithmetic and copies ran while one was open for 1% of the time, Pallas kernels for 0%

profile of v9, /device:TPU:16, one launch (start us, length us, event | category | flops | bytes accessed | tf_op | source)
XLA Modules:
  0.0 147.2 jit_solution(1644560388711796310)
XLA Ops:
  0.0 0.0 copy-start
  0.0 1.0 copy-done
  1.0 1.1 noise_copies.1
  2.1 0.0 copy-start.2
  2.1 4.4 %all-to-all-start = ((bf16[4,128,1280]{2,1,0:T(8,128)(2,1)}), bf16[4,128,1280]{2,1,0:T(8,128)(2,1)S(1)}, u32[]{:S(2)}, u32[]{:S(2)}) async-start(bf16[4,128,1280]{2,1,0:T(8,128)(2,1)} %noise_copies.1), calls=%async_computation | async-start | bytes 2621440 | tf_op jit(solution)/shard_map/all_to_all | solution.py:74
  6.6 0.0 copy-done.2
  6.6 1.9 %collective-permute-start = (bf16[384,1280]{1,0:T(8,128)(2,1)S(1)}, bf16[384,1280]{1,0:T(8,128)(2,1)S(1)}, u32[]{:S(2)}, u32[]{:S(2)}) collective-permute-start(bf16[384,1280]{1,0:T(8,128)(2,1)S(1)} %copy-done.2), channel_id=1, source_target_pairs={{0,1},{1,0},{2,3},{3,2},{4,5},{5,4},{6,7},{7,6},{8,9},{9,8},{10,11... | collective-permute-start | bytes 2949128 | tf_op jit(solution)/shard_map/ppermute | solution.py:73
  8.5 16.0 %all-to-all-done = bf16[4,128,1280]{2,1,0:T(8,128)(2,1)S(1)} async-done(((bf16[4,128,1280]{2,1,0:T(8,128)(2,1)}), bf16[4,128,1280]{2,1,0:T(8,128)(2,1)S(1)}, u32[]{:S(2)}, u32[]{:S(2)}) %all-to-all-start) | async-done | bytes 1310752 | tf_op jit(solution)/shard_map/all_to_all | solution.py:74
  24.5 0.9 fusion.18
  25.3 0.0 collective-permute-done
  25.3 0.9 fusion.17
  26.2 0.2 pad_maximum_fusion.1
  26.4 40.1 %all_to_all.35 = f16[64,2,8,384]{3,2,1,0:T(8,128)(2,1)S(1)} all-to-all(f16[64,2,8,384]{3,2,1,0:T(8,128)(2,1)S(1)} %pad_maximum_fusion.1), channel_id=1, replica_groups=mesh['y'=8,'z'=8,'x'=4,'c'=2] {'y','z'}, dimensions={0} | all-to-all | bytes 1572864 | tf_op jit(solution)/shard_map/all_to_all | solution.py:81
  66.5 0.0 copy-start.1
  66.5 0.1 convert_reduce_fusion.2
  66.7 0.1 broadcast_in_dim.14
  66.7 28.8 %all_to_all.36 = bf16[64,8,768]{2,1,0:T(8,128)(2,1)S(1)} all-to-all(bf16[64,8,768]{2,1,0:T(8,128)(2,1)S(1)} %broadcast_in_dim.14), channel_id=1, replica_groups=mesh['y'=8,'z'=8,'x'=4,'c'=2] {'y','z'}, dimensions={0} | all-to-all | bytes 1572864 | tf_op jit(solution)/shard_map/all_to_all | solution.py:23
  95.5 1.9 %collective-permute-start.1 = (bf16[512,768]{1,0:T(8,128)(2,1)S(1)}, bf16[512,768]{1,0:T(8,128)(2,1)S(1)}, u32[]{:S(2)}, u32[]{:S(2)}) collective-permute-start(bf16[512,768]{1,0:T(8,128)(2,1)S(1)} %bitcast.49), channel_id=1, source_target_pairs={{0,1},{1,0},{2,3},{3,2},{4,5},{5,4},{6,7},{7,6},{8,9},{9,8},{10,11... | collective-permute-start | bytes 2359304 | tf_op jit(solution)/shard_map/ppermute | solution.py:85
  97.5 0.0 copy-done.1
  97.5 0.1 neg.3
  97.6 0.2 convert_reduce_fusion
  97.7 2.0 %collective-permute-done.1 = bf16[512,768]{1,0:T(8,128)(2,1)S(1)} collective-permute-done((bf16[512,768]{1,0:T(8,128)(2,1)S(1)}, bf16[512,768]{1,0:T(8,128)(2,1)S(1)}, u32[]{:S(2)}, u32[]{:S(2)}) %collective-permute-start.1) | collective-permute-done | bytes 786464 | tf_op jit(solution)/shard_map/ppermute | solution.py:85
  99.7 0.2 fusion.1
  100.0 7.7 %all_to_all.37 = f32[4,8,128]{2,1,0:T(8,128)S(1)} all-to-all(f32[4,8,128]{2,1,0:T(8,128)S(1)} %broadcast_in_dim.16), channel_id=1, replica_groups=mesh['y'=8,'z'=8,'x'=4,'c'=2] {'x'}, dimensions={0} | all-to-all | bytes 32768 | tf_op jit(solution)/shard_map/all_to_all | solution.py:57
  107.7 0.4 fusion.2
  108.1 0.2 fusion.8
  108.4 0.2 fusion.3
  108.6 7.7 %all_to_all.38 = f32[4,8,128]{2,1,0:T(8,128)S(1)} all-to-all(f32[4,8,128]{2,1,0:T(8,128)S(1)} %broadcast_in_dim.18), channel_id=1, replica_groups=mesh['y'=8,'z'=8,'x'=4,'c'=2] {'x'}, dimensions={0} | all-to-all | bytes 32768 | tf_op jit(solution)/shard_map/all_to_all | solution.py:57
  116.4 0.2 fusion.4
  116.6 0.2 fusion.9
  116.9 0.2 fusion.10
  117.1 0.2 fusion.5
  117.4 7.7 %all_to_all.39 = f32[4,8,128]{2,1,0:T(8,128)S(1)} all-to-all(f32[4,8,128]{2,1,0:T(8,128)S(1)} %broadcast_in_dim.20), channel_id=1, replica_groups=mesh['y'=8,'z'=8,'x'=4,'c'=2] {'x'}, dimensions={0} | all-to-all | bytes 32768 | tf_op jit(solution)/shard_map/all_to_all | solution.py:57
  125.1 0.2 fusion.6
  125.4 0.2 fusion.11
  125.6 0.3 fusion.14
  125.9 0.8 fusion.22
  126.8 0.8 fusion
  127.7 0.1 pad_maximum_fusion
  127.8 18.3 %all_to_all.40 = bf16[4,136,1280]{2,1,0:T(8,128)(2,1)S(1)} all-to-all(bf16[4,136,1280]{2,1,0:T(8,128)(2,1)S(1)} %pad_maximum_fusion), channel_id=1, replica_groups=mesh['y'=8,'z'=8,'x'=4,'c'=2] {'x'}, dimensions={0} | all-to-all | bytes 2785280 | tf_op jit(solution)/shard_map/all_to_all | solution.py:112
  146.1 0.2 convert_reduce_fusion.1
  146.3 0.9 fusion.20
  (31 shorter events, 0.2 us)
Async XLA Ops:
  0.0 1.0 copy-start
  2.1 4.5 %copy-start.2 = (bf16[384,1280]{1,0:T(8,128)(2,1)S(1)}, bf16[384,1280]{1,0:T(8,128)(2,1)}, u32[]{:S(2)}) copy-start(bf16[384,1280]{1,0:T(8,128)(2,1)} %param.3) | copy-start | bytes 2949124
  2.1 22.3 %all-to-all-start = ((bf16[4,128,1280]{2,1,0:T(8,128)(2,1)}), bf16[4,128,1280]{2,1,0:T(8,128)(2,1)S(1)}, u32[]{:S(2)}, u32[]{:S(2)}) async-start(bf16[4,128,1280]{2,1,0:T(8,128)(2,1)} %noise_copies.1), calls=%async_computation | async-start | bytes 2621440 | tf_op jit(solution)/shard_map/all_to_all | solution.py:74
  6.6 18.8 %collective-permute-start = (bf16[384,1280]{1,0:T(8,128)(2,1)S(1)}, bf16[384,1280]{1,0:T(8,128)(2,1)S(1)}, u32[]{:S(2)}, u32[]{:S(2)}) collective-permute-start(bf16[384,1280]{1,0:T(8,128)(2,1)S(1)} %copy-done.2), channel_id=1, source_target_pairs={{0,1},{1,0},{2,3},{3,2},{4,5},{5,4},{6,7},{7,6},{8,9},{9,8},{10,11... | collective-permute-start | bytes 2949128 | tf_op jit(solution)/shard_map/ppermute | solution.py:73
  66.5 31.0 %copy-start.1 = (bf16[128,1280]{1,0:T(8,128)(2,1)S(1)}, bf16[128,1280]{1,0:T(8,128)(2,1)}, u32[]{:S(2)}) copy-start(bf16[128,1280]{1,0:T(8,128)(2,1)} %block_ref.1) | copy-start | bytes 983044
  95.5 4.2 %collective-permute-start.1 = (bf16[512,768]{1,0:T(8,128)(2,1)S(1)}, bf16[512,768]{1,0:T(8,128)(2,1)S(1)}, u32[]{:S(2)}, u32[]{:S(2)}) collective-permute-start(bf16[512,768]{1,0:T(8,128)(2,1)S(1)} %bitcast.49), channel_id=1, source_target_pairs={{0,1},{1,0},{2,3},{3,2},{4,5},{5,4},{6,7},{7,6},{8,9},{9,8},{10,11... | collective-permute-start | bytes 2359304 | tf_op jit(solution)/shard_map/ppermute | solution.py:85

commit v10 on v9

--- a/solution.py
+++ b/solution.py
@@ -48,7 +48,7 @@
         compiler_params=pltpu.CompilerParams(vmem_limit_bytes=4 * 1024 * 1024),
         cost_estimate=pl.CostEstimate(flops=0, bytes_accessed=5 * block.size * 2, transcendentals=0),
         name="noise_copies",
-    )(block)
+    )(pltpu.with_memory_space_constraint(block, pltpu.HBM))
 
 
 def sum_over_x(*parts):

time: 148 us -> 186 us (1.26)
  Pallas kernels: 1.13 us -> 40.9 us
    pallas_call x1, Pallas kernels: 1.13 us -> 40.9 us  [copies_for_x(): pl.pallas_call(copy_kernel, out_shape=jax.ShapeDtypeStruct((X, *block.sha...]
where the time goes in v10:
time: 186 us
  blocking collectives  110 us (59%)
  Pallas kernels  40.9 us (22%)
  waiting for transfers between devices  18 us (10%)
  starting transfers between devices  8.25 us (4%)
  other arithmetic  4.7 us (3%)
  matrix products  3.41 us (2%)
    pallas_call x1, Pallas kernels, copies_for_x(): pl.pallas_call(copy_kernel, out_shape=jax.ShapeDtypeStruct((X, *block.sha...  40.9 us
    all_to_all x1, blocking collectives, body(): arrived = lax.all_to_all(partial, WIDE, 0, 0)  40.1 us
    all_to_all x1, blocking collectives, gather_by_a2a(): lax.all_to_all(jnp.broadcast_to(block[None], (n, *block.shape)), axes, 0, 0)  28.8 us
    all_to_all x3, blocking collectives, sum_over_x(): lax.all_to_all(jnp.broadcast_to(send, (X, *send.shape[1:])), 'x', 0, 0)  23.1 us
    all_to_all x1, blocking collectives, body(): parts = jnp.sum(lax.all_to_all(send, 'x', 0, 0).astype(jnp.float32), axis=0)  18.3 us
    all_to_all x1, waiting for transfers between devices, body(): lax.all_to_all(copies_for_x(noise), 'x', 0, 0).reshape(rows, features)  16 us
    all_to_all x1, starting transfers between devices, body(): lax.all_to_all(copies_for_x(noise), 'x', 0, 0).reshape(rows, features)  4.44 us
  transfers between devices with their start and end apart: 3, of which 2 were waited for; matrix products, arithmetic and copies ran while one was open for 1% of the time, Pallas kernels for 0%

profile of v10, /device:TPU:16, one launch (start us, length us, event | category | flops | bytes accessed | tf_op | source)
XLA Modules:
  0.0 186.0 jit_solution(11736310624710770750)
XLA Ops:
  0.0 40.9 %noise_copies.1 = bf16[4,128,1280]{2,1,0:T(8,128)(2,1)} custom-call(bf16[128,1280]{1,0:T(8,128)(2,1)} %block_ref.1), custom_call_target="tpu_custom_call" | custom-call | bytes 1638400 | tf_op jit(solution)/shard_map/noise_copies/pallas_call | solution.py:42
  40.9 0.0 copy-start.1
  40.9 4.4 %all-to-all-start = ((bf16[4,128,1280]{2,1,0:T(8,128)(2,1)}), bf16[4,128,1280]{2,1,0:T(8,128)(2,1)S(1)}, u32[]{:S(2)}, u32[]{:S(2)}) async-start(bf16[4,128,1280]{2,1,0:T(8,128)(2,1)} %noise_copies.1), calls=%async_computation | async-start | bytes 2621440 | tf_op jit(solution)/shard_map/all_to_all | solution.py:74
  45.3 0.0 copy-done.1
  45.3 1.9 %collective-permute-start = (bf16[384,1280]{1,0:T(8,128)(2,1)S(1)}, bf16[384,1280]{1,0:T(8,128)(2,1)S(1)}, u32[]{:S(2)}, u32[]{:S(2)}) collective-permute-start(bf16[384,1280]{1,0:T(8,128)(2,1)S(1)} %copy-done.1), channel_id=1, source_target_pairs={{0,1},{1,0},{2,3},{3,2},{4,5},{5,4},{6,7},{7,6},{8,9},{9,8},{10,11... | collective-permute-start | bytes 2949128 | tf_op jit(solution)/shard_map/ppermute | solution.py:73
  47.3 16.0 %all-to-all-done = bf16[4,128,1280]{2,1,0:T(8,128)(2,1)S(1)} async-done(((bf16[4,128,1280]{2,1,0:T(8,128)(2,1)}), bf16[4,128,1280]{2,1,0:T(8,128)(2,1)S(1)}, u32[]{:S(2)}, u32[]{:S(2)}) %all-to-all-start) | async-done | bytes 1310752 | tf_op jit(solution)/shard_map/all_to_all | solution.py:74
  63.2 0.9 fusion.18
  64.1 0.0 collective-permute-done
  64.1 0.9 fusion.17
  65.0 0.2 pad_maximum_fusion.1
  65.2 40.1 %all_to_all.35 = f16[64,2,8,384]{3,2,1,0:T(8,128)(2,1)S(1)} all-to-all(f16[64,2,8,384]{3,2,1,0:T(8,128)(2,1)S(1)} %pad_maximum_fusion.1), channel_id=1, replica_groups=mesh['y'=8,'z'=8,'x'=4,'c'=2] {'y','z'}, dimensions={0} | all-to-all | bytes 1572864 | tf_op jit(solution)/shard_map/all_to_all | solution.py:81
  105.2 0.0 copy-start
  105.3 0.1 convert_reduce_fusion.2
  105.4 0.1 broadcast_in_dim.14
  105.5 28.8 %all_to_all.36 = bf16[64,8,768]{2,1,0:T(8,128)(2,1)S(1)} all-to-all(bf16[64,8,768]{2,1,0:T(8,128)(2,1)S(1)} %broadcast_in_dim.14), channel_id=1, replica_groups=mesh['y'=8,'z'=8,'x'=4,'c'=2] {'y','z'}, dimensions={0} | all-to-all | bytes 1572864 | tf_op jit(solution)/shard_map/all_to_all | solution.py:23
  134.3 1.9 %collective-permute-start.1 = (bf16[512,768]{1,0:T(8,128)(2,1)S(1)}, bf16[512,768]{1,0:T(8,128)(2,1)S(1)}, u32[]{:S(2)}, u32[]{:S(2)}) collective-permute-start(bf16[512,768]{1,0:T(8,128)(2,1)S(1)} %bitcast.49), channel_id=1, source_target_pairs={{0,1},{1,0},{2,3},{3,2},{4,5},{5,4},{6,7},{7,6},{8,9},{9,8},{10,11... | collective-permute-start | bytes 2359304 | tf_op jit(solution)/shard_map/ppermute | solution.py:85
  136.2 0.0 copy-done
  136.3 0.1 neg.3
  136.3 0.2 convert_reduce_fusion
  136.5 2.0 %collective-permute-done.1 = bf16[512,768]{1,0:T(8,128)(2,1)S(1)} collective-permute-done((bf16[512,768]{1,0:T(8,128)(2,1)S(1)}, bf16[512,768]{1,0:T(8,128)(2,1)S(1)}, u32[]{:S(2)}, u32[]{:S(2)}) %collective-permute-start.1) | collective-permute-done | bytes 786464 | tf_op jit(solution)/shard_map/ppermute | solution.py:85
  138.5 0.2 fusion.1
  138.7 7.7 %all_to_all.37 = f32[4,8,128]{2,1,0:T(8,128)S(1)} all-to-all(f32[4,8,128]{2,1,0:T(8,128)S(1)} %broadcast_in_dim.16), channel_id=1, replica_groups=mesh['y'=8,'z'=8,'x'=4,'c'=2] {'x'}, dimensions={0} | all-to-all | bytes 32768 | tf_op jit(solution)/shard_map/all_to_all | solution.py:57
  146.5 0.4 fusion.2
  146.9 0.2 fusion.8
  147.2 0.2 fusion.3
  147.4 7.7 %all_to_all.38 = f32[4,8,128]{2,1,0:T(8,128)S(1)} all-to-all(f32[4,8,128]{2,1,0:T(8,128)S(1)} %broadcast_in_dim.18), channel_id=1, replica_groups=mesh['y'=8,'z'=8,'x'=4,'c'=2] {'x'}, dimensions={0} | all-to-all | bytes 32768 | tf_op jit(solution)/shard_map/all_to_all | solution.py:57
  155.1 0.2 fusion.4
  155.4 0.2 fusion.9
  155.6 0.2 fusion.10
  155.9 0.2 fusion.5
  156.2 7.7 %all_to_all.39 = f32[4,8,128]{2,1,0:T(8,128)S(1)} all-to-all(f32[4,8,128]{2,1,0:T(8,128)S(1)} %broadcast_in_dim.20), channel_id=1, replica_groups=mesh['y'=8,'z'=8,'x'=4,'c'=2] {'x'}, dimensions={0} | all-to-all | bytes 32768 | tf_op jit(solution)/shard_map/all_to_all | solution.py:57
  163.9 0.2 fusion.6
  164.1 0.2 fusion.11
  164.4 0.3 fusion.14
  164.7 0.8 fusion.22
  165.6 0.8 fusion
  166.5 0.1 pad_maximum_fusion
  166.6 18.3 %all_to_all.40 = bf16[4,136,1280]{2,1,0:T(8,128)(2,1)S(1)} all-to-all(bf16[4,136,1280]{2,1,0:T(8,128)(2,1)S(1)} %pad_maximum_fusion), channel_id=1, replica_groups=mesh['y'=8,'z'=8,'x'=4,'c'=2] {'x'}, dimensions={0} | all-to-all | bytes 2785280 | tf_op jit(solution)/shard_map/all_to_all | solution.py:112
  184.9 0.2 convert_reduce_fusion.1
  185.1 0.9 fusion.20
  (31 shorter events, 0.2 us)
Async XLA Ops:
  40.9 4.5 %copy-start.1 = (bf16[384,1280]{1,0:T(8,128)(2,1)S(1)}, bf16[384,1280]{1,0:T(8,128)(2,1)}, u32[]{:S(2)}) copy-start(bf16[384,1280]{1,0:T(8,128)(2,1)} %param.3) | copy-start | bytes 2949124
  40.9 22.3 %all-to-all-start = ((bf16[4,128,1280]{2,1,0:T(8,128)(2,1)}), bf16[4,128,1280]{2,1,0:T(8,128)(2,1)S(1)}, u32[]{:S(2)}, u32[]{:S(2)}) async-start(bf16[4,128,1280]{2,1,0:T(8,128)(2,1)} %noise_copies.1), calls=%async_computation | async-start | bytes 2621440 | tf_op jit(solution)/shard_map/all_to_all | solution.py:74
  45.3 18.8 %collective-permute-start = (bf16[384,1280]{1,0:T(8,128)(2,1)S(1)}, bf16[384,1280]{1,0:T(8,128)(2,1)S(1)}, u32[]{:S(2)}, u32[]{:S(2)}) collective-permute-start(bf16[384,1280]{1,0:T(8,128)(2,1)S(1)} %copy-done.1), channel_id=1, source_target_pairs={{0,1},{1,0},{2,3},{3,2},{4,5},{5,4},{6,7},{7,6},{8,9},{9,8},{10,11... | collective-permute-start | bytes 2949128 | tf_op jit(solution)/shard_map/ppermute | solution.py:73
  105.2 31.0 %copy-start = (bf16[128,1280]{1,0:T(8,128)(2,1)S(1)}, bf16[128,1280]{1,0:T(8,128)(2,1)}, u32[]{:S(2)}) copy-start(bf16[128,1280]{1,0:T(8,128)(2,1)} %block_ref.1) | copy-start | bytes 983044
  134.3 4.2 %collective-permute-start.1 = (bf16[512,768]{1,0:T(8,128)(2,1)S(1)}, bf16[512,768]{1,0:T(8,128)(2,1)S(1)}, u32[]{:S(2)}, u32[]{:S(2)}) collective-permute-start(bf16[512,768]{1,0:T(8,128)(2,1)S(1)} %bitcast.49), channel_id=1, source_target_pairs={{0,1},{1,0},{2,3},{3,2},{4,5},{5,4},{6,7},{7,6},{8,9},{9,8},{10,11... | collective-permute-start | bytes 2359304 | tf_op jit(solution)/shard_map/ppermute | solution.py:85

commit v11 on v10

--- a/solution.py
+++ b/solution.py
@@ -17,6 +17,7 @@
 SEND_SCALE = 64.0
 LANES = 128
 TILE = 8
+PIECES = 4
 
 
 def gather_by_a2a(block, axes, n):
@@ -25,15 +26,18 @@
     )
 
 
-def copy_kernel(block_ref, copies_ref, sems):
-    half = block_ref.shape[0] // 2
+def copy_kernel(block_ref, copies_ref, held, in_sems, out_sems):
+    size = block_ref.shape[0] // PIECES
+    pieces = [pl.ds(p * size, size) for p in range(PIECES)]
+    loads = [pltpu.make_async_copy(block_ref.at[d], held.at[d], in_sems.at[p]) for p, d in enumerate(pieces)]
+    for load in loads:
+        load.start()
     copies = []
-    for k in range(X):
-        for h in range(2):
-            part = pl.ds(h * half, half)
-            copies.append(pltpu.make_async_copy(block_ref.at[part], copies_ref.at[k, part], sems.at[k, h]))
-    for copy in copies:
-        copy.start()
+    for p, d in enumerate(pieces):
+        loads[p].wait()
+        for k in range(X):
+            copies.append(pltpu.make_async_copy(held.at[d], copies_ref.at[k, d], out_sems.at[p, k]))
+            copies[-1].start()
     for copy in copies:
         copy.wait()
 
@@ -44,7 +48,11 @@
         out_shape=jax.ShapeDtypeStruct((X, *block.shape), block.dtype),
         in_specs=[pl.BlockSpec(memory_space=pltpu.HBM)],
         out_specs=pl.BlockSpec(memory_space=pltpu.HBM),
-        scratch_shapes=[pltpu.SemaphoreType.DMA((X, 2))],
+        scratch_shapes=[
+            pltpu.VMEM(block.shape, block.dtype),
+            pltpu.SemaphoreType.DMA((PIECES,)),
+            pltpu.SemaphoreType.DMA((PIECES, X)),
+        ],
         compiler_params=pltpu.CompilerParams(vmem_limit_bytes=4 * 1024 * 1024),
         cost_estimate=pl.CostEstimate(flops=0, bytes_accessed=5 * block.size * 2, transcendentals=0),
         name="noise_copies",

time: 186 us -> 148 us (0.80)
  Pallas kernels: 40.9 us -> 2.14 us
    pallas_call x1, Pallas kernels: 40.9 us -> 2.14 us  [copies_for_x(): pl.pallas_call(copy_kernel, out_shape=jax.ShapeDtypeStruct((X, *block.sha...]
where the time goes in v11:
time: 148 us; the launch traced here: 147 us
  blocking collectives  110 us (74%)
  waiting for transfers between devices  18 us (12%)
  starting transfers between devices  8.25 us (6%)
  other arithmetic  4.7 us (3%)
  matrix products  3.41 us (2%)
  Pallas kernels  2.14 us (1%)
    all_to_all x1, blocking collectives, body(): arrived = lax.all_to_all(partial, WIDE, 0, 0)  40.1 us
    all_to_all x1, blocking collectives, gather_by_a2a(): lax.all_to_all(jnp.broadcast_to(block[None], (n, *block.shape)), axes, 0, 0)  28.8 us
    all_to_all x3, blocking collectives, sum_over_x(): lax.all_to_all(jnp.broadcast_to(send, (X, *send.shape[1:])), 'x', 0, 0)  23.1 us
    all_to_all x1, blocking collectives, body(): parts = jnp.sum(lax.all_to_all(send, 'x', 0, 0).astype(jnp.float32), axis=0)  18.3 us
    all_to_all x1, waiting for transfers between devices, body(): lax.all_to_all(copies_for_x(noise), 'x', 0, 0).reshape(rows, features)  16 us
    all_to_all x1, starting transfers between devices, body(): lax.all_to_all(copies_for_x(noise), 'x', 0, 0).reshape(rows, features)  4.44 us
  transfers between devices with their start and end apart: 3, of which 2 were waited for; matrix products, arithmetic and copies ran while one was open for 1% of the time, Pallas kernels for 0%

profile of v11, /device:TPU:16, one launch (start us, length us, event | category | flops | bytes accessed | tf_op | source)
XLA Modules:
  0.0 147.2 jit_solution(7844774090049370832)
XLA Ops:
  0.0 2.1 %noise_copies.1 = bf16[4,128,1280]{2,1,0:T(8,128)(2,1)} custom-call(bf16[128,1280]{1,0:T(8,128)(2,1)} %block_ref.1), custom_call_target="tpu_custom_call" | custom-call | bytes 1638400 | tf_op jit(solution)/shard_map/noise_copies/pallas_call | solution.py:46
  2.1 0.0 copy-start.1
  2.2 4.4 %all-to-all-start = ((bf16[4,128,1280]{2,1,0:T(8,128)(2,1)}), bf16[4,128,1280]{2,1,0:T(8,128)(2,1)S(1)}, u32[]{:S(2)}, u32[]{:S(2)}) async-start(bf16[4,128,1280]{2,1,0:T(8,128)(2,1)} %noise_copies.1), calls=%async_computation | async-start | bytes 2621440 | tf_op jit(solution)/shard_map/all_to_all | solution.py:82
  6.6 0.0 copy-done.1
  6.6 1.9 %collective-permute-start = (bf16[384,1280]{1,0:T(8,128)(2,1)S(1)}, bf16[384,1280]{1,0:T(8,128)(2,1)S(1)}, u32[]{:S(2)}, u32[]{:S(2)}) collective-permute-start(bf16[384,1280]{1,0:T(8,128)(2,1)S(1)} %copy-done.1), channel_id=1, source_target_pairs={{0,1},{1,0},{2,3},{3,2},{4,5},{5,4},{6,7},{7,6},{8,9},{9,8},{10,11... | collective-permute-start | bytes 2949128 | tf_op jit(solution)/shard_map/ppermute | solution.py:81
  8.5 16.0 %all-to-all-done = bf16[4,128,1280]{2,1,0:T(8,128)(2,1)S(1)} async-done(((bf16[4,128,1280]{2,1,0:T(8,128)(2,1)}), bf16[4,128,1280]{2,1,0:T(8,128)(2,1)S(1)}, u32[]{:S(2)}, u32[]{:S(2)}) %all-to-all-start) | async-done | bytes 1310752 | tf_op jit(solution)/shard_map/all_to_all | solution.py:82
  24.5 0.9 fusion.18
  25.4 0.0 collective-permute-done
  25.4 0.9 fusion.17
  26.2 0.2 pad_maximum_fusion.1
  26.4 40.1 %all_to_all.35 = f16[64,2,8,384]{3,2,1,0:T(8,128)(2,1)S(1)} all-to-all(f16[64,2,8,384]{3,2,1,0:T(8,128)(2,1)S(1)} %pad_maximum_fusion.1), channel_id=1, replica_groups=mesh['y'=8,'z'=8,'x'=4,'c'=2] {'y','z'}, dimensions={0} | all-to-all | bytes 1572864 | tf_op jit(solution)/shard_map/all_to_all | solution.py:89
  66.5 0.0 copy-start
  66.5 0.1 convert_reduce_fusion.2
  66.7 0.1 broadcast_in_dim.14
  66.8 28.8 %all_to_all.36 = bf16[64,8,768]{2,1,0:T(8,128)(2,1)S(1)} all-to-all(bf16[64,8,768]{2,1,0:T(8,128)(2,1)S(1)} %broadcast_in_dim.14), channel_id=1, replica_groups=mesh['y'=8,'z'=8,'x'=4,'c'=2] {'y','z'}, dimensions={0} | all-to-all | bytes 1572864 | tf_op jit(solution)/shard_map/all_to_all | solution.py:24
  95.6 1.9 %collective-permute-start.1 = (bf16[512,768]{1,0:T(8,128)(2,1)S(1)}, bf16[512,768]{1,0:T(8,128)(2,1)S(1)}, u32[]{:S(2)}, u32[]{:S(2)}) collective-permute-start(bf16[512,768]{1,0:T(8,128)(2,1)S(1)} %bitcast.49), channel_id=1, source_target_pairs={{0,1},{1,0},{2,3},{3,2},{4,5},{5,4},{6,7},{7,6},{8,9},{9,8},{10,11... | collective-permute-start | bytes 2359304 | tf_op jit(solution)/shard_map/ppermute | solution.py:93
  97.5 0.0 copy-done
  97.5 0.1 neg.3
  97.6 0.2 convert_reduce_fusion
  97.8 2.0 %collective-permute-done.1 = bf16[512,768]{1,0:T(8,128)(2,1)S(1)} collective-permute-done((bf16[512,768]{1,0:T(8,128)(2,1)S(1)}, bf16[512,768]{1,0:T(8,128)(2,1)S(1)}, u32[]{:S(2)}, u32[]{:S(2)}) %collective-permute-start.1) | collective-permute-done | bytes 786464 | tf_op jit(solution)/shard_map/ppermute | solution.py:93
  99.7 0.2 fusion.1
  100.0 7.7 %all_to_all.37 = f32[4,8,128]{2,1,0:T(8,128)S(1)} all-to-all(f32[4,8,128]{2,1,0:T(8,128)S(1)} %broadcast_in_dim.16), channel_id=1, replica_groups=mesh['y'=8,'z'=8,'x'=4,'c'=2] {'x'}, dimensions={0} | all-to-all | bytes 32768 | tf_op jit(solution)/shard_map/all_to_all | solution.py:65
  107.7 0.4 fusion.2
  108.2 0.2 fusion.8
  108.4 0.2 fusion.3
  108.7 7.7 %all_to_all.38 = f32[4,8,128]{2,1,0:T(8,128)S(1)} all-to-all(f32[4,8,128]{2,1,0:T(8,128)S(1)} %broadcast_in_dim.18), channel_id=1, replica_groups=mesh['y'=8,'z'=8,'x'=4,'c'=2] {'x'}, dimensions={0} | all-to-all | bytes 32768 | tf_op jit(solution)/shard_map/all_to_all | solution.py:65
  116.4 0.2 fusion.4
  116.6 0.2 fusion.9
  116.9 0.2 fusion.10
  117.2 0.2 fusion.5
  117.4 7.7 %all_to_all.39 = f32[4,8,128]{2,1,0:T(8,128)S(1)} all-to-all(f32[4,8,128]{2,1,0:T(8,128)S(1)} %broadcast_in_dim.20), channel_id=1, replica_groups=mesh['y'=8,'z'=8,'x'=4,'c'=2] {'x'}, dimensions={0} | all-to-all | bytes 32768 | tf_op jit(solution)/shard_map/all_to_all | solution.py:65
  125.1 0.2 fusion.6
  125.4 0.2 fusion.11
  125.6 0.3 fusion.14
  126.0 0.8 fusion.22
  126.9 0.8 fusion
  127.7 0.1 pad_maximum_fusion
  127.8 18.3 %all_to_all.40 = bf16[4,136,1280]{2,1,0:T(8,128)(2,1)S(1)} all-to-all(bf16[4,136,1280]{2,1,0:T(8,128)(2,1)S(1)} %pad_maximum_fusion), channel_id=1, replica_groups=mesh['y'=8,'z'=8,'x'=4,'c'=2] {'x'}, dimensions={0} | all-to-all | bytes 2785280 | tf_op jit(solution)/shard_map/all_to_all | solution.py:120
  146.1 0.2 convert_reduce_fusion.1
  146.4 0.9 fusion.20
  (31 shorter events, 0.2 us)
Async XLA Ops:
  2.1 4.5 %copy-start.1 = (bf16[384,1280]{1,0:T(8,128)(2,1)S(1)}, bf16[384,1280]{1,0:T(8,128)(2,1)}, u32[]{:S(2)}) copy-start(bf16[384,1280]{1,0:T(8,128)(2,1)} %param.3) | copy-start | bytes 2949124
  2.2 22.3 %all-to-all-start = ((bf16[4,128,1280]{2,1,0:T(8,128)(2,1)}), bf16[4,128,1280]{2,1,0:T(8,128)(2,1)S(1)}, u32[]{:S(2)}, u32[]{:S(2)}) async-start(bf16[4,128,1280]{2,1,0:T(8,128)(2,1)} %noise_copies.1), calls=%async_computation | async-start | bytes 2621440 | tf_op jit(solution)/shard_map/all_to_all | solution.py:82
  6.6 18.8 %collective-permute-start = (bf16[384,1280]{1,0:T(8,128)(2,1)S(1)}, bf16[384,1280]{1,0:T(8,128)(2,1)S(1)}, u32[]{:S(2)}, u32[]{:S(2)}) collective-permute-start(bf16[384,1280]{1,0:T(8,128)(2,1)S(1)} %copy-done.1), channel_id=1, source_target_pairs={{0,1},{1,0},{2,3},{3,2},{4,5},{5,4},{6,7},{7,6},{8,9},{9,8},{10,11... | collective-permute-start | bytes 2949128 | tf_op jit(solution)/shard_map/ppermute | solution.py:81
  66.5 31.0 %copy-start = (bf16[128,1280]{1,0:T(8,128)(2,1)S(1)}, bf16[128,1280]{1,0:T(8,128)(2,1)}, u32[]{:S(2)}) copy-start(bf16[128,1280]{1,0:T(8,128)(2,1)} %block_ref.1) | copy-start | bytes 983044
  95.6 4.2 %collective-permute-start.1 = (bf16[512,768]{1,0:T(8,128)(2,1)S(1)}, bf16[512,768]{1,0:T(8,128)(2,1)S(1)}, u32[]{:S(2)}, u32[]{:S(2)}) collective-permute-start(bf16[512,768]{1,0:T(8,128)(2,1)S(1)} %bitcast.49), channel_id=1, source_target_pairs={{0,1},{1,0},{2,3},{3,2},{4,5},{5,4},{6,7},{7,6},{8,9},{9,8},{10,11... | collective-permute-start | bytes 2359304 | tf_op jit(solution)/shard_map/ppermute | solution.py:93

commit v12 on v8

--- a/solution.py
+++ b/solution.py
@@ -9,7 +9,8 @@
 F = 81920
 BALANCE_ROUNDS = 3
 Y, Z, X, C = 8, 8, 4, 2
-WIDE = ("y", "z")
+NEAR, FAR = ("y_near", "z_near"), ("y_far", "z_far")
+WIDE = (*NEAR, *FAR)
 NARROW = ("x", "c")
 SWAP = [(0, 1), (1, 0)]
 SEND_SCALE = 64.0
@@ -53,7 +54,8 @@
     arrived = lax.all_to_all(partial, WIDE, 0, 0)
     scores = jnp.sum(arrived.astype(jnp.float32), axis=0) * (1.0 / SEND_SCALE)
     block = jnp.concatenate([scores[0], scores[1]], axis=1)
-    own = lax.optimization_barrier(gather_by_a2a(jnp.exp(block).astype(jnp.bfloat16), WIDE, Y * Z))
+    own = gather_by_a2a(jnp.exp(block).astype(jnp.bfloat16), FAR, Y * Z // 4)
+    own = lax.optimization_barrier(gather_by_a2a(own, NEAR, 4))
     theirs, minus_noise = lax.optimization_barrier((lax.ppermute(own, "c", SWAP), -noise))
 
     def flip(vector):
@@ -87,6 +89,7 @@
 
 
 def solution(mesh):
-    mesh = Mesh(mesh.devices.reshape(Y, Z, X, C), (*WIDE, *NARROW))
-    spec = P(NARROW, WIDE)
+    axes = ("y_far", "y_near", "z_far", "z_near")
+    mesh = Mesh(mesh.devices.reshape(Y // 2, 2, Z // 2, 2, X, C), (*axes, *NARROW))
+    spec = P(NARROW, axes)
     return jax.shard_map(body, mesh=mesh, in_specs=(spec, spec), out_specs=spec, check_vma=False)

time: 148 us -> 147 us (level)
  the two profiles are of different devices: /device:TPU:16 before, /device:TPU:8 now
where the time goes in v12:
time: 147 us
  blocking collectives  110 us (75%)
  waiting for transfers between devices  18 us (12%)
  starting transfers between devices  8.24 us (6%)
  other arithmetic  4.7 us (3%)
  matrix products  3.42 us (2%)
  local copies, waits for them, and re-layouts  2.24 us (2%)
    all_to_all x1, blocking collectives, body(): arrived = lax.all_to_all(partial, WIDE, 0, 0)  40 us
    all_to_all x2, blocking collectives, gather_by_a2a(): lax.all_to_all(jnp.broadcast_to(block[None], (n, *block.shape)), axes, 0, 0)  28.5 us
    all_to_all x3, blocking collectives, sum_over_x(): lax.all_to_all(jnp.broadcast_to(send, (X, *send.shape[1:])), 'x', 0, 0)  23.1 us
    all_to_all x1, blocking collectives, body(): parts = jnp.sum(lax.all_to_all(send, 'x', 0, 0).astype(jnp.float32), axis=0)  18.3 us
    all_to_all x1, waiting for transfers between devices, gather_by_a2a(): lax.all_to_all(jnp.broadcast_to(block[None], (n, *block.shape)), axes, 0, 0)  16 us
    all_to_all x1, starting transfers between devices, gather_by_a2a(): lax.all_to_all(jnp.broadcast_to(block[None], (n, *block.shape)), axes, 0, 0)  4.42 us
  transfers between devices with their start and end apart: 3, of which 2 were waited for; matrix products, arithmetic and copies ran while one was open for 1% of the time, Pallas kernels for 0%

profile of v12, /device:TPU:8, one launch (start us, length us, event | category | flops | bytes accessed | tf_op | source)
XLA Modules:
  0.0 146.9 jit_solution(2681247805373800955)
XLA Ops:
  0.0 2.1 %broadcast_in_dim.20 = bf16[4,128,1280]{2,1,0:T(8,128)(2,1)} broadcast(bf16[128,1280]{1,0:T(8,128)(2,1)} %param.2), dimensions={1,2} | broadcast | bytes 1638400 | tf_op jit(solution)/shard_map/broadcast_in_dim | solution.py:22
  2.1 0.0 copy-start.1
  2.1 4.4 %all-to-all-start = ((bf16[4,128,1280]{2,1,0:T(8,128)(2,1)}), bf16[4,128,1280]{2,1,0:T(8,128)(2,1)S(1)}, u32[]{:S(2)}, u32[]{:S(2)}) async-start(bf16[4,128,1280]{2,1,0:T(8,128)(2,1)} %broadcast_in_dim.20), calls=%async_computation | async-start | bytes 2621440 | tf_op jit(solution)/shard_map/all_to_all | solution.py:22
  6.5 0.0 copy-done.1
  6.5 1.9 %collective-permute-start = (bf16[384,1280]{1,0:T(8,128)(2,1)S(1)}, bf16[384,1280]{1,0:T(8,128)(2,1)S(1)}, u32[]{:S(2)}, u32[]{:S(2)}) collective-permute-start(bf16[384,1280]{1,0:T(8,128)(2,1)S(1)} %copy-done.1), channel_id=1, source_target_pairs={{0,1},{1,0},{2,3},{3,2},{4,5},{5,4},{6,7},{7,6},{8,9},{9,8},{10,11... | collective-permute-start | bytes 2949128 | tf_op jit(solution)/shard_map/ppermute | solution.py:46
  8.5 16.0 %all-to-all-done = bf16[4,128,1280]{2,1,0:T(8,128)(2,1)S(1)} async-done(((bf16[4,128,1280]{2,1,0:T(8,128)(2,1)}), bf16[4,128,1280]{2,1,0:T(8,128)(2,1)S(1)}, u32[]{:S(2)}, u32[]{:S(2)}) %all-to-all-start) | async-done | bytes 1310752 | tf_op jit(solution)/shard_map/all_to_all | solution.py:22
  24.5 0.9 fusion.18
  25.3 0.0 collective-permute-done
  25.3 0.9 fusion.17
  26.2 0.2 pad_maximum_fusion.1
  26.4 40.0 %all_to_all.40 = f16[64,2,8,384]{3,2,1,0:T(8,128)(2,1)S(1)} all-to-all(f16[64,2,8,384]{3,2,1,0:T(8,128)(2,1)S(1)} %pad_maximum_fusion.1), channel_id=1, replica_groups=mesh['y_far'=4,'y_near'=2,'z_far'=4,'z_near'=2,'x'=4,'c'=2] {'y_near','z..., dimensions={0} | all-to-all | bytes 1572864 | tf_op jit(solution)/shard_map/all_to_all | solution.py:54
  66.5 0.1 convert_reduce_fusion.2
  66.6 0.0 copy-start
  66.7 16.9 %all_to_all.41 = bf16[16,8,768]{2,1,0:T(8,128)(2,1)S(1)} all-to-all(bf16[16,8,768]{2,1,0:T(8,128)(2,1)S(1)} %broadcast_in_dim.21), channel_id=1, replica_groups=mesh['y_far'=4,'y_near'=2,'z_far'=4,'z_near'=2,'x'=4,'c'=2] {'y_far','z_..., dimensions={0} | all-to-all | bytes 393216 | tf_op jit(solution)/shard_map/all_to_all | solution.py:22
  83.5 0.1 broadcast_in_dim.23
  83.6 11.6 %all_to_all.42 = bf16[4,128,768]{2,1,0:T(8,128)(2,1)S(1)} all-to-all(bf16[4,128,768]{2,1,0:T(8,128)(2,1)S(1)} %broadcast_in_dim.23), channel_id=1, replica_groups=mesh['y_far'=4,'y_near'=2,'z_far'=4,'z_near'=2,'x'=4,'c'=2] {'y_near','z..., dimensions={0} | all-to-all | bytes 1572864 | tf_op jit(solution)/shard_map/all_to_all | solution.py:22
  95.2 1.9 %collective-permute-start.1 = (bf16[512,768]{1,0:T(8,128)(2,1)S(1)}, bf16[512,768]{1,0:T(8,128)(2,1)S(1)}, u32[]{:S(2)}, u32[]{:S(2)}) collective-permute-start(bf16[512,768]{1,0:T(8,128)(2,1)S(1)} %bitcast.50), channel_id=1, source_target_pairs={{0,1},{1,0},{2,3},{3,2},{4,5},{5,4},{6,7},{7,6},{8,9},{9,8},{10,11... | collective-permute-start | bytes 2359304 | tf_op jit(solution)/shard_map/ppermute | solution.py:59
  97.1 0.0 copy-done
  97.1 0.1 neg.3
  97.2 0.2 convert_reduce_fusion
  97.4 2.0 %collective-permute-done.1 = bf16[512,768]{1,0:T(8,128)(2,1)S(1)} collective-permute-done((bf16[512,768]{1,0:T(8,128)(2,1)S(1)}, bf16[512,768]{1,0:T(8,128)(2,1)S(1)}, u32[]{:S(2)}, u32[]{:S(2)}) %collective-permute-start.1) | collective-permute-done | bytes 786464 | tf_op jit(solution)/shard_map/ppermute | solution.py:59
  99.4 0.2 fusion.1
  99.6 7.7 %all_to_all.43 = f32[4,8,128]{2,1,0:T(8,128)S(1)} all-to-all(f32[4,8,128]{2,1,0:T(8,128)S(1)} %broadcast_in_dim.25), channel_id=1, replica_groups=mesh['y_far'=4,'y_near'=2,'z_far'=4,'z_near'=2,'x'=4,'c'=2] {'x'}, dimensions={0} | all-to-all | bytes 32768 | tf_op jit(solution)/shard_map/all_to_all | solution.py:30
  107.3 0.4 fusion.2
  107.8 0.2 fusion.8
  108.0 0.2 fusion.3
  108.3 7.7 %all_to_all.44 = f32[4,8,128]{2,1,0:T(8,128)S(1)} all-to-all(f32[4,8,128]{2,1,0:T(8,128)S(1)} %broadcast_in_dim.27), channel_id=1, replica_groups=mesh['y_far'=4,'y_near'=2,'z_far'=4,'z_near'=2,'x'=4,'c'=2] {'x'}, dimensions={0} | all-to-all | bytes 32768 | tf_op jit(solution)/shard_map/all_to_all | solution.py:30
  116.0 0.2 fusion.4
  116.3 0.2 fusion.9
  116.5 0.2 fusion.10
  116.8 0.2 fusion.5
  117.0 7.7 %all_to_all.45 = f32[4,8,128]{2,1,0:T(8,128)S(1)} all-to-all(f32[4,8,128]{2,1,0:T(8,128)S(1)} %broadcast_in_dim.29), channel_id=1, replica_groups=mesh['y_far'=4,'y_near'=2,'z_far'=4,'z_near'=2,'x'=4,'c'=2] {'x'}, dimensions={0} | all-to-all | bytes 32768 | tf_op jit(solution)/shard_map/all_to_all | solution.py:30
  124.8 0.2 fusion.6
  125.0 0.2 fusion.11
  125.3 0.3 fusion.14
  125.6 0.8 fusion.22
  126.5 0.8 fusion
  127.3 0.1 pad_maximum_fusion
  127.4 18.3 %all_to_all.46 = bf16[4,136,1280]{2,1,0:T(8,128)(2,1)S(1)} all-to-all(bf16[4,136,1280]{2,1,0:T(8,128)(2,1)S(1)} %pad_maximum_fusion), channel_id=1, replica_groups=mesh['y_far'=4,'y_near'=2,'z_far'=4,'z_near'=2,'x'=4,'c'=2] {'x'}, dimensions={0} | all-to-all | bytes 2785280 | tf_op jit(solution)/shard_map/all_to_all | solution.py:86
  145.8 0.2 convert_reduce_fusion.1
  146.0 0.9 fusion.20
  (32 shorter events, 0.2 us)
Async XLA Ops:
  2.1 4.4 %copy-start.1 = (bf16[384,1280]{1,0:T(8,128)(2,1)S(1)}, bf16[384,1280]{1,0:T(8,128)(2,1)}, u32[]{:S(2)}) copy-start(bf16[384,1280]{1,0:T(8,128)(2,1)} %param.3) | copy-start | bytes 2949124
  2.1 22.3 %all-to-all-start = ((bf16[4,128,1280]{2,1,0:T(8,128)(2,1)}), bf16[4,128,1280]{2,1,0:T(8,128)(2,1)S(1)}, u32[]{:S(2)}, u32[]{:S(2)}) async-start(bf16[4,128,1280]{2,1,0:T(8,128)(2,1)} %broadcast_in_dim.20), calls=%async_computation | async-start | bytes 2621440 | tf_op jit(solution)/shard_map/all_to_all | solution.py:22
  6.5 18.8 %collective-permute-start = (bf16[384,1280]{1,0:T(8,128)(2,1)S(1)}, bf16[384,1280]{1,0:T(8,128)(2,1)S(1)}, u32[]{:S(2)}, u32[]{:S(2)}) collective-permute-start(bf16[384,1280]{1,0:T(8,128)(2,1)S(1)} %copy-done.1), channel_id=1, source_target_pairs={{0,1},{1,0},{2,3},{3,2},{4,5},{5,4},{6,7},{7,6},{8,9},{9,8},{10,11... | collective-permute-start | bytes 2949128 | tf_op jit(solution)/shard_map/ppermute | solution.py:46
  66.6 30.5 %copy-start = (bf16[128,1280]{1,0:T(8,128)(2,1)S(1)}, bf16[128,1280]{1,0:T(8,128)(2,1)}, u32[]{:S(2)}) copy-start(bf16[128,1280]{1,0:T(8,128)(2,1)} %param.2) | copy-start | bytes 983044
  95.2 4.2 %collective-permute-start.1 = (bf16[512,768]{1,0:T(8,128)(2,1)S(1)}, bf16[512,768]{1,0:T(8,128)(2,1)S(1)}, u32[]{:S(2)}, u32[]{:S(2)}) collective-permute-start(bf16[512,768]{1,0:T(8,128)(2,1)S(1)} %bitcast.50), channel_id=1, source_target_pairs={{0,1},{1,0},{2,3},{3,2},{4,5},{5,4},{6,7},{7,6},{8,9},{9,8},{10,11... | collective-permute-start | bytes 2359304 | tf_op jit(solution)/shard_map/ppermute | solution.py:59

commit v13 on v12

--- a/solution.py
+++ b/solution.py
@@ -10,7 +10,7 @@
 BALANCE_ROUNDS = 3
 Y, Z, X, C = 8, 8, 4, 2
 NEAR, FAR = ("y_near", "z_near"), ("y_far", "z_far")
-WIDE = (*NEAR, *FAR)
+WIDE = ("y_far", "y_near", "z_far", "z_near")
 NARROW = ("x", "c")
 SWAP = [(0, 1), (1, 0)]
 SEND_SCALE = 64.0
@@ -51,6 +51,8 @@
         return (scores * (SEND_SCALE / math.sqrt(F))).astype(jnp.float16).reshape(Y * Z, 1, rows // (Y * Z), -1)
 
     partial = jnp.concatenate([partial_scores(latents), partial_scores(other)], axis=1)
+    shape = partial.shape
+    partial = partial.reshape(2, 2, Y // 2, Z // 2, *shape[1:]).transpose(2, 0, 3, 1, 4, 5, 6).reshape(shape)
     arrived = lax.all_to_all(partial, WIDE, 0, 0)
     scores = jnp.sum(arrived.astype(jnp.float32), axis=0) * (1.0 / SEND_SCALE)
     block = jnp.concatenate([scores[0], scores[1]], axis=1)
@@ -89,7 +91,6 @@
 
 
 def solution(mesh):
-    axes = ("y_far", "y_near", "z_far", "z_near")
-    mesh = Mesh(mesh.devices.reshape(Y // 2, 2, Z // 2, 2, X, C), (*axes, *NARROW))
-    spec = P(NARROW, axes)
+    mesh = Mesh(mesh.devices.reshape(Y // 2, 2, Z // 2, 2, X, C), (*WIDE, *NARROW))
+    spec = P(NARROW, WIDE)
     return jax.shard_map(body, mesh=mesh, in_specs=(spec, spec), out_specs=spec, check_vma=False)

time: 147 us -> 147 us (level)
  no operation moved by 1% of the time
where the time goes in v13:
time: 147 us
  blocking collectives  110 us (75%)
  waiting for transfers between devices  18 us (12%)
  starting transfers between devices  8.24 us (6%)
  other arithmetic  4.69 us (3%)
  matrix products  3.42 us (2%)
  local copies, waits for them, and re-layouts  2.4 us (2%)
    all_to_all x1, blocking collectives, body(): arrived = lax.all_to_all(partial, WIDE, 0, 0)  39 us
    all_to_all x2, blocking collectives, gather_by_a2a(): lax.all_to_all(jnp.broadcast_to(block[None], (n, *block.shape)), axes, 0, 0)  29.4 us
    all_to_all x3, blocking collectives, sum_over_x(): lax.all_to_all(jnp.broadcast_to(send, (X, *send.shape[1:])), 'x', 0, 0)  23.1 us
    all_to_all x1, blocking collectives, body(): parts = jnp.sum(lax.all_to_all(send, 'x', 0, 0).astype(jnp.float32), axis=0)  18.3 us
    all_to_all x1, waiting for transfers between devices, gather_by_a2a(): lax.all_to_all(jnp.broadcast_to(block[None], (n, *block.shape)), axes, 0, 0)  16 us
    all_to_all x1, starting transfers between devices, gather_by_a2a(): lax.all_to_all(jnp.broadcast_to(block[None], (n, *block.shape)), axes, 0, 0)  4.42 us
  transfers between devices with their start and end apart: 3, of which 2 were waited for; matrix products, arithmetic and copies ran while one was open for 1% of the time, Pallas kernels for 0%

profile of v13, /device:TPU:8, one launch (start us, length us, event | category | flops | bytes accessed | tf_op | source)
XLA Modules:
  0.0 147.0 jit_solution(9158164082266422705)
XLA Ops:
  0.0 2.1 %broadcast_in_dim.20 = bf16[4,128,1280]{2,1,0:T(8,128)(2,1)} broadcast(bf16[128,1280]{1,0:T(8,128)(2,1)} %param.2), dimensions={1,2} | broadcast | bytes 1638400 | tf_op jit(solution)/shard_map/broadcast_in_dim | solution.py:22
  2.1 0.0 copy-start.1
  2.1 4.4 %all-to-all-start = ((bf16[4,128,1280]{2,1,0:T(8,128)(2,1)}), bf16[4,128,1280]{2,1,0:T(8,128)(2,1)S(1)}, u32[]{:S(2)}, u32[]{:S(2)}) async-start(bf16[4,128,1280]{2,1,0:T(8,128)(2,1)} %broadcast_in_dim.20), calls=%async_computation | async-start | bytes 2621440 | tf_op jit(solution)/shard_map/all_to_all | solution.py:22
  6.5 0.0 copy-done.1
  6.5 1.9 %collective-permute-start = (bf16[384,1280]{1,0:T(8,128)(2,1)S(1)}, bf16[384,1280]{1,0:T(8,128)(2,1)S(1)}, u32[]{:S(2)}, u32[]{:S(2)}) collective-permute-start(bf16[384,1280]{1,0:T(8,128)(2,1)S(1)} %copy-done.1), channel_id=1, source_target_pairs={{0,1},{1,0},{2,3},{3,2},{4,5},{5,4},{6,7},{7,6},{8,9},{9,8},{10,11... | collective-permute-start | bytes 2949128 | tf_op jit(solution)/shard_map/ppermute | solution.py:46
  8.5 16.0 %all-to-all-done = bf16[4,128,1280]{2,1,0:T(8,128)(2,1)S(1)} async-done(((bf16[4,128,1280]{2,1,0:T(8,128)(2,1)}), bf16[4,128,1280]{2,1,0:T(8,128)(2,1)S(1)}, u32[]{:S(2)}, u32[]{:S(2)}) %all-to-all-start) | async-done | bytes 1310752 | tf_op jit(solution)/shard_map/all_to_all | solution.py:22
  24.5 0.9 fusion.15
  25.3 0.0 collective-permute-done
  25.3 0.9 fusion.16
  26.2 0.2 pad_maximum_fusion.1
  26.4 0.2 copy.7
  26.6 39.0 %all_to_all.40 = f16[64,2,8,384]{3,2,1,0:T(8,128)(2,1)S(1)} all-to-all(f16[64,2,8,384]{3,2,1,0:T(8,128)(2,1)S(1)} %bitcast.56), channel_id=1, replica_groups=mesh['y_far'=4,'y_near'=2,'z_far'=4,'z_near'=2,'x'=4,'c'=2] {'y_far','y_..., dimensions={0} | all-to-all | bytes 1572864 | tf_op jit(solution)/shard_map/all_to_all | solution.py:56
  65.6 0.1 convert_reduce_fusion.2
  65.8 0.0 copy-start
  65.8 17.9 %all_to_all.41 = bf16[16,8,768]{2,1,0:T(8,128)(2,1)S(1)} all-to-all(bf16[16,8,768]{2,1,0:T(8,128)(2,1)S(1)} %broadcast_in_dim.21), channel_id=1, replica_groups=mesh['y_far'=4,'y_near'=2,'z_far'=4,'z_near'=2,'x'=4,'c'=2] {'y_far','z_..., dimensions={0} | all-to-all | bytes 393216 | tf_op jit(solution)/shard_map/all_to_all | solution.py:22
  83.8 0.1 broadcast_in_dim.23
  83.8 11.5 %all_to_all.42 = bf16[4,128,768]{2,1,0:T(8,128)(2,1)S(1)} all-to-all(bf16[4,128,768]{2,1,0:T(8,128)(2,1)S(1)} %broadcast_in_dim.23), channel_id=1, replica_groups=mesh['y_far'=4,'y_near'=2,'z_far'=4,'z_near'=2,'x'=4,'c'=2] {'y_near','z..., dimensions={0} | all-to-all | bytes 1572864 | tf_op jit(solution)/shard_map/all_to_all | solution.py:22
  95.3 1.9 %collective-permute-start.1 = (bf16[512,768]{1,0:T(8,128)(2,1)S(1)}, bf16[512,768]{1,0:T(8,128)(2,1)S(1)}, u32[]{:S(2)}, u32[]{:S(2)}) collective-permute-start(bf16[512,768]{1,0:T(8,128)(2,1)S(1)} %bitcast.47), channel_id=1, source_target_pairs={{0,1},{1,0},{2,3},{3,2},{4,5},{5,4},{6,7},{7,6},{8,9},{9,8},{10,11... | collective-permute-start | bytes 2359304 | tf_op jit(solution)/shard_map/ppermute | solution.py:61
  97.2 0.0 copy-done
  97.2 0.1 neg.3
  97.3 0.2 convert_reduce_fusion
  97.5 2.0 %collective-permute-done.1 = bf16[512,768]{1,0:T(8,128)(2,1)S(1)} collective-permute-done((bf16[512,768]{1,0:T(8,128)(2,1)S(1)}, bf16[512,768]{1,0:T(8,128)(2,1)S(1)}, u32[]{:S(2)}, u32[]{:S(2)}) %collective-permute-start.1) | collective-permute-done | bytes 786464 | tf_op jit(solution)/shard_map/ppermute | solution.py:61
  99.5 0.2 fusion.1
  99.7 7.7 %all_to_all.43 = f32[4,8,128]{2,1,0:T(8,128)S(1)} all-to-all(f32[4,8,128]{2,1,0:T(8,128)S(1)} %broadcast_in_dim.25), channel_id=1, replica_groups=mesh['y_far'=4,'y_near'=2,'z_far'=4,'z_near'=2,'x'=4,'c'=2] {'x'}, dimensions={0} | all-to-all | bytes 32768 | tf_op jit(solution)/shard_map/all_to_all | solution.py:30
  107.5 0.4 fusion.2
  107.9 0.2 fusion.8
  108.2 0.2 fusion.3
  108.4 7.7 %all_to_all.44 = f32[4,8,128]{2,1,0:T(8,128)S(1)} all-to-all(f32[4,8,128]{2,1,0:T(8,128)S(1)} %broadcast_in_dim.27), channel_id=1, replica_groups=mesh['y_far'=4,'y_near'=2,'z_far'=4,'z_near'=2,'x'=4,'c'=2] {'x'}, dimensions={0} | all-to-all | bytes 32768 | tf_op jit(solution)/shard_map/all_to_all | solution.py:30
  116.1 0.2 fusion.4
  116.4 0.2 fusion.9
  116.6 0.2 fusion.10
  116.9 0.2 fusion.5
  117.1 7.7 %all_to_all.45 = f32[4,8,128]{2,1,0:T(8,128)S(1)} all-to-all(f32[4,8,128]{2,1,0:T(8,128)S(1)} %broadcast_in_dim.29), channel_id=1, replica_groups=mesh['y_far'=4,'y_near'=2,'z_far'=4,'z_near'=2,'x'=4,'c'=2] {'x'}, dimensions={0} | all-to-all | bytes 32768 | tf_op jit(solution)/shard_map/all_to_all | solution.py:30
  124.9 0.2 fusion.6
  125.1 0.2 fusion.11
  125.4 0.3 fusion.14
  125.7 0.8 fusion.20
  126.6 0.8 fusion
  127.4 0.1 pad_maximum_fusion
  127.5 18.3 %all_to_all.46 = bf16[4,136,1280]{2,1,0:T(8,128)(2,1)S(1)} all-to-all(bf16[4,136,1280]{2,1,0:T(8,128)(2,1)S(1)} %pad_maximum_fusion), channel_id=1, replica_groups=mesh['y_far'=4,'y_near'=2,'z_far'=4,'z_near'=2,'x'=4,'c'=2] {'x'}, dimensions={0} | all-to-all | bytes 2785280 | tf_op jit(solution)/shard_map/all_to_all | solution.py:88
  145.9 0.2 convert_reduce_fusion.1
  146.1 0.9 fusion.18
  (32 shorter events, 0.2 us)
Async XLA Ops:
  2.1 4.4 %copy-start.1 = (bf16[384,1280]{1,0:T(8,128)(2,1)S(1)}, bf16[384,1280]{1,0:T(8,128)(2,1)}, u32[]{:S(2)}) copy-start(bf16[384,1280]{1,0:T(8,128)(2,1)} %param.3) | copy-start | bytes 2949124
  2.1 22.3 %all-to-all-start = ((bf16[4,128,1280]{2,1,0:T(8,128)(2,1)}), bf16[4,128,1280]{2,1,0:T(8,128)(2,1)S(1)}, u32[]{:S(2)}, u32[]{:S(2)}) async-start(bf16[4,128,1280]{2,1,0:T(8,128)(2,1)} %broadcast_in_dim.20), calls=%async_computation | async-start | bytes 2621440 | tf_op jit(solution)/shard_map/all_to_all | solution.py:22
  6.5 18.8 %collective-permute-start = (bf16[384,1280]{1,0:T(8,128)(2,1)S(1)}, bf16[384,1280]{1,0:T(8,128)(2,1)S(1)}, u32[]{:S(2)}, u32[]{:S(2)}) collective-permute-start(bf16[384,1280]{1,0:T(8,128)(2,1)S(1)} %copy-done.1), channel_id=1, source_target_pairs={{0,1},{1,0},{2,3},{3,2},{4,5},{5,4},{6,7},{7,6},{8,9},{9,8},{10,11... | collective-permute-start | bytes 2949128 | tf_op jit(solution)/shard_map/ppermute | solution.py:46
  65.8 31.4 %copy-start = (bf16[128,1280]{1,0:T(8,128)(2,1)S(1)}, bf16[128,1280]{1,0:T(8,128)(2,1)}, u32[]{:S(2)}) copy-start(bf16[128,1280]{1,0:T(8,128)(2,1)} %param.2) | copy-start | bytes 983044
  95.3 4.2 %collective-permute-start.1 = (bf16[512,768]{1,0:T(8,128)(2,1)S(1)}, bf16[512,768]{1,0:T(8,128)(2,1)S(1)}, u32[]{:S(2)}, u32[]{:S(2)}) collective-permute-start(bf16[512,768]{1,0:T(8,128)(2,1)S(1)} %bitcast.47), channel_id=1, source_target_pairs={{0,1},{1,0},{2,3},{3,2},{4,5},{5,4},{6,7},{7,6},{8,9},{9,8},{10,11... | collective-permute-start | bytes 2359304 | tf_op jit(solution)/shard_map/ppermute | solution.py:61

commit v14 on v8

--- a/solution.py
+++ b/solution.py
@@ -81,9 +81,10 @@
     partial_target = jnp.dot(weights[:, : clips // 2], latents, preferred_element_type=jnp.float32)
     partial_target += jnp.dot(weights[:, clips // 2 :], other, preferred_element_type=jnp.float32)
     send = jnp.concatenate([partial_target.astype(jnp.bfloat16).reshape(X, draws, features), totals], axis=1)
-    parts = jnp.sum(lax.all_to_all(send, "x", 0, 0).astype(jnp.float32), axis=0)
-    own_total = parts[draws, :draws] + parts[draws + 1, :draws]
-    return (parts[:draws] / own_total[:, None] + minus_noise.astype(jnp.float32)).astype(jnp.bfloat16)
+    got = lax.all_to_all(send, "x", 0, 0).astype(jnp.float32)
+    parts = (got[0, :draws] + got[1, :draws]) + (got[2, :draws] + got[3, :draws])
+    own_total = jnp.sum(got[:, draws : draws + 2, :draws], axis=(0, 1))
+    return (parts / own_total[:, None] + minus_noise.astype(jnp.float32)).astype(jnp.bfloat16)
 
 
 def solution(mesh):

time: 148 us -> 148 us (level)
  no operation moved by 1% of the time
where the time goes in v14:
time: 148 us; the launch traced here: 147 us
  blocking collectives  110 us (74%)
  waiting for transfers between devices  18 us (12%)
  starting transfers between devices  8.24 us (6%)
  other arithmetic  4.76 us (3%)
  matrix products  3.41 us (2%)
  local copies, waits for them, and re-layouts  2.22 us (2%)
    all_to_all x1, blocking collectives, body(): arrived = lax.all_to_all(partial, WIDE, 0, 0)  40.1 us
    all_to_all x1, blocking collectives, gather_by_a2a(): lax.all_to_all(jnp.broadcast_to(block[None], (n, *block.shape)), axes, 0, 0)  28.8 us
    all_to_all x3, blocking collectives, sum_over_x(): lax.all_to_all(jnp.broadcast_to(send, (X, *send.shape[1:])), 'x', 0, 0)  23.1 us
    all_to_all x1, blocking collectives, body(): got = lax.all_to_all(send, 'x', 0, 0).astype(jnp.float32)  18.3 us
    all_to_all x1, waiting for transfers between devices, gather_by_a2a(): lax.all_to_all(jnp.broadcast_to(block[None], (n, *block.shape)), axes, 0, 0)  16 us
    all_to_all x1, starting transfers between devices, gather_by_a2a(): lax.all_to_all(jnp.broadcast_to(block[None], (n, *block.shape)), axes, 0, 0)  4.42 us
  transfers between devices with their start and end apart: 3, of which 2 were waited for; matrix products, arithmetic and copies ran while one was open for 1% of the time, Pallas kernels for 0%

profile of v14, /device:TPU:16, one launch (start us, length us, event | category | flops | bytes accessed | tf_op | source)
XLA Modules:
  0.0 147.3 jit_solution(5802073511225613484)
XLA Ops:
  0.0 2.1 %broadcast_in_dim.16 = bf16[4,128,1280]{2,1,0:T(8,128)(2,1)} broadcast(bf16[128,1280]{1,0:T(8,128)(2,1)} %param.2), dimensions={1,2} | broadcast | bytes 1638400 | tf_op jit(solution)/shard_map/broadcast_in_dim | solution.py:21
  2.1 0.0 copy-start.1
  2.1 4.4 %all-to-all-start = ((bf16[4,128,1280]{2,1,0:T(8,128)(2,1)}), bf16[4,128,1280]{2,1,0:T(8,128)(2,1)S(1)}, u32[]{:S(2)}, u32[]{:S(2)}) async-start(bf16[4,128,1280]{2,1,0:T(8,128)(2,1)} %broadcast_in_dim.16), calls=%async_computation | async-start | bytes 2621440 | tf_op jit(solution)/shard_map/all_to_all | solution.py:21
  6.5 0.0 copy-done.1
  6.5 1.9 %collective-permute-start = (bf16[384,1280]{1,0:T(8,128)(2,1)S(1)}, bf16[384,1280]{1,0:T(8,128)(2,1)S(1)}, u32[]{:S(2)}, u32[]{:S(2)}) collective-permute-start(bf16[384,1280]{1,0:T(8,128)(2,1)S(1)} %copy-done.1), channel_id=1, source_target_pairs={{0,1},{1,0},{2,3},{3,2},{4,5},{5,4},{6,7},{7,6},{8,9},{9,8},{10,11... | collective-permute-start | bytes 2949128 | tf_op jit(solution)/shard_map/ppermute | solution.py:45
  8.5 16.0 %all-to-all-done = bf16[4,128,1280]{2,1,0:T(8,128)(2,1)S(1)} async-done(((bf16[4,128,1280]{2,1,0:T(8,128)(2,1)}), bf16[4,128,1280]{2,1,0:T(8,128)(2,1)S(1)}, u32[]{:S(2)}, u32[]{:S(2)}) %all-to-all-start) | async-done | bytes 1310752 | tf_op jit(solution)/shard_map/all_to_all | solution.py:21
  24.5 0.9 fusion.18
  25.3 0.0 collective-permute-done
  25.3 0.9 fusion.17
  26.2 0.2 pad_maximum_fusion.1
  26.4 40.1 %all_to_all.35 = f16[64,2,8,384]{3,2,1,0:T(8,128)(2,1)S(1)} all-to-all(f16[64,2,8,384]{3,2,1,0:T(8,128)(2,1)S(1)} %pad_maximum_fusion.1), channel_id=1, replica_groups=mesh['y'=8,'z'=8,'x'=4,'c'=2] {'y','z'}, dimensions={0} | all-to-all | bytes 1572864 | tf_op jit(solution)/shard_map/all_to_all | solution.py:53
  66.5 0.0 copy-start
  66.5 0.1 convert_reduce_fusion.1
  66.6 0.1 broadcast_in_dim.17
  66.7 28.8 %all_to_all.36 = bf16[64,8,768]{2,1,0:T(8,128)(2,1)S(1)} all-to-all(bf16[64,8,768]{2,1,0:T(8,128)(2,1)S(1)} %broadcast_in_dim.17), channel_id=1, replica_groups=mesh['y'=8,'z'=8,'x'=4,'c'=2] {'y','z'}, dimensions={0} | all-to-all | bytes 1572864 | tf_op jit(solution)/shard_map/all_to_all | solution.py:21
  95.5 1.9 %collective-permute-start.1 = (bf16[512,768]{1,0:T(8,128)(2,1)S(1)}, bf16[512,768]{1,0:T(8,128)(2,1)S(1)}, u32[]{:S(2)}, u32[]{:S(2)}) collective-permute-start(bf16[512,768]{1,0:T(8,128)(2,1)S(1)} %bitcast.55), channel_id=1, source_target_pairs={{0,1},{1,0},{2,3},{3,2},{4,5},{5,4},{6,7},{7,6},{8,9},{9,8},{10,11... | collective-permute-start | bytes 2359304 | tf_op jit(solution)/shard_map/ppermute | solution.py:57
  97.4 0.0 copy-done
  97.5 0.1 neg.3
  97.5 0.2 convert_reduce_fusion
  97.7 2.0 %collective-permute-done.1 = bf16[512,768]{1,0:T(8,128)(2,1)S(1)} collective-permute-done((bf16[512,768]{1,0:T(8,128)(2,1)S(1)}, bf16[512,768]{1,0:T(8,128)(2,1)S(1)}, u32[]{:S(2)}, u32[]{:S(2)}) %collective-permute-start.1) | collective-permute-done | bytes 786464 | tf_op jit(solution)/shard_map/ppermute | solution.py:57
  99.7 0.2 fusion.1
  100.0 7.7 %all_to_all.37 = f32[4,8,128]{2,1,0:T(8,128)S(1)} all-to-all(f32[4,8,128]{2,1,0:T(8,128)S(1)} %broadcast_in_dim.19), channel_id=1, replica_groups=mesh['y'=8,'z'=8,'x'=4,'c'=2] {'x'}, dimensions={0} | all-to-all | bytes 32768 | tf_op jit(solution)/shard_map/all_to_all | solution.py:29
  107.7 0.4 fusion.2
  108.1 0.2 fusion.8
  108.4 0.2 fusion.3
  108.6 7.7 %all_to_all.38 = f32[4,8,128]{2,1,0:T(8,128)S(1)} all-to-all(f32[4,8,128]{2,1,0:T(8,128)S(1)} %broadcast_in_dim.21), channel_id=1, replica_groups=mesh['y'=8,'z'=8,'x'=4,'c'=2] {'x'}, dimensions={0} | all-to-all | bytes 32768 | tf_op jit(solution)/shard_map/all_to_all | solution.py:29
  116.3 0.2 fusion.4
  116.6 0.2 fusion.9
  116.8 0.2 fusion.10
  117.1 0.2 fusion.5
  117.4 7.7 %all_to_all.39 = f32[4,8,128]{2,1,0:T(8,128)S(1)} all-to-all(f32[4,8,128]{2,1,0:T(8,128)S(1)} %broadcast_in_dim.23), channel_id=1, replica_groups=mesh['y'=8,'z'=8,'x'=4,'c'=2] {'x'}, dimensions={0} | all-to-all | bytes 32768 | tf_op jit(solution)/shard_map/all_to_all | solution.py:29
  125.1 0.2 fusion.6
  125.3 0.2 fusion.11
  125.6 0.3 fusion.14
  125.9 0.8 fusion.25
  126.8 0.8 fusion
  127.7 0.1 pad_maximum_fusion
  127.8 18.3 %all_to_all.40 = bf16[4,136,1280]{2,1,0:T(8,128)(2,1)S(1)} all-to-all(bf16[4,136,1280]{2,1,0:T(8,128)(2,1)S(1)} %pad_maximum_fusion), channel_id=1, replica_groups=mesh['y'=8,'z'=8,'x'=4,'c'=2] {'x'}, dimensions={0} | all-to-all | bytes 2785280 | tf_op jit(solution)/shard_map/all_to_all | solution.py:84
  146.1 0.2 convert_element_type.59
  146.3 0.9 fusion.23
  (31 shorter events, 0.2 us)
Async XLA Ops:
  2.1 4.4 %copy-start.1 = (bf16[384,1280]{1,0:T(8,128)(2,1)S(1)}, bf16[384,1280]{1,0:T(8,128)(2,1)}, u32[]{:S(2)}) copy-start(bf16[384,1280]{1,0:T(8,128)(2,1)} %param.3) | copy-start | bytes 2949124
  2.1 22.3 %all-to-all-start = ((bf16[4,128,1280]{2,1,0:T(8,128)(2,1)}), bf16[4,128,1280]{2,1,0:T(8,128)(2,1)S(1)}, u32[]{:S(2)}, u32[]{:S(2)}) async-start(bf16[4,128,1280]{2,1,0:T(8,128)(2,1)} %broadcast_in_dim.16), calls=%async_computation | async-start | bytes 2621440 | tf_op jit(solution)/shard_map/all_to_all | solution.py:21
  6.5 18.8 %collective-permute-start = (bf16[384,1280]{1,0:T(8,128)(2,1)S(1)}, bf16[384,1280]{1,0:T(8,128)(2,1)S(1)}, u32[]{:S(2)}, u32[]{:S(2)}) collective-permute-start(bf16[384,1280]{1,0:T(8,128)(2,1)S(1)} %copy-done.1), channel_id=1, source_target_pairs={{0,1},{1,0},{2,3},{3,2},{4,5},{5,4},{6,7},{7,6},{8,9},{9,8},{10,11... | collective-permute-start | bytes 2949128 | tf_op jit(solution)/shard_map/ppermute | solution.py:45
  66.5 31.0 %copy-start = (bf16[128,1280]{1,0:T(8,128)(2,1)S(1)}, bf16[128,1280]{1,0:T(8,128)(2,1)}, u32[]{:S(2)}) copy-start(bf16[128,1280]{1,0:T(8,128)(2,1)} %param.2) | copy-start | bytes 983044
  95.5 4.2 %collective-permute-start.1 = (bf16[512,768]{1,0:T(8,128)(2,1)S(1)}, bf16[512,768]{1,0:T(8,128)(2,1)S(1)}, u32[]{:S(2)}, u32[]{:S(2)}) collective-permute-start(bf16[512,768]{1,0:T(8,128)(2,1)S(1)} %bitcast.55), channel_id=1, source_target_pairs={{0,1},{1,0},{2,3},{3,2},{4,5},{5,4},{6,7},{7,6},{8,9},{9,8},{10,11... | collective-permute-start | bytes 2359304 | tf_op jit(solution)/shard_map/ppermute | solution.py:57

commit v15 on v14

--- a/solution.py
+++ b/solution.py
@@ -81,9 +81,11 @@
     partial_target = jnp.dot(weights[:, : clips // 2], latents, preferred_element_type=jnp.float32)
     partial_target += jnp.dot(weights[:, clips // 2 :], other, preferred_element_type=jnp.float32)
     send = jnp.concatenate([partial_target.astype(jnp.bfloat16).reshape(X, draws, features), totals], axis=1)
-    got = lax.all_to_all(send, "x", 0, 0).astype(jnp.float32)
-    parts = (got[0, :draws] + got[1, :draws]) + (got[2, :draws] + got[3, :draws])
-    own_total = jnp.sum(got[:, draws : draws + 2, :draws], axis=(0, 1))
+    got = lax.all_to_all(send, "x", 0, 0)
+    tail = lax.optimization_barrier(got[:, draws:, :draws])
+    own_total = jnp.sum(tail[:, :2].astype(jnp.float32), axis=(0, 1))
+    part = [got[k, :draws].astype(jnp.float32) for k in range(X)]
+    parts = (part[0] + part[1]) + (part[2] + part[3])
     return (parts / own_total[:, None] + minus_noise.astype(jnp.float32)).astype(jnp.bfloat16)
 
 

time: 148 us -> 148 us (level)
  no operation moved by 1% of the time
where the time goes in v15:
time: 148 us; the launch traced here: 147 us
  blocking collectives  110 us (74%)
  waiting for transfers between devices  18 us (12%)
  starting transfers between devices  8.24 us (6%)
  other arithmetic  4.63 us (3%)
  matrix products  3.41 us (2%)
  local copies, waits for them, and re-layouts  2.23 us (2%)
    all_to_all x1, blocking collectives, body(): arrived = lax.all_to_all(partial, WIDE, 0, 0)  40.1 us
    all_to_all x1, blocking collectives, gather_by_a2a(): lax.all_to_all(jnp.broadcast_to(block[None], (n, *block.shape)), axes, 0, 0)  28.8 us
    all_to_all x3, blocking collectives, sum_over_x(): lax.all_to_all(jnp.broadcast_to(send, (X, *send.shape[1:])), 'x', 0, 0)  23.1 us
    all_to_all x1, blocking collectives, body(): got = lax.all_to_all(send, 'x', 0, 0)  18.3 us
    all_to_all x1, waiting for transfers between devices, gather_by_a2a(): lax.all_to_all(jnp.broadcast_to(block[None], (n, *block.shape)), axes, 0, 0)  16 us
    all_to_all x1, starting transfers between devices, gather_by_a2a(): lax.all_to_all(jnp.broadcast_to(block[None], (n, *block.shape)), axes, 0, 0)  4.42 us
  transfers between devices with their start and end apart: 3, of which 2 were waited for; matrix products, arithmetic and copies ran while one was open for 1% of the time, Pallas kernels for 0%

profile of v15, /device:TPU:16, one launch (start us, length us, event | category | flops | bytes accessed | tf_op | source)
XLA Modules:
  0.0 147.1 jit_solution(640739123579015468)
XLA Ops:
  0.0 2.1 %broadcast_in_dim.16 = bf16[4,128,1280]{2,1,0:T(8,128)(2,1)} broadcast(bf16[128,1280]{1,0:T(8,128)(2,1)} %param.2), dimensions={1,2} | broadcast | bytes 1638400 | tf_op jit(solution)/shard_map/broadcast_in_dim | solution.py:21
  2.1 0.0 copy-start.1
  2.1 4.4 %all-to-all-start = ((bf16[4,128,1280]{2,1,0:T(8,128)(2,1)}), bf16[4,128,1280]{2,1,0:T(8,128)(2,1)S(1)}, u32[]{:S(2)}, u32[]{:S(2)}) async-start(bf16[4,128,1280]{2,1,0:T(8,128)(2,1)} %broadcast_in_dim.16), calls=%async_computation | async-start | bytes 2621440 | tf_op jit(solution)/shard_map/all_to_all | solution.py:21
  6.5 0.0 copy-done.1
  6.5 1.9 %collective-permute-start = (bf16[384,1280]{1,0:T(8,128)(2,1)S(1)}, bf16[384,1280]{1,0:T(8,128)(2,1)S(1)}, u32[]{:S(2)}, u32[]{:S(2)}) collective-permute-start(bf16[384,1280]{1,0:T(8,128)(2,1)S(1)} %copy-done.1), channel_id=1, source_target_pairs={{0,1},{1,0},{2,3},{3,2},{4,5},{5,4},{6,7},{7,6},{8,9},{9,8},{10,11... | collective-permute-start | bytes 2949128 | tf_op jit(solution)/shard_map/ppermute | solution.py:45
  8.5 16.0 %all-to-all-done = bf16[4,128,1280]{2,1,0:T(8,128)(2,1)S(1)} async-done(((bf16[4,128,1280]{2,1,0:T(8,128)(2,1)}), bf16[4,128,1280]{2,1,0:T(8,128)(2,1)S(1)}, u32[]{:S(2)}, u32[]{:S(2)}) %all-to-all-start) | async-done | bytes 1310752 | tf_op jit(solution)/shard_map/all_to_all | solution.py:21
  24.5 0.9 fusion.18
  25.3 0.0 collective-permute-done
  25.3 0.9 fusion.17
  26.2 0.2 pad_maximum_fusion.1
  26.4 40.1 %all_to_all.35 = f16[64,2,8,384]{3,2,1,0:T(8,128)(2,1)S(1)} all-to-all(f16[64,2,8,384]{3,2,1,0:T(8,128)(2,1)S(1)} %pad_maximum_fusion.1), channel_id=1, replica_groups=mesh['y'=8,'z'=8,'x'=4,'c'=2] {'y','z'}, dimensions={0} | all-to-all | bytes 1572864 | tf_op jit(solution)/shard_map/all_to_all | solution.py:53
  66.5 0.0 copy-start
  66.5 0.1 convert_reduce_fusion.1
  66.6 0.1 broadcast_in_dim.17
  66.7 28.8 %all_to_all.36 = bf16[64,8,768]{2,1,0:T(8,128)(2,1)S(1)} all-to-all(bf16[64,8,768]{2,1,0:T(8,128)(2,1)S(1)} %broadcast_in_dim.17), channel_id=1, replica_groups=mesh['y'=8,'z'=8,'x'=4,'c'=2] {'y','z'}, dimensions={0} | all-to-all | bytes 1572864 | tf_op jit(solution)/shard_map/all_to_all | solution.py:21
  95.5 1.9 %collective-permute-start.1 = (bf16[512,768]{1,0:T(8,128)(2,1)S(1)}, bf16[512,768]{1,0:T(8,128)(2,1)S(1)}, u32[]{:S(2)}, u32[]{:S(2)}) collective-permute-start(bf16[512,768]{1,0:T(8,128)(2,1)S(1)} %bitcast.53), channel_id=1, source_target_pairs={{0,1},{1,0},{2,3},{3,2},{4,5},{5,4},{6,7},{7,6},{8,9},{9,8},{10,11... | collective-permute-start | bytes 2359304 | tf_op jit(solution)/shard_map/ppermute | solution.py:57
  97.4 0.0 copy-done
  97.5 0.1 neg.3
  97.5 0.2 convert_reduce_fusion
  97.7 2.0 %collective-permute-done.1 = bf16[512,768]{1,0:T(8,128)(2,1)S(1)} collective-permute-done((bf16[512,768]{1,0:T(8,128)(2,1)S(1)}, bf16[512,768]{1,0:T(8,128)(2,1)S(1)}, u32[]{:S(2)}, u32[]{:S(2)}) %collective-permute-start.1) | collective-permute-done | bytes 786464 | tf_op jit(solution)/shard_map/ppermute | solution.py:57
  99.7 0.2 fusion.1
  100.0 7.7 %all_to_all.37 = f32[4,8,128]{2,1,0:T(8,128)S(1)} all-to-all(f32[4,8,128]{2,1,0:T(8,128)S(1)} %broadcast_in_dim.19), channel_id=1, replica_groups=mesh['y'=8,'z'=8,'x'=4,'c'=2] {'x'}, dimensions={0} | all-to-all | bytes 32768 | tf_op jit(solution)/shard_map/all_to_all | solution.py:29
  107.7 0.4 fusion.2
  108.1 0.2 fusion.8
  108.4 0.2 fusion.3
  108.6 7.7 %all_to_all.38 = f32[4,8,128]{2,1,0:T(8,128)S(1)} all-to-all(f32[4,8,128]{2,1,0:T(8,128)S(1)} %broadcast_in_dim.21), channel_id=1, replica_groups=mesh['y'=8,'z'=8,'x'=4,'c'=2] {'x'}, dimensions={0} | all-to-all | bytes 32768 | tf_op jit(solution)/shard_map/all_to_all | solution.py:29
  116.3 0.2 fusion.4
  116.6 0.2 fusion.9
  116.8 0.2 fusion.10
  117.1 0.2 fusion.5
  117.4 7.7 %all_to_all.39 = f32[4,8,128]{2,1,0:T(8,128)S(1)} all-to-all(f32[4,8,128]{2,1,0:T(8,128)S(1)} %broadcast_in_dim.23), channel_id=1, replica_groups=mesh['y'=8,'z'=8,'x'=4,'c'=2] {'x'}, dimensions={0} | all-to-all | bytes 32768 | tf_op jit(solution)/shard_map/all_to_all | solution.py:29
  125.1 0.2 fusion.6
  125.3 0.2 fusion.11
  125.6 0.3 fusion.14
  125.9 0.8 fusion.22
  126.8 0.8 fusion
  127.7 0.1 pad_maximum_fusion
  127.8 18.3 %all_to_all.40 = bf16[4,136,1280]{2,1,0:T(8,128)(2,1)S(1)} all-to-all(bf16[4,136,1280]{2,1,0:T(8,128)(2,1)S(1)} %pad_maximum_fusion), channel_id=1, replica_groups=mesh['y'=8,'z'=8,'x'=4,'c'=2] {'x'}, dimensions={0} | all-to-all | bytes 2785280 | tf_op jit(solution)/shard_map/all_to_all | solution.py:84
  146.1 1.0 fusion.20
  (32 shorter events, 0.2 us)
Async XLA Ops:
  2.1 4.4 %copy-start.1 = (bf16[384,1280]{1,0:T(8,128)(2,1)S(1)}, bf16[384,1280]{1,0:T(8,128)(2,1)}, u32[]{:S(2)}) copy-start(bf16[384,1280]{1,0:T(8,128)(2,1)} %param.3) | copy-start | bytes 2949124
  2.1 22.3 %all-to-all-start = ((bf16[4,128,1280]{2,1,0:T(8,128)(2,1)}), bf16[4,128,1280]{2,1,0:T(8,128)(2,1)S(1)}, u32[]{:S(2)}, u32[]{:S(2)}) async-start(bf16[4,128,1280]{2,1,0:T(8,128)(2,1)} %broadcast_in_dim.16), calls=%async_computation | async-start | bytes 2621440 | tf_op jit(solution)/shard_map/all_to_all | solution.py:21
  6.5 18.8 %collective-permute-start = (bf16[384,1280]{1,0:T(8,128)(2,1)S(1)}, bf16[384,1280]{1,0:T(8,128)(2,1)S(1)}, u32[]{:S(2)}, u32[]{:S(2)}) collective-permute-start(bf16[384,1280]{1,0:T(8,128)(2,1)S(1)} %copy-done.1), channel_id=1, source_target_pairs={{0,1},{1,0},{2,3},{3,2},{4,5},{5,4},{6,7},{7,6},{8,9},{9,8},{10,11... | collective-permute-start | bytes 2949128 | tf_op jit(solution)/shard_map/ppermute | solution.py:45
  66.5 31.0 %copy-start = (bf16[128,1280]{1,0:T(8,128)(2,1)S(1)}, bf16[128,1280]{1,0:T(8,128)(2,1)}, u32[]{:S(2)}) copy-start(bf16[128,1280]{1,0:T(8,128)(2,1)} %param.2) | copy-start | bytes 983044
  95.5 4.2 %collective-permute-start.1 = (bf16[512,768]{1,0:T(8,128)(2,1)S(1)}, bf16[512,768]{1,0:T(8,128)(2,1)S(1)}, u32[]{:S(2)}, u32[]{:S(2)}) collective-permute-start(bf16[512,768]{1,0:T(8,128)(2,1)S(1)} %bitcast.53), channel_id=1, source_target_pairs={{0,1},{1,0},{2,3},{3,2},{4,5},{5,4},{6,7},{7,6},{8,9},{9,8},{10,11... | collective-permute-start | bytes 2359304 | tf_op jit(solution)/shard_map/ppermute | solution.py:57
